TPU v7x, 128 devices: a whole 4x4x4 slice. The times are simulated.
128 devices in a mesh: pfx: 16 (over x, z), tp: 8 (over y, core).
Axes of the slice: x: 4, y: 4, z: 4, core: 2. Of those that a mesh axis runs over, the one named last changes fastest.
Arguments:
- queries: bfloat16 [512, 16384], P('pfx', 'tp'), may hold values from -8 to 8
- route: int32 [512], P('pfx'), may hold values from 0 to 15, as said below
- place: int32 [16], replicated, may hold values from 0 to 15, each once
- suffix_len: int32 [512], P('pfx'), may hold values from 1 to 256, as said below
- prefix_keys: bfloat16 [131072, 1024], P('pfx', 'tp'), may hold values from -8 to 8
- prefix_values: bfloat16 [131072, 1024], P('pfx', 'tp'), may hold values from -6 to 6
- suffix_keys: bfloat16 [512, 256, 1024], P('pfx', None, 'tp'), may hold values from -8 to 8
- suffix_values: bfloat16 [512, 256, 1024], P('pfx', None, 'tp'), may hold values from -6 to 6
- out_weight: bfloat16 [16384, 16384], P('tp', 'pfx'), may hold values from -0.1875 to 0.1875
Outputs:
- mixture: bfloat16 [512, 16384], P('tp', 'pfx')
Inputs may be any that keep to these rules, and one draw needn't show every extreme that they name: `route`: within the rows of one device (aligned blocks of 32 requests) no prefix is named more than 6 times, and one prefix is named exactly 6 times in every block. Prefix p's cache rows start at place[p] * 8192. `suffix_len`: every aligned block of 32 requests holds one of length 256.
All inputs are finite; a program needn't handle non-finite values.
Results may differ from a plain program's by a relative error of at most 0.019.
Values may be sent and summed in bfloat16 or wider, within the bound.
No kernel may reach another device: no remote copies, remote signals or barrier semaphores. Data moves between devices by JAX's collectives and lax.ppermute only.
A program may use at most 128 MiB of HBM per device.

v0:
```python
import jax
import jax.numpy as jnp
from jax import lax
from jax.sharding import PartitionSpec as P

HDIM = 128


def soft_parts(scores):
    row_top = jnp.max(scores, axis=-1, keepdims=True)
    exponent = jnp.exp(scores - row_top)
    totals = jnp.sum(exponent, axis=-1)
    weights = exponent.astype(jnp.bfloat16)
    return (weights, totals, row_top[..., 0] + jnp.log(totals))


def suffix_part(
    queries, suffix_len, suffix_keys, suffix_values, key_heads, group_size, head_depth, score_scale
):
    item_count = queries.shape[0]
    cache_length = suffix_keys.shape[1]
    query_heads = queries.reshape(item_count, key_heads, group_size, head_depth)
    key_rows = suffix_keys.reshape(item_count, cache_length, key_heads, head_depth)
    value_rows = suffix_values.reshape(item_count, cache_length, key_heads, head_depth)
    scores = (
        jnp.einsum("rkgd,rlkd->rkgl", query_heads, key_rows, preferred_element_type=jnp.float32)
        * score_scale
    )
    live_mask = (
        lax.broadcasted_iota(jnp.int32, (item_count, 1, 1, cache_length), 3)
        < suffix_len[:, None, None, None]
    )
    scores = jnp.where(live_mask, scores, -1e30)
    weights, totals, log_total = soft_parts(scores)
    result = (
        jnp.einsum("rkgl,rlkd->rkgd", weights, value_rows, preferred_element_type=jnp.float32)
        / totals[..., None]
    )
    return (
        result.reshape(item_count, key_heads * group_size, head_depth),
        log_total.reshape(item_count, key_heads * group_size),
    )


def prefix_part(
    flat_queries, prefix_keys, prefix_values, key_heads, group_size, head_depth, score_scale
):
    key_rows = prefix_keys.reshape(-1, key_heads, head_depth)
    value_rows = prefix_values.reshape(-1, key_heads, head_depth)

    def one_query(query):
        query_heads = query.reshape(key_heads, group_size, head_depth)
        scores = (
            jnp.einsum("kgd,lkd->kgl", query_heads, key_rows, preferred_element_type=jnp.float32)
            * score_scale
        )
        weights, totals, log_total = soft_parts(scores)
        result = (
            jnp.einsum("kgl,lkd->kgd", weights, value_rows, preferred_element_type=jnp.float32)
            / totals[..., None]
        )
        return (
            result.astype(jnp.bfloat16).reshape(key_heads * group_size * head_depth),
            log_total.reshape(key_heads * group_size),
        )

    return lax.map(one_query, flat_queries, batch_size=32)


def merge_parts(prefix_out, prefix_lse, suffix_out, suffix_lse):
    total_lse = jnp.logaddexp(prefix_lse, suffix_lse)
    merged = (
        jnp.exp(prefix_lse - total_lse)[..., None] * prefix_out
        + jnp.exp(suffix_lse - total_lse)[..., None] * suffix_out
    )
    return merged.astype(jnp.bfloat16)


def on_device(
    queries,
    route,
    place,
    suffix_len,
    prefix_keys,
    prefix_values,
    suffix_keys,
    suffix_values,
    out_weight,
):
    req_rows, row_width = queries.shape
    head_depth = HDIM
    key_heads = prefix_keys.shape[1] // head_depth
    head_count = row_width // head_depth
    group_size = head_count // key_heads
    score_scale = head_depth ** (-0.5)
    owner_count = lax.axis_size("pfx")
    slot_count = 3 * req_rows // owner_count
    suffix_out, suffix_lse = suffix_part(
        queries,
        suffix_len,
        suffix_keys,
        suffix_values,
        key_heads,
        group_size,
        head_depth,
        score_scale,
    )
    owners_of = place[route]
    same_owner = owners_of[:, None] == owners_of[None, :]
    earlier = lax.broadcasted_iota(jnp.int32, (req_rows, req_rows), 1) < lax.broadcasted_iota(
        jnp.int32, (req_rows, req_rows), 0
    )
    slot_rank = jnp.sum((same_owner & earlier).astype(jnp.int32), axis=1)
    dest_row = owners_of * slot_count + slot_rank
    query_buffer = (
        jnp.zeros((owner_count * slot_count, row_width), jnp.bfloat16).at[dest_row].set(queries)
    )
    received = lax.all_to_all(
        query_buffer.reshape(owner_count, slot_count, row_width),
        "pfx",
        split_axis=0,
        concat_axis=0,
        tiled=True,
    )
    sources = received.shape[0]
    items = received.shape[1]
    prefix_out, prefix_lse = prefix_part(
        received.reshape(sources * items, row_width),
        prefix_keys,
        prefix_values,
        key_heads,
        group_size,
        head_depth,
        score_scale,
    )
    prefix_out, prefix_lse = (
        prefix_out.reshape(sources, items, row_width),
        prefix_lse.reshape(sources, items, head_count),
    )
    back_out, back_lse = (
        lax.all_to_all(prefix_out, "pfx", split_axis=0, concat_axis=0, tiled=True),
        lax.all_to_all(prefix_lse, "pfx", split_axis=0, concat_axis=0, tiled=True),
    )
    picked_out = back_out.reshape(owner_count * slot_count, head_count, head_depth)[
        dest_row
    ].astype(jnp.float32)
    picked_lse = back_lse.reshape(owner_count * slot_count, head_count)[dest_row]
    attention = merge_parts(picked_out, picked_lse, suffix_out, suffix_lse).reshape(
        req_rows, row_width
    )
    terms = jnp.dot(
        lax.all_gather(attention, "pfx", axis=0, tiled=True),
        out_weight,
        preferred_element_type=jnp.float32,
    )
    return lax.psum_scatter(terms.astype(jnp.bfloat16), "tp", scatter_dimension=0, tiled=True)


def solution(mesh):
    placed = (
        P("pfx", "tp"),
        P("pfx"),
        P(),
        P("pfx"),
        P("pfx", "tp"),
        P("pfx", "tp"),
        P("pfx", None, "tp"),
        P("pfx", None, "tp"),
        P("tp", "pfx"),
    )
    return jax.shard_map(
        on_device, mesh=mesh, in_specs=placed, out_specs=P("tp", "pfx"), check_vma=False
    )
```

profile of v0, /device:TPU:1, one launch (start us, length us, event | category | flops | bytes accessed | tf_op | source)
XLA Modules:
  0.0 230.7 jit_solution(3917921266053636199)
XLA Ops:
  6.5 0.8 compare_select_fusion.1
  7.4 1.4 gather_fusion
  8.7 0.2 convert_reduce_fusion
  8.9 1.3 scatter_custom_fusion
  10.2 0.9 reshape.216
  11.1 8.4 %all-to-all-start = ((bf16[16,6,2048]{2,1,0:T(8,128)(2,1)}), bf16[16,6,2048]{2,1,0:T(8,128)(2,1)S(1)}, u32[]{:S(2)}, u32[]{:S(2)}) async-start(bf16[16,6,2048]{2,1,0:T(8,128)(2,1)} %reshape.216), calls=%async_computation | async-start | bytes 1048576 | tf_op jit(solution)/shard_map/all_to_all | solution.py:118
  19.6 0.9 copy.11
  20.5 0.7 iota_compare_fusion
  21.3 8.6 %all-to-all-done = bf16[16,6,2048]{2,1,0:T(8,128)(2,1)S(1)} async-done(((bf16[16,6,2048]{2,1,0:T(8,128)(2,1)}), bf16[16,6,2048]{2,1,0:T(8,128)(2,1)S(1)}, u32[]{:S(2)}, u32[]{:S(2)}) %all-to-all-start) | async-done | bytes 393248 | tf_op jit(solution)/shard_map/all_to_all | solution.py:118
  29.9 0.1 reshape_reshape.9
  30.0 84.2 %while.12 = (s32[]{:T(128)}, bf16[3,32,2048]{2,1,0:T(8,128)(2,1)S(1)}, f32[3,32,16]{2,1,0:T(8,128)}, bf16[3,32,2048]{2,1,0:T(8,128)(2,1)S(1)}, bf16[8192,1,128]{...) while((s32[]{:T(128)}, bf16[3,32,2048]{2,1,0:T(8,128)(2,1)S(1)}, f32[3,32,16]{2,1,0:T(8,128)}, ...), condition=%wide.region_5.6_spmd, body=%wide.region_2.5_spmd.sunk | while | flops 2181168640 | bytes 55867988 | solution.py:67
  30.1 9.7 %multiply_reduce_fusion.2 = (f32[32,16]{1,0:T(8,128)S(1)}, f32[32,16,8192]{2,1,0:T(8,128)}) fusion(bf16[32,16,128]{2,1,0:T(8,128)(2,1)S(1)} %bitcast.51, bf16[8192,1,128]{2,0,1:T(8,128)(2,1)} %get-tuple-element.117), kind=kOutput, calls=%fused_computation.5.clone.1 | convolution fusion | flops 1082129920 | bytes 19007488 | tf_op jit(solution)/shard_map/while/body/eval_jaxpr/vmap(kgd,lkd->kgl)/dot_general | solution.py:54
  39.7 8.6 %fusion.48 = f32[32,16]{1,0:T(8,128)S(1)} fusion(f32[32,16,8192]{2,1,0:T(8,128)} %get-tuple-element.97, f32[32,16]{1,0:T(8,128)S(1)} %get-tuple-element.98), kind=kLoop, calls=%fused_computation.6.clone.1 | loop fusion | flops 12582400 | bytes 16781312 | tf_op jit(solution)/shard_map/while/body/eval_jaxpr/vmap()/reduce_sum | solution.py:12
  48.3 0.6 bitcast_dynamic-update-slice_fusion.2
  49.0 9.0 %fusion.49 = bf16[32,16,128]{2,1,0:T(8,128)(2,1)S(1)} fusion(bf16[8192,1,128]{2,0,1:T(8,128)(2,1)} %get-tuple-element.118, f32[32,16,8192]{2,1,0:T(8,128)} %get-tuple-element.97, f32[32,16]{1,0:T(8,128)S(1)} %get-tuple-element.98, f32[32,16]{1,0:T(8,128)S(1)} %fusion.48), kind=kOutput, calls=%fused_computation.13.clone.1 | convolution fusion | flops 1086455808 | bytes 19009536 | tf_op jit(solution)/shard_map/while/body/eval_jaxpr/vmap(kgl,lkd->kgd)/dot_general | solution.py:59
  58.0 0.1 broadcast_in_dim.52
  58.2 9.7 %multiply_reduce_fusion.2 = (f32[32,16]{1,0:T(8,128)S(1)}, f32[32,16,8192]{2,1,0:T(8,128)}) fusion(bf16[32,16,128]{2,1,0:T(8,128)(2,1)S(1)} %bitcast.51, bf16[8192,1,128]{2,0,1:T(8,128)(2,1)} %get-tuple-element.117), kind=kOutput, calls=%fused_computation.5.clone.1 | convolution fusion | flops 1082129920 | bytes 19007488 | tf_op jit(solution)/shard_map/while/body/eval_jaxpr/vmap(kgd,lkd->kgl)/dot_general | solution.py:54
  67.8 8.6 %fusion.48 = f32[32,16]{1,0:T(8,128)S(1)} fusion(f32[32,16,8192]{2,1,0:T(8,128)} %get-tuple-element.97, f32[32,16]{1,0:T(8,128)S(1)} %get-tuple-element.98), kind=kLoop, calls=%fused_computation.6.clone.1 | loop fusion | flops 12582400 | bytes 16781312 | tf_op jit(solution)/shard_map/while/body/eval_jaxpr/vmap()/reduce_sum | solution.py:12
  76.4 0.6 bitcast_dynamic-update-slice_fusion.2
  77.0 9.0 %fusion.49 = bf16[32,16,128]{2,1,0:T(8,128)(2,1)S(1)} fusion(bf16[8192,1,128]{2,0,1:T(8,128)(2,1)} %get-tuple-element.118, f32[32,16,8192]{2,1,0:T(8,128)} %get-tuple-element.97, f32[32,16]{1,0:T(8,128)S(1)} %get-tuple-element.98, f32[32,16]{1,0:T(8,128)S(1)} %fusion.48), kind=kOutput, calls=%fused_computation.13.clone.1 | convolution fusion | flops 1086455808 | bytes 19009536 | tf_op jit(solution)/shard_map/while/body/eval_jaxpr/vmap(kgl,lkd->kgd)/dot_general | solution.py:59
  86.1 0.1 broadcast_in_dim.52
  86.2 9.7 %multiply_reduce_fusion.2 = (f32[32,16]{1,0:T(8,128)S(1)}, f32[32,16,8192]{2,1,0:T(8,128)}) fusion(bf16[32,16,128]{2,1,0:T(8,128)(2,1)S(1)} %bitcast.51, bf16[8192,1,128]{2,0,1:T(8,128)(2,1)} %get-tuple-element.117), kind=kOutput, calls=%fused_computation.5.clone.1 | convolution fusion | flops 1082129920 | bytes 19007488 | tf_op jit(solution)/shard_map/while/body/eval_jaxpr/vmap(kgd,lkd->kgl)/dot_general | solution.py:54
  95.9 8.6 %fusion.48 = f32[32,16]{1,0:T(8,128)S(1)} fusion(f32[32,16,8192]{2,1,0:T(8,128)} %get-tuple-element.97, f32[32,16]{1,0:T(8,128)S(1)} %get-tuple-element.98), kind=kLoop, calls=%fused_computation.6.clone.1 | loop fusion | flops 12582400 | bytes 16781312 | tf_op jit(solution)/shard_map/while/body/eval_jaxpr/vmap()/reduce_sum | solution.py:12
  104.5 0.6 bitcast_dynamic-update-slice_fusion.2
  105.1 9.0 %fusion.49 = bf16[32,16,128]{2,1,0:T(8,128)(2,1)S(1)} fusion(bf16[8192,1,128]{2,0,1:T(8,128)(2,1)} %get-tuple-element.118, f32[32,16,8192]{2,1,0:T(8,128)} %get-tuple-element.97, f32[32,16]{1,0:T(8,128)S(1)} %get-tuple-element.98, f32[32,16]{1,0:T(8,128)S(1)} %fusion.48), kind=kOutput, calls=%fused_computation.13.clone.1 | convolution fusion | flops 1086455808 | bytes 19009536 | tf_op jit(solution)/shard_map/while/body/eval_jaxpr/vmap(kgl,lkd->kgd)/dot_general | solution.py:59
  114.1 0.1 broadcast_in_dim.52
  114.2 1.4 reshape_reshape.10
  115.7 3.5 %all-to-all-start.1 = ((f32[16,6,16]{2,1,0:T(8,128)}), f32[16,6,16]{2,1,0:T(8,128)S(1)}, u32[]{:S(2)}, u32[]{:S(2)}) async-start(f32[16,6,16]{2,1,0:T(8,128)} %reshape_reshape.10), calls=%async_computation.1 | async-start | bytes 131072 | tf_op jit(solution)/shard_map/all_to_all | solution.py:142
  119.2 0.7 fusion.33
  119.9 0.9 reshape_reshape.11
  120.9 4.8 %all-to-all-done.1 = f32[16,6,16]{2,1,0:T(8,128)S(1)} async-done(((f32[16,6,16]{2,1,0:T(8,128)}), f32[16,6,16]{2,1,0:T(8,128)S(1)}, u32[]{:S(2)}, u32[]{:S(2)}) %all-to-all-start.1) | async-done | bytes 6176 | tf_op jit(solution)/shard_map/all_to_all | solution.py:142
  125.7 3.6 %all-to-all-start.2 = ((bf16[16,6,2048]{2,1,0:T(8,128)(2,1)}), bf16[16,6,2048]{2,1,0:T(8,128)(2,1)S(1)}, u32[]{:S(2)}, u32[]{:S(2)}) async-start(bf16[16,6,2048]{2,1,0:T(8,128)(2,1)} %reshape_reshape.11), calls=%async_computation.2 | async-start | bytes 1048576 | tf_op jit(solution)/shard_map/all_to_all | solution.py:141
  129.3 0.2 all-gather.2.cloned.1.call-start
  129.5 0.2 fusion.23
  129.8 0.0 copy-start.1
  129.8 0.6 gather_fusion.1
  130.4 0.6 subtract_exponential_fusion.3
  131.0 7.1 %all-to-all-done.2 = bf16[16,6,2048]{2,1,0:T(8,128)(2,1)S(1)} async-done(((bf16[16,6,2048]{2,1,0:T(8,128)(2,1)}), bf16[16,6,2048]{2,1,0:T(8,128)(2,1)S(1)}, u32[]{:S(2)}, u32[]{:S(2)}) %all-to-all-start.2) | async-done | bytes 393248 | tf_op jit(solution)/shard_map/all_to_all | solution.py:141
  138.2 0.5 reshape.221
  138.6 0.7 gather_fusion.2
  139.3 2.1 fusion.21
  141.4 0.7 copy.14
  142.1 0.0 all-gather.2.cloned.1.call-update
  142.1 0.0 reduce-scatter.2.cloned.1.call-start
  142.2 46.0 %all-gather.2.cloned.1.call-done = bf16[512,2048]{1,0:T(8,128)(2,1)} async-done(((bf16[32,2048]{1,0:T(8,128)(2,1)}), bf16[512,2048]{1,0:T(8,128)(2,1)}) %all-gather.2.cloned.1.call-update) | async-done | bytes 2097168 | tf_op jit(solution)/shard_map/all_gather | solution.py:152
  188.2 6.1 %convolution_convert_fusion = bf16[512,1024]{1,0:T(8,128)(2,1)} fusion(bf16[512,2048]{1,0:T(8,128)(2,1)} %all-gather.2.cloned.1.call-done, bf16[2048,1024]{1,0:T(8,128)(2,1)} %param.19), kind=kOutput, calls=%fused_computation.18 | convolution fusion | flops 2148007936 | bytes 7340032 | tf_op jit(solution)/shard_map/dot_general | solution.py:151
  194.4 0.0 reduce-scatter.2.cloned.1.call-update
  194.4 29.5 %reduce-scatter.2.cloned.1.call-done = bf16[64,1024]{1,0:T(8,128)(2,1)} async-done(((bf16[512,1024]{1,0:T(8,128)(2,1)}), bf16[64,1024]{1,0:T(8,128)(2,1)}) %reduce-scatter.2.cloned.1.call-update) | async-done | bytes 131088 | tf_op jit(solution)/shard_map/reduce_scatter | solution.py:156
  (20 shorter events, 0.2 us)
Async XLA Ops:
  6.5 112.6 %copy-start = (bf16[32,256,128]{2,1,0:T(8,128)(2,1)S(1)}, bf16[32,256,128]{2,1,0:T(8,128)(2,1)}, u32[]{:S(2)}) copy-start(bf16[32,256,128]{2,1,0:T(8,128)(2,1)} %param.17) | copy-start | bytes 6291460
  11.1 18.7 %all-to-all-start = ((bf16[16,6,2048]{2,1,0:T(8,128)(2,1)}), bf16[16,6,2048]{2,1,0:T(8,128)(2,1)S(1)}, u32[]{:S(2)}, u32[]{:S(2)}) async-start(bf16[16,6,2048]{2,1,0:T(8,128)(2,1)} %reshape.216), calls=%async_computation | async-start | bytes 1048576 | tf_op jit(solution)/shard_map/all_to_all | solution.py:118
  115.7 10.0 %all-to-all-start.1 = ((f32[16,6,16]{2,1,0:T(8,128)}), f32[16,6,16]{2,1,0:T(8,128)S(1)}, u32[]{:S(2)}, u32[]{:S(2)}) async-start(f32[16,6,16]{2,1,0:T(8,128)} %reshape_reshape.10), calls=%async_computation.1 | async-start | bytes 131072 | tf_op jit(solution)/shard_map/all_to_all | solution.py:142
  125.7 12.5 %all-to-all-start.2 = ((bf16[16,6,2048]{2,1,0:T(8,128)(2,1)}), bf16[16,6,2048]{2,1,0:T(8,128)(2,1)S(1)}, u32[]{:S(2)}, u32[]{:S(2)}) async-start(bf16[16,6,2048]{2,1,0:T(8,128)(2,1)} %reshape_reshape.11), calls=%async_computation.2 | async-start | bytes 1048576 | tf_op jit(solution)/shard_map/all_to_all | solution.py:141
  129.3 59.0 %all-gather.2.cloned.1.call-start = ((), (), s32[]{:S(2)}) async-start(), calls=%async_computation.4 | async-start | bytes 2228224 | tf_op jit(solution)/shard_map/all_gather | solution.py:152
  129.5 1.5 copy-start.2
  129.8 1.3 copy-start.1
  142.1 81.7 %reduce-scatter.2.cloned.1.call-start = ((), (), s32[]{:S(2)}) async-start(), calls=%async_computation.5 | async-start | bytes 1179648 | tf_op jit(solution)/shard_map/reduce_scatter | solution.py:156
Sparse Core Ops, SparseCore 0:
  142.3 45.9 all-gather.1
  194.5 29.3 reduce-scatter.1
where the time goes:
time: 234 us; the launch traced here: 231 us
  waiting for transfers between devices  96.2 us (41%)
  matrix products  65 us (28%)
  other arithmetic  30.3 us (13%)
  starting transfers between devices  15.8 us (7%)
  between operations  13.5 us (6%)
  local copies, waits for them, and re-layouts  9.8 us (4%)
    all_gather x1, waiting for transfers between devices, on_device(): lax.all_gather(attention, 'pfx', axis=0, tiled=True)  46 us
    reduce_scatter x1, waiting for transfers between devices, on_device(): lax.psum_scatter(terms.astype(jnp.bfloat16), 'tp', scatter_dimension=0, t...  29.5 us
    dot_general x3, matrix products, one_query(): jnp.einsum('kgd,lkd->kgl', query_heads, key_rows, preferred_element_type=...  29 us
    dot_general x3, matrix products, one_query(): jnp.einsum('kgl,lkd->kgd', weights, value_rows, preferred_element_type=jn...  27.1 us
    reduce_sum x4, other arithmetic, soft_parts(): totals = jnp.sum(exponent, axis=-1)  26 us
    all_to_all x1, waiting for transfers between devices, on_device(): lax.all_to_all(query_buffer.reshape(owner_count, slot_count, row_width),...  8.62 us
    all_to_all x1, starting transfers between devices, on_device(): lax.all_to_all(query_buffer.reshape(owner_count, slot_count, row_width),...  8.43 us
    all_to_all x1, waiting for transfers between devices, on_device(): lax.all_to_all(prefix_out, 'pfx', split_axis=0, concat_axis=0, tiled=True)  7.15 us
  transfers between devices with their start and end apart: 5, of which 5 were waited for; matrix products, arithmetic and copies ran while one was open for 2% of the time, Pallas kernels for 0%

commit v1 on v0

v1 whole, which is shorter than its diff:
```python
import functools

import jax
import jax.numpy as jnp
from jax import lax
from jax.experimental import pallas as pl
from jax.experimental.pallas import tpu as pltpu
from jax.sharding import PartitionSpec as P

HDIM = 128
SLOTS = 8
CAP = 6
LOG2E = 1.4426950408889634
LN2 = 0.6931471805599453
F32 = jnp.float32
BF16 = jnp.bfloat16
VMEM = pl.BlockSpec(memory_space=pltpu.VMEM)
SMEM = pl.BlockSpec(memory_space=pltpu.SMEM)
PARAMS = pltpu.CompilerParams(vmem_limit_bytes=48 * 2**20)
NT = (((1,), (1,)), ((), ()))


def iota(shape, dim):
    return lax.broadcasted_iota(jnp.int32, shape, dim)


def one_hot(condition):
    return jnp.where(condition, 1.0, 0.0).astype(BF16)


def dest_rows(route_ref, place_ref, count_ref, add):
    for owner in range(place_ref.shape[0]):
        count_ref[owner] = 0
    for r in range(route_ref.shape[0]):
        owner = place_ref[route_ref[r]]
        rank = count_ref[owner]
        count_ref[owner] = rank + 1
        add(r, owner * SLOTS + rank)


def pack_kernel(route_ref, place_ref, q_ref, out_ref, count_ref):
    rows = q_ref.shape[0]
    lane = iota((SLOTS, 128), 1)
    dest = [jnp.full((SLOTS, 128), -1, jnp.int32)]

    def add(r, row):
        dest[0] = jnp.where(lane == r, row, dest[0])

    dest_rows(route_ref, place_ref, count_ref, add)
    pick = one_hot(iota((out_ref.shape[0], rows), 0) == dest[0][:1, :rows])
    out_ref[...] = jnp.dot(pick, q_ref[...], preferred_element_type=F32).astype(BF16)


def suffix_kernel(
    route_ref, place_ref, len_ref, q_ref, k_ref, v_ref, out_ref, lse_ref, dest_ref, count_ref
):
    requests, cache, depth = k_ref.shape
    heads = q_ref.shape[1] // depth
    batch = 16
    dest = [jnp.zeros((requests, 128), jnp.int32)]
    row = iota((requests, 128), 0)

    def add(r, place):
        dest[0] = jnp.where(row == r, place, dest[0])

    dest_rows(route_ref, place_ref, count_ref, add)
    dest_ref[...] = dest[0]
    for b in range(requests // batch):
        first = b * batch
        sl = slice(first, first + batch)
        q = jnp.concatenate([q_ref[sl, h * depth : (h + 1) * depth] for h in range(heads)], axis=0)
        own = iota((batch, 128), 0)
        live = jnp.zeros((batch, 128), jnp.int32)
        for r in range(batch):
            live = jnp.where(own == r, len_ref[first + r], live)
        keys = k_ref[sl].reshape(batch * cache, depth)
        values = v_ref[sl].reshape(batch * cache, depth)
        scores = lax.dot_general(q, keys, NT, preferred_element_type=F32)
        column = iota((batch, batch * cache), 1)
        start = iota((batch, batch * cache), 0) * cache
        inside = (column >= start) & (column < start + live[:, :1])
        bias = jnp.where(inside, 0.0, -jnp.inf)
        scores = scores * (depth**-0.5 * LOG2E) + jnp.concatenate([bias] * heads, axis=0)
        top = jnp.max(scores, axis=1, keepdims=True)
        weights = jnp.exp2(scores - top).astype(BF16)
        both = jnp.dot(
            weights,
            jnp.concatenate([values, jnp.ones_like(values)], axis=1),
            preferred_element_type=F32,
        )
        total = both[:, depth:]
        out = both[:, :depth] / total
        lse = top * LN2 + jnp.log(total)
        for h in range(heads):
            part = slice(h * batch, (h + 1) * batch)
            out_ref[sl, h * depth : (h + 1) * depth] = out[part]
            lse_ref[sl, h * depth : (h + 1) * depth] = lse[part]


KEYS = 4096
COLS = 512


def prefix_kernel(recv_ref, k_ref, v_ref, out_ref, q_ref, acc_ref, top_ref):
    depth = k_ref.shape[1]
    heads = recv_ref.shape[1] // depth
    sources = recv_ref.shape[0] // SLOTS
    items = sources * CAP
    rows = heads * items
    item = iota((items, recv_ref.shape[0]), 0)
    pick = one_hot(iota(item.shape, 1) == item // CAP * SLOTS + item % CAP)
    scale = depth**-0.5 * LOG2E
    for h in range(heads):
        q = jnp.dot(
            pick, recv_ref[:, h * depth : (h + 1) * depth], preferred_element_type=F32
        )
        q = q * scale
        high = q.astype(BF16)
        part = slice(h * items, (h + 1) * items)
        q_ref[part, :depth] = high
        q_ref[part, depth:] = (q - high.astype(F32)).astype(BF16)

    def scores_of(i, c):
        keys = k_ref[pl.ds(i * KEYS, KEYS), :]
        return lax.dot_general(
            jnp.concatenate([keys, keys], axis=1),
            q_ref[pl.ds(c * COLS, COLS), :],
            NT,
            preferred_element_type=F32,
        )

    def value_rows(i):
        values = v_ref[pl.ds(i * KEYS, KEYS), :]
        return jnp.concatenate([values.T, jnp.ones((16, KEYS), BF16)], axis=0)

    steps = k_ref.shape[0] // KEYS
    blocks = rows // COLS
    acc_ref[...] = jnp.zeros_like(acc_ref)

    def step(i, carry):
        turned = value_rows(i)
        for c in range(blocks):
            weights = jnp.exp2(scores_of(i, c)).astype(BF16)
            acc_ref[:, c * COLS : (c + 1) * COLS] += jnp.dot(
                turned, weights, preferred_element_type=F32
            )
        return carry

    lax.fori_loop(0, steps, step, 0)
    top_ref[...] = jnp.zeros_like(top_ref)
    total = acc_ref[depth : depth + 1, :]
    fine = (total > 2.0**-64) & (total < 2.0**100)

    @pl.when(jnp.min(jnp.where(fine, 1.0, 0.0)) < 0.5)
    def _():
        for c in range(blocks):
            sl = slice(c * COLS, (c + 1) * COLS)

            def find(i, top):
                return jnp.maximum(top, jnp.max(scores_of(i, c), axis=0, keepdims=True))

            top = lax.fori_loop(0, steps, find, jnp.full((1, COLS), -jnp.inf, F32))
            top_ref[:, sl] = jnp.broadcast_to(top, (8, COLS))
            acc_ref[:, sl] = jnp.zeros((acc_ref.shape[0], COLS), F32)

            def again(i, carry):
                weights = jnp.exp2(scores_of(i, c) - top).astype(BF16)
                acc_ref[:, sl] += jnp.dot(value_rows(i), weights, preferred_element_type=F32)
                return carry

            lax.fori_loop(0, steps, again, 0)

    total = acc_ref[depth : depth + 1, :]
    inverse = 1.0 / total
    lse = top_ref[:1, :] * LN2 + jnp.log(total)
    high = lse.astype(BF16).astype(F32)
    middle = (lse - high).astype(BF16).astype(F32)
    low = lse - high - middle
    wide = iota((8, rows), 0)
    pieces = jnp.where(wide == 0, high, jnp.where(wide == 1, middle, low))
    row = iota((recv_ref.shape[0], items), 0)
    column = iota(row.shape, 1)
    result_row = one_hot(row == column // CAP * SLOTS + column % CAP)
    lse_row = one_hot(row == column // CAP * SLOTS + CAP)
    spread = jnp.concatenate([result_row, lse_row], axis=1)
    offset = iota((items, depth), 1) - 3 * (iota((items, depth), 0) % CAP)
    for h in range(heads):
        part = slice(h * items, (h + 1) * items)
        out = (acc_ref[:depth, part] * inverse[:, part]).T
        three = pieces[:, part].T
        packed = jnp.where(
            offset == 0,
            three[:, 0:1],
            jnp.where(
                offset == 1, three[:, 1:2], jnp.where(offset == 2, three[:, 2:3], 0.0)
            ),
        )
        both = jnp.concatenate([out.astype(BF16), packed.astype(BF16)], axis=0)
        out_ref[:, h * depth : (h + 1) * depth] = jnp.dot(
            spread, both, preferred_element_type=F32
        ).astype(BF16)


def merge_kernel(back_ref, dest_ref, suffix_ref, lse_ref, out_ref):
    copies, requests, width = out_ref.shape
    depth = HDIM
    dest = dest_ref[:, :1]
    column = iota((requests, back_ref.shape[0]), 1)
    pick_out = one_hot(column == dest)
    pick_lse = one_hot(column == dest // SLOTS * SLOTS + CAP)
    offset = iota((requests, depth), 1) - 3 * (dest % SLOTS)
    mine = (offset >= 0) & (offset < 3)
    for h in range(width // depth):
        sl = slice(h * depth, (h + 1) * depth)
        prefix = jnp.dot(pick_out, back_ref[:, sl], preferred_element_type=F32)
        pieces = jnp.dot(pick_lse, back_ref[:, sl], preferred_element_type=F32)
        prefix_lse = jnp.sum(jnp.where(mine, pieces, 0.0), axis=1, keepdims=True)
        suffix_lse = lse_ref[:, sl]
        top = jnp.maximum(prefix_lse, suffix_lse)
        prefix_part = jnp.exp(prefix_lse - top)
        suffix_part = jnp.exp(suffix_lse - top)
        merged = (prefix_part * prefix + suffix_part * suffix_ref[:, sl]) / (
            prefix_part + suffix_part
        )
        merged = merged.astype(BF16)
        for copy in range(copies):
            out_ref[copy, :, sl] = merged


def project_kernel(core_ref, a_ref, w_ref, mine_ref, other_ref):
    core = core_ref[0]
    block = a_ref.shape[0] // 8
    order = [(y, core) for y in range(4)] + [(y, 1 - core) for y in range(4)]
    a = jnp.concatenate(
        [a_ref[pl.ds(pl.multiple_of((2 * y + c) * block, block), block), :] for y, c in order],
        axis=0,
    )
    half = a.shape[0] // 2
    tile = 256
    for n in range(w_ref.shape[1] // tile):
        sl = slice(n * tile, (n + 1) * tile)
        out = jnp.dot(a, w_ref[:, sl], preferred_element_type=F32)
        mine_ref[:, sl] = out[:half]
        other_ref[:, sl] = out[half:].astype(BF16)


def pair_kernel(y_ref, mine_ref, got_ref, own_ref, one_ref, two_ref, three_ref):
    y = y_ref[0]
    block = own_ref.shape[0]

    def part(k):
        start = pl.multiple_of(lax.rem(y + k, 4) * block, block)
        return mine_ref[pl.ds(start, block), :] + got_ref[pl.ds(start, block), :].astype(F32)

    one_ref[...] = part(1).astype(BF16)
    two_ref[...] = part(2).astype(BF16)
    three_ref[...] = part(3).astype(BF16)
    own_ref[...] = part(0)


def sum_kernel(own_ref, one_ref, two_ref, three_ref, out_ref):
    out_ref[...] = (
        own_ref[...]
        + one_ref[...].astype(F32)
        + two_ref[...].astype(F32)
        + three_ref[...].astype(F32)
    ).astype(BF16)


def call(kernel, outs, specs, scratch=(), cost=None):
    shapes = [jax.ShapeDtypeStruct(shape, dtype) for shape, dtype in outs]
    many = len(shapes) > 1
    return pl.pallas_call(
        kernel,
        out_shape=shapes if many else shapes[0],
        in_specs=specs,
        out_specs=[VMEM] * len(shapes) if many else VMEM,
        scratch_shapes=list(scratch),
        compiler_params=PARAMS,
        cost_estimate=cost,
    )


def on_device(
    queries, route, place, suffix_len, prefix_keys, prefix_values, suffix_keys, suffix_values, out_weight
):
    requests, width = queries.shape
    owners = lax.axis_size("pfx")
    heads = width // HDIM
    buffer_rows = owners * SLOTS
    rows = owners * CAP * heads
    count = pltpu.SMEM((owners,), jnp.int32)
    tp = lax.axis_index("tp")
    core, y = (tp % 2).reshape(1), (tp // 2).reshape(1)

    def exchange(x):
        shape = x.shape
        x = lax.all_to_all(
            x.reshape(owners, -1, width), "pfx", split_axis=0, concat_axis=0, tiled=True
        )
        return x.reshape(shape)

    packed = call(pack_kernel, [((buffer_rows, width), BF16)], [SMEM, SMEM, VMEM], [count])(
        route, place, queries
    )
    received = exchange(packed)
    suffix_out, suffix_lse, dest = call(
        suffix_kernel,
        [((requests, width), F32), ((requests, width), F32), ((requests, 128), jnp.int32)],
        [SMEM, SMEM, SMEM, VMEM, VMEM, VMEM],
        [count],
        pl.CostEstimate(flops=2 * 10**9, bytes_accessed=5 * 10**6, transcendentals=2 * 10**6),
    )(route, place, suffix_len, queries, suffix_keys, suffix_values)
    prefix = call(
        prefix_kernel,
        [((buffer_rows, width), BF16)],
        [VMEM, VMEM, VMEM],
        [
            pltpu.VMEM((rows, 2 * HDIM), BF16),
            pltpu.VMEM((HDIM + 16, rows), F32),
            pltpu.VMEM((8, rows), F32),
        ],
        pl.CostEstimate(flops=10**10, bytes_accessed=5 * 10**6, transcendentals=12 * 10**6),
    )(received, prefix_keys, prefix_values)
    back = exchange(prefix)
    copies = call(merge_kernel, [((owners, requests, width), BF16)], [VMEM] * 4)(
        back, dest, suffix_out, suffix_lse
    )
    attention = lax.all_to_all(copies, "pfx", split_axis=0, concat_axis=0, tiled=True)
    attention = attention.reshape(owners * requests, width)
    columns = out_weight.shape[1]
    half = owners * requests // 2
    mine, other = call(
        project_kernel,
        [((half, columns), F32), ((half, columns), BF16)],
        [SMEM, VMEM, VMEM],
        (),
        pl.CostEstimate(flops=2 * 10**9, bytes_accessed=8 * 10**6, transcendentals=0),
    )(core, attention, out_weight)
    got = lax.ppermute(other, "tp", [(i, i ^ 1) for i in range(8)])
    block = half // 4
    own, *parts = call(
        pair_kernel, [((block, columns), F32)] + [((block, columns), BF16)] * 3, [SMEM, VMEM, VMEM]
    )(y, mine, got)
    arrived = [
        lax.ppermute(part, "tp", [(i, (i + 2 * k) % 8) for i in range(8)])
        for k, part in zip((1, 2, 3), parts)
    ]
    return call(sum_kernel, [((block, columns), BF16)], [VMEM] * 4)(own, *arrived)


def solution(mesh):
    placed = (
        P("pfx", "tp"),
        P("pfx"),
        P(),
        P("pfx"),
        P("pfx", "tp"),
        P("pfx", "tp"),
        P("pfx", None, "tp"),
        P("pfx", None, "tp"),
        P("tp", "pfx"),
    )
    return jax.shard_map(
        on_device, mesh=mesh, in_specs=placed, out_specs=P("tp", "pfx"), check_vma=False
    )
```

time: 234 us -> 126 us (0.54); the launches traced: 231 us -> 126 us
  matrix products: 65 us -> 0 us
  waiting for transfers between devices: 96.2 us -> 34.6 us
  Pallas kernels: 0 us -> 47.2 us
  other arithmetic: 30.3 us -> 0 us
  blocking collectives: 0 us -> 18.5 us
  between operations: 13.5 us -> 0.12 us
  local copies, waits for them, and re-layouts: 9.8 us -> 7 us
  starting transfers between devices: 15.8 us -> 18.3 us
    dot_general x9 -> x0, matrix products: 65 us -> none  [the longest x3 29 us: one_query(): jnp.einsum('kgd,lkd->kgl', query_heads, key_rows, preferred_element_type=...]
    pallas_call x0 -> x7, Pallas kernels: none -> 47.2 us  [the longest x1 33.4 us: on_device(): call(prefix_kernel, [((buffer_rows, width), BF16)], [VMEM, VMEM, VMEM], [...]
    all_gather x1 -> x0, waiting for transfers between devices: 46 us -> none  [on_device(): lax.all_gather(attention, 'pfx', axis=0, tiled=True)]
    reduce_scatter x1 -> x0, waiting for transfers between devices: 29.5 us -> none  [on_device(): lax.psum_scatter(terms.astype(jnp.bfloat16), 'tp', scatter_dimension=0, t...]
    reduce_sum x5 -> x0, other arithmetic: 26.2 us -> none  [the longest x4 26 us: soft_parts(): totals = jnp.sum(exponent, axis=-1)]
    all_to_all x0 -> x1, blocking collectives: none -> 18.5 us  [exchange(): lax.all_to_all(x.reshape(owners, -1, width), 'pfx', split_axis=0, concat_...]
    ppermute x0 -> x4, starting transfers between devices: none -> 10.8 us  [the longest x1 5.79 us: on_device(): got = lax.ppermute(other, 'tp', [(i, i ^ 1) for i in range(8)])]
    all_to_all x3 -> x2, starting transfers between devices: 15.5 us -> 7.51 us  [the longest x1 3.79 us: exchange(): lax.all_to_all(x.reshape(owners, -1, width), 'pfx', split_axis=0, concat_...]
  transfers between devices with their start and end apart: 5 -> 6, of which waited for: 5 -> 5; matrix products, arithmetic and copies ran while one was open for 2% -> 0% of each run, Pallas kernels for 0% -> 4%
where the time goes in v1:
time: 126 us
  Pallas kernels  47.2 us (37%)
  waiting for transfers between devices  34.6 us (27%)
  blocking collectives  18.5 us (15%)
  starting transfers between devices  18.3 us (15%)
  local copies, waits for them, and re-layouts  7 us (6%)
    pallas_call x1, Pallas kernels, on_device(): call(prefix_kernel, [((buffer_rows, width), BF16)], [VMEM, VMEM, VMEM], [...  33.4 us
    all_to_all x1, waiting for transfers between devices, on_device(): lax.all_to_all(copies, 'pfx', split_axis=0, concat_axis=0, tiled=True)  25.2 us
    all_to_all x1, blocking collectives, exchange(): lax.all_to_all(x.reshape(owners, -1, width), 'pfx', split_axis=0, concat_...  18.5 us
    unnamed x22, local copies, waits for them, and re-layouts  7 us
    ppermute x1, starting transfers between devices, on_device(): got = lax.ppermute(other, 'tp', [(i, i ^ 1) for i in range(8)])  5.79 us
    pallas_call x1, Pallas kernels, on_device(): call(project_kernel, [((half, columns), F32), ((half, columns), BF16)], [...  5.32 us
    ppermute x3, starting transfers between devices, on_device(): lax.ppermute(part, 'tp', [(i, (i + 2 * k) % 8) for i in range(8)])  5.04 us
    ppermute x3, waiting for transfers between devices, on_device(): lax.ppermute(part, 'tp', [(i, (i + 2 * k) % 8) for i in range(8)])  4.99 us
  transfers between devices with their start and end apart: 6, of which 5 were waited for; matrix products, arithmetic and copies ran while one was open for 0% of the time, Pallas kernels for 4%

profile of v1, /device:TPU:1, one launch (start us, length us, event | category | flops | bytes accessed | tf_op | source)
XLA Modules:
  0.0 125.8 jit_solution(8718561677786561227)
XLA Ops:
  0.0 0.0 copy-start
  0.0 0.9 copy-done
  0.9 0.0 copy-start.2
  0.9 0.7 copy-done.2
  1.6 0.0 copy-start.4
  1.6 0.7 copy-done.4
  2.2 0.9 shard_map.91
  3.2 18.5 %all_to_all.15 = bf16[16,8,2048]{2,1,0:T(8,128)(2,1)S(1)} all-to-all(bf16[16,8,2048]{2,1,0:T(8,128)(2,1)S(1)} %bitcast.7), channel_id=1, replica_groups=mesh['pfx'=16,'tp'=8] {'pfx'}, dimensions={0} | all-to-all | bytes 1048576 | tf_op jit(solution)/shard_map/all_to_all | solution.py:298
  21.7 0.0 copy-start.6
  21.7 1.6 %copy-done.6 = bf16[8192,128]{1,0:T(8,128)(2,1)S(1)} copy-done((bf16[8192,128]{1,0:T(8,128)(2,1)S(1)}, bf16[8192,128]{1,0:T(8,128)(2,1)}, u32[]{:S(2)}) %copy-start.6) | copy-done | bytes 2097176
  23.3 0.0 copy-start.7
  23.3 1.6 %copy-done.7 = bf16[8192,128]{1,0:T(8,128)(2,1)S(1)} copy-done((bf16[8192,128]{1,0:T(8,128)(2,1)S(1)}, bf16[8192,128]{1,0:T(8,128)(2,1)}, u32[]{:S(2)}) %copy-start.7) | copy-done | bytes 2097176
  24.9 0.0 copy-start.1
  24.9 0.0 copy-start.3
  24.9 0.0 copy-start.5
  24.9 0.0 copy-start.8
  24.9 0.0 copy-start.10
  24.9 33.4 %shard_map.92 = bf16[128,2048]{1,0:T(8,128)(2,1)} custom-call(bf16[128,2048]{1,0:T(8,128)(2,1)S(1)} %bitcast.10, bf16[8192,128]{1,0:T(8,128)(2,1)S(1)} %copy-done.6, bf16[8192,128]{1,0:T(8,128)(2,1)S(1)} %copy-done.7), custom_call_target="tpu_custom_call" | custom-call | flops 10000000000 | bytes 5000000 | tf_op jit(solution)/shard_map/pallas_call | solution.py:314
  58.4 3.8 %all-to-all-start.1 = ((bf16[16,8,2048]{2,1,0:T(8,128)(2,1)}), bf16[16,8,2048]{2,1,0:T(8,128)(2,1)S(1)}, u32[]{:S(2)}, u32[]{:S(2)}) async-start(bf16[16,8,2048]{2,1,0:T(8,128)(2,1)} %bitcast.4), calls=%async_computation.1 | async-start | bytes 1048576 | tf_op jit(solution)/shard_map/all_to_all | solution.py:298
  62.2 0.0 copy-done.1
  62.2 0.0 copy-done.3
  62.2 0.0 copy-done.5
  62.2 0.0 copy-done.8
  62.2 0.0 copy-done.10
  62.2 0.0 copy-start.9
  62.2 1.6 %copy-done.9 = bf16[32,256,128]{2,1,0:T(8,128)(2,1)S(1)} copy-done((bf16[32,256,128]{2,1,0:T(8,128)(2,1)S(1)}, bf16[32,256,128]{2,1,0:T(8,128)(2,1)}, u32[]{:S(2)}) %copy-start.9) | copy-done | bytes 2097176
  63.8 4.5 %shard_map.93 = (f32[32,2048]{1,0:T(8,128)S(1)}, f32[32,2048]{1,0:T(8,128)S(1)}, s32[32,128]{1,0:T(8,128)S(1)}) custom-call(s32[32]{0:T(128)S(1)} %copy-done.3, s32[16]{0:T(128)S(1)} %copy-done.5, s32[32]{0:T(128)S(1)} %copy-done.10, bf16[32,2048]{1,0:T(8,128)(2,1)S(1)} %copy-done.1, bf16[32,256,128]{2,1,0:T(8,128)(2,1)S(1)} %copy-done.8, ...), custom_call_target="tpu_custom_call" | custom-call | flops 2000000000 | bytes 5000000 | tf_op jit(solution)/shard_map/pallas_call | solution.py:307
  68.3 2.7 %all-to-all-done.1 = bf16[16,8,2048]{2,1,0:T(8,128)(2,1)S(1)} async-done(((bf16[16,8,2048]{2,1,0:T(8,128)(2,1)}), bf16[16,8,2048]{2,1,0:T(8,128)(2,1)S(1)}, u32[]{:S(2)}, u32[]{:S(2)}) %all-to-all-start.1) | async-done | bytes 524320 | tf_op jit(solution)/shard_map/all_to_all | solution.py:298
  71.1 2.1 %shard_map.94 = bf16[16,32,2048]{2,1,0:T(8,128)(2,1)} custom-call(bf16[128,2048]{1,0:T(8,128)(2,1)S(1)} %bitcast.9, s32[32,128]{1,0:T(8,128)S(1)} %get-tuple-element.14.dest_ref, f32[32,2048]{1,0:T(8,128)S(1)} %get-tuple-element.15.suffix_ref, f32[32,2048]{1,0:T(8,128)S(1)} %get-tuple-element.16.lse_ref), custom_call_target="tpu_custom_call" | custom-call | tf_op jit(solution)/shard_map/pallas_call | solution.py:326
  73.2 3.7 %all-to-all-start.2 = ((bf16[16,32,2048]{2,1,0:T(8,128)(2,1)}), bf16[16,32,2048]{2,1,0:T(8,128)(2,1)S(1)}, u32[]{:S(2)}, u32[]{:S(2)}) async-start(bf16[16,32,2048]{2,1,0:T(8,128)(2,1)} %shard_map.94), calls=%async_computation.2 | async-start | bytes 4194304 | tf_op jit(solution)/shard_map/all_to_all | solution.py:329
  77.0 25.2 %all-to-all-done.2 = bf16[16,32,2048]{2,1,0:T(8,128)(2,1)S(1)} async-done(((bf16[16,32,2048]{2,1,0:T(8,128)(2,1)}), bf16[16,32,2048]{2,1,0:T(8,128)(2,1)S(1)}, u32[]{:S(2)}, u32[]{:S(2)}) %all-to-all-start.2) | async-done | bytes 2097184 | tf_op jit(solution)/shard_map/all_to_all | solution.py:329
  102.1 5.3 %shard_map.95 = (f32[256,1024]{1,0:T(8,128)S(1)}, bf16[256,1024]{1,0:T(8,128)(2,1)}) custom-call(s32[1]{0:T(128)} %bitcast.1.core_ref, bf16[512,2048]{1,0:T(8,128)(2,1)S(1)} %bitcast.8, bf16[2048,1024]{1,0:T(8,128)(2,1)} %w_ref.1), custom_call_target="tpu_custom_call" | custom-call | flops 2000000000 | bytes 8000000 | tf_op jit(solution)/shard_map/pallas_call | solution.py:333
  107.5 5.8 %collective-permute-start = (bf16[256,1024]{1,0:T(8,128)(2,1)}, bf16[256,1024]{1,0:T(8,128)(2,1)S(1)}, u32[]{:S(2)}, u32[]{:S(2)}) collective-permute-start(bf16[256,1024]{1,0:T(8,128)(2,1)} %get-tuple-element.18), channel_id=1, source_target_pairs={{0,1},{1,0},{2,3},{3,2},{4,5},{5,4},{6,7},{7,6},{8,9},{9,8},{10,11... | collective-permute-start | bytes 1572872 | tf_op jit(solution)/shard_map/ppermute | solution.py:340
  113.3 1.7 %collective-permute-done.got_ref = bf16[256,1024]{1,0:T(8,128)(2,1)S(1)} collective-permute-done((bf16[256,1024]{1,0:T(8,128)(2,1)}, bf16[256,1024]{1,0:T(8,128)(2,1)S(1)}, u32[]{:S(2)}, u32[]{:S(2)}) %collective-permute-start) | collective-permute-done | bytes 524320 | tf_op jit(solution)/shard_map/ppermute | solution.py:340
  115.0 0.1 shard_map.96
  115.1 1.4 %collective-permute-start.1 = (bf16[64,1024]{1,0:T(8,128)(2,1)S(1)}, bf16[64,1024]{1,0:T(8,128)(2,1)S(1)}, u32[]{:S(2)}, u32[]{:S(2)}) collective-permute-start(bf16[64,1024]{1,0:T(8,128)(2,1)S(1)} %get-tuple-element.20), channel_id=1, source_target_pairs={{0,2},{1,3},{2,4},{3,5},{4,6},{5,7},{6,0},{7,1},{8,10},{9,11},{10,... | collective-permute-start | bytes 393224 | tf_op jit(solution)/shard_map/ppermute | solution.py:346
  116.5 2.6 %collective-permute-start.2 = (bf16[64,1024]{1,0:T(8,128)(2,1)S(1)}, bf16[64,1024]{1,0:T(8,128)(2,1)S(1)}, u32[]{:S(2)}, u32[]{:S(2)}) collective-permute-start(bf16[64,1024]{1,0:T(8,128)(2,1)S(1)} %get-tuple-element.21), channel_id=1, source_target_pairs={{0,4},{1,5},{2,6},{3,7},{4,0},{5,1},{6,2},{7,3},{8,12},{9,13},{10,... | collective-permute-start | bytes 393224 | tf_op jit(solution)/shard_map/ppermute | solution.py:346
  119.1 1.1 collective-permute-start.3
  120.1 1.1 collective-permute-done.1.one_ref
  121.2 3.9 %collective-permute-done.2.two_ref = bf16[64,1024]{1,0:T(8,128)(2,1)S(1)} collective-permute-done((bf16[64,1024]{1,0:T(8,128)(2,1)S(1)}, bf16[64,1024]{1,0:T(8,128)(2,1)S(1)}, u32[]{:S(2)}, u32[]{:S(2)}) %collective-permute-start.2) | collective-permute-done | bytes 131104 | tf_op jit(solution)/shard_map/ppermute | solution.py:346
  125.1 0.0 collective-permute-done.3.three_ref
  125.1 0.7 shard_map.97
Async XLA Ops:
  0.0 0.9 copy-start
  0.9 0.7 copy-start.2
  1.6 0.7 copy-start.4
  21.7 1.6 %copy-start.6 = (bf16[8192,128]{1,0:T(8,128)(2,1)S(1)}, bf16[8192,128]{1,0:T(8,128)(2,1)}, u32[]{:S(2)}) copy-start(bf16[8192,128]{1,0:T(8,128)(2,1)} %k_ref.2) | copy-start | bytes 6291460
  23.3 1.6 %copy-start.7 = (bf16[8192,128]{1,0:T(8,128)(2,1)S(1)}, bf16[8192,128]{1,0:T(8,128)(2,1)}, u32[]{:S(2)}) copy-start(bf16[8192,128]{1,0:T(8,128)(2,1)} %v_ref.2) | copy-start | bytes 6291460
  24.9 37.3 %copy-start.1 = (bf16[32,2048]{1,0:T(8,128)(2,1)S(1)}, bf16[32,2048]{1,0:T(8,128)(2,1)}, u32[]{:S(2)}) copy-start(bf16[32,2048]{1,0:T(8,128)(2,1)} %q_ref.3) | copy-start | bytes 393220
  24.9 37.3 %copy-start.3 = (s32[32]{0:T(128)S(1)}, s32[32]{0:T(128)}, u32[]{:S(2)}) copy-start(s32[32]{0:T(128)} %route_ref.3) | copy-start | bytes 388
  24.9 37.3 %copy-start.5 = (s32[16]{0:T(128)S(1)}, s32[16]{0:T(128)}, u32[]{:S(2)}) copy-start(s32[16]{0:T(128)} %place_ref.3) | copy-start | bytes 196
  24.9 37.3 %copy-start.8 = (bf16[32,256,128]{2,1,0:T(8,128)(2,1)S(1)}, bf16[32,256,128]{2,1,0:T(8,128)(2,1)}, u32[]{:S(2)}) copy-start(bf16[32,256,128]{2,1,0:T(8,128)(2,1)} %k_ref.3) | copy-start | bytes 6291460
  24.9 37.3 %copy-start.10 = (s32[32]{0:T(128)S(1)}, s32[32]{0:T(128)}, u32[]{:S(2)}) copy-start(s32[32]{0:T(128)} %len_ref.1) | copy-start | bytes 388
  58.4 12.7 %all-to-all-start.1 = ((bf16[16,8,2048]{2,1,0:T(8,128)(2,1)}), bf16[16,8,2048]{2,1,0:T(8,128)(2,1)S(1)}, u32[]{:S(2)}, u32[]{:S(2)}) async-start(bf16[16,8,2048]{2,1,0:T(8,128)(2,1)} %bitcast.4), calls=%async_computation.1 | async-start | bytes 1048576 | tf_op jit(solution)/shard_map/all_to_all | solution.py:298
  62.2 1.6 %copy-start.9 = (bf16[32,256,128]{2,1,0:T(8,128)(2,1)S(1)}, bf16[32,256,128]{2,1,0:T(8,128)(2,1)}, u32[]{:S(2)}) copy-start(bf16[32,256,128]{2,1,0:T(8,128)(2,1)} %v_ref.3) | copy-start | bytes 6291460
  73.2 28.9 %all-to-all-start.2 = ((bf16[16,32,2048]{2,1,0:T(8,128)(2,1)}), bf16[16,32,2048]{2,1,0:T(8,128)(2,1)S(1)}, u32[]{:S(2)}, u32[]{:S(2)}) async-start(bf16[16,32,2048]{2,1,0:T(8,128)(2,1)} %shard_map.94), calls=%async_computation.2 | async-start | bytes 4194304 | tf_op jit(solution)/shard_map/all_to_all | solution.py:329
  107.5 7.5 %collective-permute-start = (bf16[256,1024]{1,0:T(8,128)(2,1)}, bf16[256,1024]{1,0:T(8,128)(2,1)S(1)}, u32[]{:S(2)}, u32[]{:S(2)}) collective-permute-start(bf16[256,1024]{1,0:T(8,128)(2,1)} %get-tuple-element.18), channel_id=1, source_target_pairs={{0,1},{1,0},{2,3},{3,2},{4,5},{5,4},{6,7},{7,6},{8,9},{9,8},{10,11... | collective-permute-start | bytes 1572872 | tf_op jit(solution)/shard_map/ppermute | solution.py:340
  115.1 6.1 %collective-permute-start.1 = (bf16[64,1024]{1,0:T(8,128)(2,1)S(1)}, bf16[64,1024]{1,0:T(8,128)(2,1)S(1)}, u32[]{:S(2)}, u32[]{:S(2)}) collective-permute-start(bf16[64,1024]{1,0:T(8,128)(2,1)S(1)} %get-tuple-element.20), channel_id=1, source_target_pairs={{0,2},{1,3},{2,4},{3,5},{4,6},{5,7},{6,0},{7,1},{8,10},{9,11},{10,... | collective-permute-start | bytes 393224 | tf_op jit(solution)/shard_map/ppermute | solution.py:346
  116.5 8.7 %collective-permute-start.2 = (bf16[64,1024]{1,0:T(8,128)(2,1)S(1)}, bf16[64,1024]{1,0:T(8,128)(2,1)S(1)}, u32[]{:S(2)}, u32[]{:S(2)}) collective-permute-start(bf16[64,1024]{1,0:T(8,128)(2,1)S(1)} %get-tuple-element.21), channel_id=1, source_target_pairs={{0,4},{1,5},{2,6},{3,7},{4,0},{5,1},{6,2},{7,3},{8,12},{9,13},{10,... | collective-permute-start | bytes 393224 | tf_op jit(solution)/shard_map/ppermute | solution.py:346
  119.1 6.1 %collective-permute-start.3 = (bf16[64,1024]{1,0:T(8,128)(2,1)S(1)}, bf16[64,1024]{1,0:T(8,128)(2,1)S(1)}, u32[]{:S(2)}, u32[]{:S(2)}) collective-permute-start(bf16[64,1024]{1,0:T(8,128)(2,1)S(1)} %get-tuple-element.22), channel_id=1, source_target_pairs={{0,6},{1,7},{2,0},{3,1},{4,2},{5,3},{6,4},{7,5},{8,14},{9,15},{10,... | collective-permute-start | bytes 393224 | tf_op jit(solution)/shard_map/ppermute | solution.py:346

commit v2 on v1

--- a/solution.py
+++ b/solution.py
@@ -16,7 +16,7 @@
 BF16 = jnp.bfloat16
 VMEM = pl.BlockSpec(memory_space=pltpu.VMEM)
 SMEM = pl.BlockSpec(memory_space=pltpu.SMEM)
-PARAMS = pltpu.CompilerParams(vmem_limit_bytes=48 * 2**20)
+HBM = pl.BlockSpec(memory_space=pltpu.HBM)
 NT = (((1,), (1,)), ((), ()))
 
 
@@ -38,8 +38,14 @@
         add(r, owner * SLOTS + rank)
 
 
-def pack_kernel(route_ref, place_ref, q_ref, out_ref, count_ref):
+def pack_kernel(route_in, place_in, q_in, out_ref, route_ref, place_ref, q_ref, count_ref, sems):
     rows = q_ref.shape[0]
+    pairs = [(route_in, route_ref), (place_in, place_ref), (q_in, q_ref)]
+    loads = [pltpu.make_async_copy(a, b, sems.at[i]) for i, (a, b) in enumerate(pairs)]
+    for load in loads:
+        load.start()
+    for load in loads[:2]:
+        load.wait()
     lane = iota((SLOTS, 128), 1)
     dest = [jnp.full((SLOTS, 128), -1, jnp.int32)]
 
@@ -48,11 +54,29 @@
 
     dest_rows(route_ref, place_ref, count_ref, add)
     pick = one_hot(iota((out_ref.shape[0], rows), 0) == dest[0][:1, :rows])
-    out_ref[...] = jnp.dot(pick, q_ref[...], preferred_element_type=F32).astype(BF16)
+    loads[2].wait()
+    rows_all = out_ref.shape[0]
+    row, other = iota((rows_all, rows_all), 0), iota((rows_all, rows_all), 1)
+    gather = one_hot((row % SLOTS == CAP) & (row // SLOTS == other // SLOTS))
+    ones = jnp.ones((rows, 128), BF16)
+    taken = jnp.dot(pick, ones, preferred_element_type=F32).astype(BF16)
+    counts = jnp.dot(gather, taken, preferred_element_type=F32)
+    out = jnp.dot(pick, q_ref[...], preferred_element_type=F32)
+    out_ref[:, :128] = (out[:, :128] + counts).astype(BF16)
+    out_ref[:, 128:] = out[:, 128:].astype(BF16)
 
 
 def suffix_kernel(
-    route_ref, place_ref, len_ref, q_ref, k_ref, v_ref, out_ref, lse_ref, dest_ref, count_ref
+    route_ref,
+    place_ref,
+    len_ref,
+    q_ref,
+    k_ref,
+    v_ref,
+    out_ref,
+    lse_ref,
+    dest_ref,
+    count_ref,
 ):
     requests, cache, depth = k_ref.shape
     heads = q_ref.shape[1] // depth
@@ -98,17 +122,45 @@
 
 
 KEYS = 4096
-COLS = 512
-
-
-def prefix_kernel(recv_ref, k_ref, v_ref, out_ref, q_ref, acc_ref, top_ref):
+GROUP = 32
+
+
+def prefix_kernel(recv_ref, k_in, v_in, out_ref, k_ref, v_ref, q_ref, acc_ref, top_ref, sems):
     depth = k_ref.shape[1]
-    heads = recv_ref.shape[1] // depth
-    sources = recv_ref.shape[0] // SLOTS
-    items = sources * CAP
-    rows = heads * items
-    item = iota((items, recv_ref.shape[0]), 0)
-    pick = one_hot(iota(item.shape, 1) == item // CAP * SLOTS + item % CAP)
+    buffer_rows, width = recv_ref.shape
+    heads = width // depth
+    cols = heads * GROUP
+    items = buffer_rows // SLOTS * CAP
+    blocks = items // GROUP
+    steps = k_ref.shape[0] // KEYS
+    loads = []
+    for i in range(steps):
+        sl = pl.ds(i * KEYS, KEYS)
+        loads.append(pltpu.make_async_copy(k_in.at[sl, :], k_ref.at[sl, :], sems.at[0, i]))
+        loads.append(pltpu.make_async_copy(v_in.at[sl, :], v_ref.at[sl, :], sems.at[1, i]))
+    for load in loads:
+        load.start()
+
+    square = (buffer_rows, buffer_rows)
+    row, other = iota(square, 0), iota(square, 1)
+    counts = jnp.dot(
+        one_hot(other == row // SLOTS * SLOTS + CAP),
+        recv_ref[:, :buffer_rows],
+        preferred_element_type=F32,
+    )
+    live = row % SLOTS < counts.astype(jnp.int32)
+    live_bits = one_hot(live)
+    place_down = jnp.dot(one_hot(other < row), live_bits, preferred_element_type=F32)
+    place_down = place_down.astype(jnp.int32)
+    live_across = jnp.where(live, 1.0, 0.0).T
+    place_across = jnp.dot(
+        live_across.astype(BF16), one_hot(row < other), preferred_element_type=F32
+    ).astype(jnp.int32)
+    used = jnp.sum(jnp.where(live[:, :1], 1.0, 0.0)).astype(jnp.int32)
+    active = (used + GROUP - 1) // GROUP
+    short = (items, buffer_rows)
+    pick = one_hot((place_across[:items] == iota(short, 0)) & (live_across[:items] > 0.5))
+
     scale = depth**-0.5 * LOG2E
     for h in range(heads):
         q = jnp.dot(
@@ -116,15 +168,18 @@
         )
         q = q * scale
         high = q.astype(BF16)
-        part = slice(h * items, (h + 1) * items)
-        q_ref[part, :depth] = high
-        q_ref[part, depth:] = (q - high.astype(F32)).astype(BF16)
+        low = (q - high.astype(F32)).astype(BF16)
+        for b in range(blocks):
+            to = slice(b * cols + h * GROUP, b * cols + (h + 1) * GROUP)
+            of = slice(b * GROUP, (b + 1) * GROUP)
+            q_ref[to, :depth] = high[of]
+            q_ref[to, depth:] = low[of]
 
     def scores_of(i, c):
         keys = k_ref[pl.ds(i * KEYS, KEYS), :]
         return lax.dot_general(
             jnp.concatenate([keys, keys], axis=1),
-            q_ref[pl.ds(c * COLS, COLS), :],
+            q_ref[pl.ds(c * cols, cols), :],
             NT,
             preferred_element_type=F32,
         )
@@ -133,20 +188,22 @@
         values = v_ref[pl.ds(i * KEYS, KEYS), :]
         return jnp.concatenate([values.T, jnp.ones((16, KEYS), BF16)], axis=0)
 
-    steps = k_ref.shape[0] // KEYS
-    blocks = rows // COLS
-    acc_ref[...] = jnp.zeros_like(acc_ref)
-
-    def step(i, carry):
+    for c in range(blocks):
+        start = jnp.where(c < active, 0.0, 1.0)
+        acc_ref[:, c * cols : (c + 1) * cols] = jnp.full((acc_ref.shape[0], cols), start, F32)
+    for i in range(steps):
+        loads[2 * i].wait()
+        loads[2 * i + 1].wait()
         turned = value_rows(i)
         for c in range(blocks):
-            weights = jnp.exp2(scores_of(i, c)).astype(BF16)
-            acc_ref[:, c * COLS : (c + 1) * COLS] += jnp.dot(
-                turned, weights, preferred_element_type=F32
-            )
-        return carry
-
-    lax.fori_loop(0, steps, step, 0)
+
+            def add(c=c, i=i, turned=turned):
+                weights = jnp.exp2(scores_of(i, c)).astype(BF16)
+                acc_ref[:, c * cols : (c + 1) * cols] += jnp.dot(
+                    turned, weights, preferred_element_type=F32
+                )
+
+            pl.when(c < active)(add)
     top_ref[...] = jnp.zeros_like(top_ref)
     total = acc_ref[depth : depth + 1, :]
     fine = (total > 2.0**-64) & (total < 2.0**100)
@@ -154,14 +211,14 @@
     @pl.when(jnp.min(jnp.where(fine, 1.0, 0.0)) < 0.5)
     def _():
         for c in range(blocks):
-            sl = slice(c * COLS, (c + 1) * COLS)
+            sl = slice(c * cols, (c + 1) * cols)
 
             def find(i, top):
                 return jnp.maximum(top, jnp.max(scores_of(i, c), axis=0, keepdims=True))
 
-            top = lax.fori_loop(0, steps, find, jnp.full((1, COLS), -jnp.inf, F32))
-            top_ref[:, sl] = jnp.broadcast_to(top, (8, COLS))
-            acc_ref[:, sl] = jnp.zeros((acc_ref.shape[0], COLS), F32)
+            top = lax.fori_loop(0, steps, find, jnp.full((1, cols), -jnp.inf, F32))
+            top_ref[:, sl] = jnp.broadcast_to(top, (8, cols))
+            acc_ref[:, sl] = jnp.zeros((acc_ref.shape[0], cols), F32)
 
             def again(i, carry):
                 weights = jnp.exp2(scores_of(i, c) - top).astype(BF16)
@@ -176,29 +233,39 @@
     high = lse.astype(BF16).astype(F32)
     middle = (lse - high).astype(BF16).astype(F32)
     low = lse - high - middle
-    wide = iota((8, rows), 0)
+    wide = iota((8, blocks * cols), 0)
     pieces = jnp.where(wide == 0, high, jnp.where(wide == 1, middle, low))
-    row = iota((recv_ref.shape[0], items), 0)
-    column = iota(row.shape, 1)
-    result_row = one_hot(row == column // CAP * SLOTS + column % CAP)
-    lse_row = one_hot(row == column // CAP * SLOTS + CAP)
+    tall = (buffer_rows, items)
+    result_row = one_hot((place_down[:, :items] == iota(tall, 1)) & live[:, :items])
+    gather = one_hot((row % SLOTS == CAP) & (row // SLOTS == other // SLOTS))
+    lse_row = jnp.dot(gather, result_row, preferred_element_type=F32).astype(BF16)
     spread = jnp.concatenate([result_row, lse_row], axis=1)
-    offset = iota((items, depth), 1) - 3 * (iota((items, depth), 0) % CAP)
-    for h in range(heads):
-        part = slice(h * items, (h + 1) * items)
-        out = (acc_ref[:depth, part] * inverse[:, part]).T
-        three = pieces[:, part].T
-        packed = jnp.where(
-            offset == 0,
-            three[:, 0:1],
-            jnp.where(
-                offset == 1, three[:, 1:2], jnp.where(offset == 2, three[:, 2:3], 0.0)
-            ),
-        )
-        both = jnp.concatenate([out.astype(BF16), packed.astype(BF16)], axis=0)
-        out_ref[:, h * depth : (h + 1) * depth] = jnp.dot(
-            spread, both, preferred_element_type=F32
-        ).astype(BF16)
+    slot = jnp.dot(
+        pick, (row % SLOTS).astype(F32).astype(BF16), preferred_element_type=F32
+    ).astype(jnp.int32)
+    offset = iota((items, depth), 1) - 3 * slot[:, :depth]
+    four = depth // GROUP
+    for h0 in range(0, heads, four):
+        outs, threes = [], []
+        for b in range(blocks):
+            sl = slice(b * cols + h0 * GROUP, b * cols + (h0 + four) * GROUP)
+            outs.append((acc_ref[:depth, sl] * inverse[:, sl]).T)
+            threes.append(pieces[:, sl].T)
+        for h in range(four):
+            part = slice(h * GROUP, (h + 1) * GROUP)
+            out = jnp.concatenate([x[part] for x in outs], axis=0)
+            three = jnp.concatenate([x[part] for x in threes], axis=0)
+            packed = jnp.where(
+                offset == 0,
+                three[:, 0:1],
+                jnp.where(
+                    offset == 1, three[:, 1:2], jnp.where(offset == 2, three[:, 2:3], 0.0)
+                ),
+            )
+            both = jnp.concatenate([out.astype(BF16), packed.astype(BF16)], axis=0)
+            out_ref[:, (h0 + h) * depth : (h0 + h + 1) * depth] = jnp.dot(
+                spread, both, preferred_element_type=F32
+            ).astype(BF16)
 
 
 def merge_kernel(back_ref, dest_ref, suffix_ref, lse_ref, out_ref):
@@ -227,18 +294,20 @@
             out_ref[copy, :, sl] = merged
 
 
+TILE = 256
+
+
 def project_kernel(core_ref, a_ref, w_ref, mine_ref, other_ref):
     core = core_ref[0]
     block = a_ref.shape[0] // 8
+    half = 4 * block
     order = [(y, core) for y in range(4)] + [(y, 1 - core) for y in range(4)]
     a = jnp.concatenate(
         [a_ref[pl.ds(pl.multiple_of((2 * y + c) * block, block), block), :] for y, c in order],
         axis=0,
     )
-    half = a.shape[0] // 2
-    tile = 256
-    for n in range(w_ref.shape[1] // tile):
-        sl = slice(n * tile, (n + 1) * tile)
+    for n in range(w_ref.shape[1] // TILE):
+        sl = slice(n * TILE, (n + 1) * TILE)
         out = jnp.dot(a, w_ref[:, sl], preferred_element_type=F32)
         mine_ref[:, sl] = out[:half]
         other_ref[:, sl] = out[half:].astype(BF16)
@@ -267,7 +336,7 @@
     ).astype(BF16)
 
 
-def call(kernel, outs, specs, scratch=(), cost=None):
+def call(kernel, outs, specs, scratch=(), cost=None, mib=16):
     shapes = [jax.ShapeDtypeStruct(shape, dtype) for shape, dtype in outs]
     many = len(shapes) > 1
     return pl.pallas_call(
@@ -276,7 +345,7 @@
         in_specs=specs,
         out_specs=[VMEM] * len(shapes) if many else VMEM,
         scratch_shapes=list(scratch),
-        compiler_params=PARAMS,
+        compiler_params=pltpu.CompilerParams(vmem_limit_bytes=mib * 2**20),
         cost_estimate=cost,
     )
 
@@ -295,14 +364,24 @@
 
     def exchange(x):
         shape = x.shape
-        x = lax.all_to_all(
-            x.reshape(owners, -1, width), "pfx", split_axis=0, concat_axis=0, tiled=True
-        )
+        x = x.reshape(owners, -1, shape[1])
+        x = lax.all_to_all(x, "pfx", split_axis=0, concat_axis=0, tiled=True)
         return x.reshape(shape)
 
-    packed = call(pack_kernel, [((buffer_rows, width), BF16)], [SMEM, SMEM, VMEM], [count])(
-        route, place, queries
-    )
+    packed = call(
+        pack_kernel,
+        [((buffer_rows, width), BF16)],
+        [HBM, HBM, HBM],
+        [
+            pltpu.SMEM(route.shape, jnp.int32),
+            pltpu.SMEM(place.shape, jnp.int32),
+            pltpu.VMEM(queries.shape, BF16),
+            count,
+            pltpu.SemaphoreType.DMA((3,)),
+        ],
+        None,
+        62,
+    )(route, place, queries)
     received = exchange(packed)
     suffix_out, suffix_lse, dest = call(
         suffix_kernel,
@@ -310,24 +389,28 @@
         [SMEM, SMEM, SMEM, VMEM, VMEM, VMEM],
         [count],
         pl.CostEstimate(flops=2 * 10**9, bytes_accessed=5 * 10**6, transcendentals=2 * 10**6),
+        32,
     )(route, place, suffix_len, queries, suffix_keys, suffix_values)
     prefix = call(
         prefix_kernel,
         [((buffer_rows, width), BF16)],
-        [VMEM, VMEM, VMEM],
+        [VMEM, HBM, HBM],
         [
+            pltpu.VMEM(prefix_keys.shape, BF16),
+            pltpu.VMEM(prefix_values.shape, BF16),
             pltpu.VMEM((rows, 2 * HDIM), BF16),
             pltpu.VMEM((HDIM + 16, rows), F32),
             pltpu.VMEM((8, rows), F32),
+            pltpu.SemaphoreType.DMA((2, prefix_keys.shape[0] // KEYS)),
         ],
         pl.CostEstimate(flops=10**10, bytes_accessed=5 * 10**6, transcendentals=12 * 10**6),
+        62,
     )(received, prefix_keys, prefix_values)
     back = exchange(prefix)
     copies = call(merge_kernel, [((owners, requests, width), BF16)], [VMEM] * 4)(
         back, dest, suffix_out, suffix_lse
     )
-    attention = lax.all_to_all(copies, "pfx", split_axis=0, concat_axis=0, tiled=True)
-    attention = attention.reshape(owners * requests, width)
+    attention = exchange(copies.reshape(owners * requests, width))
     columns = out_weight.shape[1]
     half = owners * requests // 2
     mine, other = call(
@@ -336,6 +419,7 @@
         [SMEM, VMEM, VMEM],
         (),
         pl.CostEstimate(flops=2 * 10**9, bytes_accessed=8 * 10**6, transcendentals=0),
+        24,
     )(core, attention, out_weight)
     got = lax.ppermute(other, "tp", [(i, i ^ 1) for i in range(8)])
     block = half // 4

time: 126 us -> 125 us (level)
  starting transfers between devices: 18.3 us -> 25.1 us
  Pallas kernels: 47.2 us -> 41.1 us
  local copies, waits for them, and re-layouts: 7 us -> 5.38 us
    all_to_all x2, starting transfers between devices: 7.51 us -> 14.6 us  [exchange(): x = lax.all_to_all(x, 'pfx', split_axis=0, concat_axis=0, tiled=True)]
    pallas_call x2, Pallas kernels: 34.4 us -> 30.5 us  [the longest x1 28.4 us: on_device(): call(prefix_kernel, [((buffer_rows, width), BF16)], [VMEM, HBM, HBM], [pl...]
    pallas_call x1, Pallas kernels: 5.32 us -> 3.12 us  [on_device(): call(project_kernel, [((half, columns), F32), ((half, columns), BF16)], [...]
    unnamed x22 -> x14, local copies, waits for them, and re-layouts: 7 us -> 5.38 us
where the time goes in v2:
time: 125 us; the launch traced here: 124 us
  Pallas kernels  41.1 us (33%)
  waiting for transfers between devices  33.6 us (27%)
  starting transfers between devices  25.1 us (20%)
  blocking collectives  18.8 us (15%)
  local copies, waits for them, and re-layouts  5.38 us (4%)
    pallas_call x1, Pallas kernels, on_device(): call(prefix_kernel, [((buffer_rows, width), BF16)], [VMEM, HBM, HBM], [pl...  28.4 us
    all_to_all x2, waiting for transfers between devices, exchange(): x = lax.all_to_all(x, 'pfx', split_axis=0, concat_axis=0, tiled=True)  26.8 us
    all_to_all x1, blocking collectives, exchange(): x = lax.all_to_all(x, 'pfx', split_axis=0, concat_axis=0, tiled=True)  18.8 us
    all_to_all x2, starting transfers between devices, exchange(): x = lax.all_to_all(x, 'pfx', split_axis=0, concat_axis=0, tiled=True)  14.6 us
    ppermute x1, starting transfers between devices, on_device(): got = lax.ppermute(other, 'tp', [(i, i ^ 1) for i in range(8)])  5.42 us
    unnamed x14, local copies, waits for them, and re-layouts  5.38 us
    ppermute x3, starting transfers between devices, on_device(): lax.ppermute(part, 'tp', [(i, (i + 2 * k) % 8) for i in range(8)])  5.06 us
    ppermute x3, waiting for transfers between devices, on_device(): lax.ppermute(part, 'tp', [(i, (i + 2 * k) % 8) for i in range(8)])  4.99 us
  transfers between devices with their start and end apart: 6, of which 5 were waited for; matrix products, arithmetic and copies ran while one was open for 0% of the time, Pallas kernels for 4%

profile of v2, /device:TPU:1, one launch (start us, length us, event | category | flops | bytes accessed | tf_op | source)
XLA Modules:
  0.0 124.1 jit_solution(364451109748980879)
XLA Ops:
  0.0 2.2 %shard_map.91 = bf16[128,2048]{1,0:T(8,128)(2,1)} custom-call(s32[32]{0:T(128)} %route_ref.1, s32[16]{0:T(128)} %place_ref.1, bf16[32,2048]{1,0:T(8,128)(2,1)} %q_ref.1), custom_call_target="tpu_custom_call" | custom-call | tf_op jit(solution)/shard_map/pallas_call | solution.py:371
  2.2 18.8 %all_to_all.15 = bf16[16,8,2048]{2,1,0:T(8,128)(2,1)} all-to-all(bf16[16,8,2048]{2,1,0:T(8,128)(2,1)} %bitcast.9), channel_id=1, replica_groups=mesh['pfx'=16,'tp'=8] {'pfx'}, dimensions={0} | all-to-all | bytes 1048576 | tf_op jit(solution)/shard_map/all_to_all | solution.py:368
  21.0 0.0 copy-start
  21.0 0.0 copy-start.1
  21.0 0.0 copy-start.2
  21.0 0.0 copy-start.6
  21.0 28.4 %shard_map.92 = bf16[128,2048]{1,0:T(8,128)(2,1)} custom-call(bf16[128,2048]{1,0:T(8,128)(2,1)} %bitcast.11, bf16[8192,128]{1,0:T(8,128)(2,1)} %k_in.1, bf16[8192,128]{1,0:T(8,128)(2,1)} %v_in.1), custom_call_target="tpu_custom_call" | custom-call | flops 10000000000 | bytes 5000000 | tf_op jit(solution)/shard_map/pallas_call | solution.py:394
  49.4 9.5 %all-to-all-start.1 = ((bf16[16,8,2048]{2,1,0:T(8,128)(2,1)}), bf16[16,8,2048]{2,1,0:T(8,128)(2,1)S(1)}, u32[]{:S(2)}, u32[]{:S(2)}) async-start(bf16[16,8,2048]{2,1,0:T(8,128)(2,1)} %bitcast.10), calls=%async_computation.1 | async-start | bytes 1048576 | tf_op jit(solution)/shard_map/all_to_all | solution.py:368
  58.9 0.0 copy-done
  58.9 0.0 copy-done.1
  58.9 0.0 copy-done.2
  58.9 0.0 copy-done.6
  58.9 0.0 copy-start.4
  59.0 1.6 %copy-done.4 = bf16[32,256,128]{2,1,0:T(8,128)(2,1)S(1)} copy-done((bf16[32,256,128]{2,1,0:T(8,128)(2,1)S(1)}, bf16[32,256,128]{2,1,0:T(8,128)(2,1)}, u32[]{:S(2)}) %copy-start.4) | copy-done | bytes 2097176
  60.5 0.0 copy-start.5
  60.5 1.6 %copy-done.5 = bf16[32,256,128]{2,1,0:T(8,128)(2,1)S(1)} copy-done((bf16[32,256,128]{2,1,0:T(8,128)(2,1)S(1)}, bf16[32,256,128]{2,1,0:T(8,128)(2,1)}, u32[]{:S(2)}) %copy-start.5) | copy-done | bytes 2097176
  62.1 4.5 %shard_map.93 = (f32[32,2048]{1,0:T(8,128)S(1)}, f32[32,2048]{1,0:T(8,128)S(1)}, s32[32,128]{1,0:T(8,128)S(1)}) custom-call(s32[32]{0:T(128)S(1)} %copy-done.1, s32[16]{0:T(128)S(1)} %copy-done.2, s32[32]{0:T(128)S(1)} %copy-done.6, bf16[32,2048]{1,0:T(8,128)(2,1)S(1)} %copy-done, bf16[32,256,128]{2,1,0:T(8,128)(2,1)S(1)} %copy-done.4, ...), custom_call_target="tpu_custom_call" | custom-call | flops 2000000000 | bytes 5000000 | tf_op jit(solution)/shard_map/pallas_call | solution.py:386
  66.6 1.5 %all-to-all-done.1 = bf16[16,8,2048]{2,1,0:T(8,128)(2,1)S(1)} async-done(((bf16[16,8,2048]{2,1,0:T(8,128)(2,1)}), bf16[16,8,2048]{2,1,0:T(8,128)(2,1)S(1)}, u32[]{:S(2)}, u32[]{:S(2)}) %all-to-all-start.1) | async-done | bytes 524320 | tf_op jit(solution)/shard_map/all_to_all | solution.py:368
  68.1 2.2 %shard_map.94 = bf16[16,32,2048]{2,1,0:T(8,128)(2,1)} custom-call(bf16[128,2048]{1,0:T(8,128)(2,1)S(1)} %bitcast.8, s32[32,128]{1,0:T(8,128)S(1)} %get-tuple-element.14.dest_ref, f32[32,2048]{1,0:T(8,128)S(1)} %get-tuple-element.15.suffix_ref, f32[32,2048]{1,0:T(8,128)S(1)} %get-tuple-element.16.lse_ref), custom_call_target="tpu_custom_call" | custom-call | tf_op jit(solution)/shard_map/pallas_call | solution.py:410
  70.3 5.1 %all-to-all-start.2 = ((bf16[16,32,2048]{2,1,0:T(8,128)(2,1)}), bf16[16,32,2048]{2,1,0:T(8,128)(2,1)S(1)}, u32[]{:S(2)}, u32[]{:S(2)}) async-start(bf16[16,32,2048]{2,1,0:T(8,128)(2,1)} %shard_map.94), calls=%async_computation.2 | async-start | bytes 4194304 | tf_op jit(solution)/shard_map/all_to_all | solution.py:368
  75.4 25.3 %all-to-all-done.2 = bf16[16,32,2048]{2,1,0:T(8,128)(2,1)S(1)} async-done(((bf16[16,32,2048]{2,1,0:T(8,128)(2,1)}), bf16[16,32,2048]{2,1,0:T(8,128)(2,1)S(1)}, u32[]{:S(2)}, u32[]{:S(2)}) %all-to-all-start.2) | async-done | bytes 2097184 | tf_op jit(solution)/shard_map/all_to_all | solution.py:368
  100.7 0.0 copy-start.3
  100.7 2.2 %copy-done.3 = bf16[2048,1024]{1,0:T(8,128)(2,1)S(1)} copy-done((bf16[2048,1024]{1,0:T(8,128)(2,1)S(1)}, bf16[2048,1024]{1,0:T(8,128)(2,1)}, u32[]{:S(2)}) %copy-start.3) | copy-done | bytes 4194328
  102.9 3.1 %shard_map.95 = (f32[256,1024]{1,0:T(8,128)S(1)}, bf16[256,1024]{1,0:T(8,128)(2,1)}) custom-call(s32[1]{0:T(128)} %bitcast.1.core_ref, bf16[512,2048]{1,0:T(8,128)(2,1)S(1)} %bitcast.7, bf16[2048,1024]{1,0:T(8,128)(2,1)S(1)} %copy-done.3), custom_call_target="tpu_custom_call" | custom-call | flops 2000000000 | bytes 8000000 | tf_op jit(solution)/shard_map/pallas_call | solution.py:416
  106.1 5.4 %collective-permute-start = (bf16[256,1024]{1,0:T(8,128)(2,1)}, bf16[256,1024]{1,0:T(8,128)(2,1)S(1)}, u32[]{:S(2)}, u32[]{:S(2)}) collective-permute-start(bf16[256,1024]{1,0:T(8,128)(2,1)} %get-tuple-element.18), channel_id=1, source_target_pairs={{0,1},{1,0},{2,3},{3,2},{4,5},{5,4},{6,7},{7,6},{8,9},{9,8},{10,11... | collective-permute-start | bytes 1572872 | tf_op jit(solution)/shard_map/ppermute | solution.py:424
  111.5 1.7 %collective-permute-done.got_ref = bf16[256,1024]{1,0:T(8,128)(2,1)S(1)} collective-permute-done((bf16[256,1024]{1,0:T(8,128)(2,1)}, bf16[256,1024]{1,0:T(8,128)(2,1)S(1)}, u32[]{:S(2)}, u32[]{:S(2)}) %collective-permute-start) | collective-permute-done | bytes 524320 | tf_op jit(solution)/shard_map/ppermute | solution.py:424
  113.2 0.1 shard_map.96
  113.3 1.4 %collective-permute-start.1 = (bf16[64,1024]{1,0:T(8,128)(2,1)S(1)}, bf16[64,1024]{1,0:T(8,128)(2,1)S(1)}, u32[]{:S(2)}, u32[]{:S(2)}) collective-permute-start(bf16[64,1024]{1,0:T(8,128)(2,1)S(1)} %get-tuple-element.20), channel_id=1, source_target_pairs={{0,2},{1,3},{2,4},{3,5},{4,6},{5,7},{6,0},{7,1},{8,10},{9,11},{10,... | collective-permute-start | bytes 393224 | tf_op jit(solution)/shard_map/ppermute | solution.py:430
  114.7 2.6 %collective-permute-start.2 = (bf16[64,1024]{1,0:T(8,128)(2,1)S(1)}, bf16[64,1024]{1,0:T(8,128)(2,1)S(1)}, u32[]{:S(2)}, u32[]{:S(2)}) collective-permute-start(bf16[64,1024]{1,0:T(8,128)(2,1)S(1)} %get-tuple-element.21), channel_id=1, source_target_pairs={{0,4},{1,5},{2,6},{3,7},{4,0},{5,1},{6,2},{7,3},{8,12},{9,13},{10,... | collective-permute-start | bytes 393224 | tf_op jit(solution)/shard_map/ppermute | solution.py:430
  117.3 1.1 collective-permute-start.3
  118.4 1.1 collective-permute-done.1.one_ref
  119.4 3.9 %collective-permute-done.2.two_ref = bf16[64,1024]{1,0:T(8,128)(2,1)S(1)} collective-permute-done((bf16[64,1024]{1,0:T(8,128)(2,1)S(1)}, bf16[64,1024]{1,0:T(8,128)(2,1)S(1)}, u32[]{:S(2)}, u32[]{:S(2)}) %collective-permute-start.2) | collective-permute-done | bytes 131104 | tf_op jit(solution)/shard_map/ppermute | solution.py:430
  123.3 0.0 collective-permute-done.3.three_ref
  123.4 0.7 shard_map.97
Async XLA Ops:
  21.0 37.9 %copy-start = (bf16[32,2048]{1,0:T(8,128)(2,1)S(1)}, bf16[32,2048]{1,0:T(8,128)(2,1)}, u32[]{:S(2)}) copy-start(bf16[32,2048]{1,0:T(8,128)(2,1)} %q_ref.1) | copy-start | bytes 393220
  21.0 37.9 %copy-start.1 = (s32[32]{0:T(128)S(1)}, s32[32]{0:T(128)}, u32[]{:S(2)}) copy-start(s32[32]{0:T(128)} %route_ref.1) | copy-start | bytes 388
  21.0 37.9 %copy-start.2 = (s32[16]{0:T(128)S(1)}, s32[16]{0:T(128)}, u32[]{:S(2)}) copy-start(s32[16]{0:T(128)} %place_ref.1) | copy-start | bytes 196
  21.0 37.9 %copy-start.6 = (s32[32]{0:T(128)S(1)}, s32[32]{0:T(128)}, u32[]{:S(2)}) copy-start(s32[32]{0:T(128)} %len_ref.1) | copy-start | bytes 388
  49.4 18.7 %all-to-all-start.1 = ((bf16[16,8,2048]{2,1,0:T(8,128)(2,1)}), bf16[16,8,2048]{2,1,0:T(8,128)(2,1)S(1)}, u32[]{:S(2)}, u32[]{:S(2)}) async-start(bf16[16,8,2048]{2,1,0:T(8,128)(2,1)} %bitcast.10), calls=%async_computation.1 | async-start | bytes 1048576 | tf_op jit(solution)/shard_map/all_to_all | solution.py:368
  58.9 1.6 %copy-start.4 = (bf16[32,256,128]{2,1,0:T(8,128)(2,1)S(1)}, bf16[32,256,128]{2,1,0:T(8,128)(2,1)}, u32[]{:S(2)}) copy-start(bf16[32,256,128]{2,1,0:T(8,128)(2,1)} %k_ref.1) | copy-start | bytes 6291460
  60.5 1.6 %copy-start.5 = (bf16[32,256,128]{2,1,0:T(8,128)(2,1)S(1)}, bf16[32,256,128]{2,1,0:T(8,128)(2,1)}, u32[]{:S(2)}) copy-start(bf16[32,256,128]{2,1,0:T(8,128)(2,1)} %v_ref.1) | copy-start | bytes 6291460
  70.3 30.5 %all-to-all-start.2 = ((bf16[16,32,2048]{2,1,0:T(8,128)(2,1)}), bf16[16,32,2048]{2,1,0:T(8,128)(2,1)S(1)}, u32[]{:S(2)}, u32[]{:S(2)}) async-start(bf16[16,32,2048]{2,1,0:T(8,128)(2,1)} %shard_map.94), calls=%async_computation.2 | async-start | bytes 4194304 | tf_op jit(solution)/shard_map/all_to_all | solution.py:368
  100.7 2.2 %copy-start.3 = (bf16[2048,1024]{1,0:T(8,128)(2,1)S(1)}, bf16[2048,1024]{1,0:T(8,128)(2,1)}, u32[]{:S(2)}) copy-start(bf16[2048,1024]{1,0:T(8,128)(2,1)} %w_ref.1) | copy-start | bytes 12582916
  106.1 7.2 %collective-permute-start = (bf16[256,1024]{1,0:T(8,128)(2,1)}, bf16[256,1024]{1,0:T(8,128)(2,1)S(1)}, u32[]{:S(2)}, u32[]{:S(2)}) collective-permute-start(bf16[256,1024]{1,0:T(8,128)(2,1)} %get-tuple-element.18), channel_id=1, source_target_pairs={{0,1},{1,0},{2,3},{3,2},{4,5},{5,4},{6,7},{7,6},{8,9},{9,8},{10,11... | collective-permute-start | bytes 1572872 | tf_op jit(solution)/shard_map/ppermute | solution.py:424
  113.3 6.1 %collective-permute-start.1 = (bf16[64,1024]{1,0:T(8,128)(2,1)S(1)}, bf16[64,1024]{1,0:T(8,128)(2,1)S(1)}, u32[]{:S(2)}, u32[]{:S(2)}) collective-permute-start(bf16[64,1024]{1,0:T(8,128)(2,1)S(1)} %get-tuple-element.20), channel_id=1, source_target_pairs={{0,2},{1,3},{2,4},{3,5},{4,6},{5,7},{6,0},{7,1},{8,10},{9,11},{10,... | collective-permute-start | bytes 393224 | tf_op jit(solution)/shard_map/ppermute | solution.py:430
  114.7 8.7 %collective-permute-start.2 = (bf16[64,1024]{1,0:T(8,128)(2,1)S(1)}, bf16[64,1024]{1,0:T(8,128)(2,1)S(1)}, u32[]{:S(2)}, u32[]{:S(2)}) collective-permute-start(bf16[64,1024]{1,0:T(8,128)(2,1)S(1)} %get-tuple-element.21), channel_id=1, source_target_pairs={{0,4},{1,5},{2,6},{3,7},{4,0},{5,1},{6,2},{7,3},{8,12},{9,13},{10,... | collective-permute-start | bytes 393224 | tf_op jit(solution)/shard_map/ppermute | solution.py:430
  117.3 6.1 %collective-permute-start.3 = (bf16[64,1024]{1,0:T(8,128)(2,1)S(1)}, bf16[64,1024]{1,0:T(8,128)(2,1)S(1)}, u32[]{:S(2)}, u32[]{:S(2)}) collective-permute-start(bf16[64,1024]{1,0:T(8,128)(2,1)S(1)} %get-tuple-element.22), channel_id=1, source_target_pairs={{0,6},{1,7},{2,0},{3,1},{4,2},{5,3},{6,4},{7,5},{8,14},{9,15},{10,... | collective-permute-start | bytes 393224 | tf_op jit(solution)/shard_map/ppermute | solution.py:430

commit v3 on v2

--- a/solution.py
+++ b/solution.py
@@ -9,6 +9,7 @@
 
 HDIM = 128
 SLOTS = 8
+EXTRA = 128
 CAP = 6
 LOG2E = 1.4426950408889634
 LN2 = 0.6931471805599453
@@ -55,15 +56,10 @@
     dest_rows(route_ref, place_ref, count_ref, add)
     pick = one_hot(iota((out_ref.shape[0], rows), 0) == dest[0][:1, :rows])
     loads[2].wait()
-    rows_all = out_ref.shape[0]
-    row, other = iota((rows_all, rows_all), 0), iota((rows_all, rows_all), 1)
-    gather = one_hot((row % SLOTS == CAP) & (row // SLOTS == other // SLOTS))
-    ones = jnp.ones((rows, 128), BF16)
-    taken = jnp.dot(pick, ones, preferred_element_type=F32).astype(BF16)
-    counts = jnp.dot(gather, taken, preferred_element_type=F32)
-    out = jnp.dot(pick, q_ref[...], preferred_element_type=F32)
-    out_ref[:, :128] = (out[:, :128] + counts).astype(BF16)
-    out_ref[:, 128:] = out[:, 128:].astype(BF16)
+    width = q_ref.shape[1]
+    live = jnp.dot(pick, jnp.ones((rows, EXTRA), BF16), preferred_element_type=F32)
+    out_ref[:, :width] = jnp.dot(pick, q_ref[...], preferred_element_type=F32).astype(BF16)
+    out_ref[:, width:] = live.astype(BF16)
 
 
 def suffix_kernel(
@@ -121,89 +117,99 @@
             lse_ref[sl, h * depth : (h + 1) * depth] = lse[part]
 
 
-KEYS = 4096
+CHUNKS = (1024, 3072, 4096)
 GROUP = 32
 
 
 def prefix_kernel(recv_ref, k_in, v_in, out_ref, k_ref, v_ref, q_ref, acc_ref, top_ref, sems):
     depth = k_ref.shape[1]
-    buffer_rows, width = recv_ref.shape
+    buffer_rows = recv_ref.shape[0]
+    width = recv_ref.shape[1] - EXTRA
     heads = width // depth
     cols = heads * GROUP
     items = buffer_rows // SLOTS * CAP
     blocks = items // GROUP
-    steps = k_ref.shape[0] // KEYS
-    loads = []
-    for i in range(steps):
-        sl = pl.ds(i * KEYS, KEYS)
-        loads.append(pltpu.make_async_copy(k_in.at[sl, :], k_ref.at[sl, :], sems.at[0, i]))
-        loads.append(pltpu.make_async_copy(v_in.at[sl, :], v_ref.at[sl, :], sems.at[1, i]))
-    for load in loads:
+    steps = len(CHUNKS)
+    spans = [slice(sum(CHUNKS[:i]), sum(CHUNKS[: i + 1])) for i in range(steps)]
+    loads = [
+        [
+            pltpu.make_async_copy(k_in.at[sl, :], k_ref.at[sl, :], sems.at[0, i]),
+            pltpu.make_async_copy(v_in.at[sl, :], v_ref.at[sl, :], sems.at[1, i]),
+        ]
+        for i, sl in enumerate(spans)
+    ]
+    for load in loads[0]:
         load.start()
 
     square = (buffer_rows, buffer_rows)
     row, other = iota(square, 0), iota(square, 1)
-    counts = jnp.dot(
-        one_hot(other == row // SLOTS * SLOTS + CAP),
-        recv_ref[:, :buffer_rows],
-        preferred_element_type=F32,
-    )
-    live = row % SLOTS < counts.astype(jnp.int32)
-    live_bits = one_hot(live)
-    place_down = jnp.dot(one_hot(other < row), live_bits, preferred_element_type=F32)
-    place_down = place_down.astype(jnp.int32)
-    live_across = jnp.where(live, 1.0, 0.0).T
-    place_across = jnp.dot(
-        live_across.astype(BF16), one_hot(row < other), preferred_element_type=F32
-    ).astype(jnp.int32)
-    used = jnp.sum(jnp.where(live[:, :1], 1.0, 0.0)).astype(jnp.int32)
+    bits = recv_ref[:, width:]
+    place_down = jnp.dot(one_hot(other < row), bits, preferred_element_type=F32)
+    place_across = lax.dot_general(
+        bits, one_hot(row < other), (((0,), (0,)), ((), ())), preferred_element_type=F32
+    )
+    live_across = lax.dot_general(
+        bits, one_hot(row == other), (((0,), (0,)), ((), ())), preferred_element_type=F32
+    )
+    live = bits.astype(F32) > 0.5
+    place_down = jnp.where(live, place_down.astype(jnp.int32), -1)
+    used = (jnp.max(place_down) + 1).astype(jnp.int32)
     active = (used + GROUP - 1) // GROUP
     short = (items, buffer_rows)
-    pick = one_hot((place_across[:items] == iota(short, 0)) & (live_across[:items] > 0.5))
+    pick = one_hot(
+        (place_across[:items].astype(jnp.int32) == iota(short, 0)) & (live_across[:items] > 0.5)
+    )
 
     scale = depth**-0.5 * LOG2E
-    for h in range(heads):
+    four = 4
+    for h0 in range(0, heads, four):
         q = jnp.dot(
-            pick, recv_ref[:, h * depth : (h + 1) * depth], preferred_element_type=F32
-        )
-        q = q * scale
-        high = q.astype(BF16)
-        low = (q - high.astype(F32)).astype(BF16)
+            pick, recv_ref[:, h0 * depth : (h0 + four) * depth], preferred_element_type=F32
+        ).astype(BF16)
         for b in range(blocks):
-            to = slice(b * cols + h * GROUP, b * cols + (h + 1) * GROUP)
             of = slice(b * GROUP, (b + 1) * GROUP)
-            q_ref[to, :depth] = high[of]
-            q_ref[to, depth:] = low[of]
-
-    def scores_of(i, c):
-        keys = k_ref[pl.ds(i * KEYS, KEYS), :]
-        return lax.dot_general(
-            jnp.concatenate([keys, keys], axis=1),
-            q_ref[pl.ds(c * cols, cols), :],
-            NT,
-            preferred_element_type=F32,
-        )
-
-    def value_rows(i):
-        values = v_ref[pl.ds(i * KEYS, KEYS), :]
-        return jnp.concatenate([values.T, jnp.ones((16, KEYS), BF16)], axis=0)
+            for h in range(four):
+                start = b * cols + (h0 + h) * GROUP
+                q_ref[start : start + GROUP, :] = q[of, h * depth : (h + 1) * depth]
+
+    def scores_of(span, c):
+        q = q_ref[c * cols : (c + 1) * cols, :]
+        return lax.dot_general(k_ref[span, :], q, NT, preferred_element_type=F32) * scale
+
+    def value_rows(span):
+        values = v_ref[span, :]
+        return jnp.concatenate([values.T, jnp.ones((16, values.shape[0]), BF16)], axis=0)
 
     for c in range(blocks):
         start = jnp.where(c < active, 0.0, 1.0)
         acc_ref[:, c * cols : (c + 1) * cols] = jnp.full((acc_ref.shape[0], cols), start, F32)
-    for i in range(steps):
-        loads[2 * i].wait()
-        loads[2 * i + 1].wait()
-        turned = value_rows(i)
-        for c in range(blocks):
-
-            def add(c=c, i=i, turned=turned):
-                weights = jnp.exp2(scores_of(i, c)).astype(BF16)
-                acc_ref[:, c * cols : (c + 1) * cols] += jnp.dot(
-                    turned, weights, preferred_element_type=F32
-                )
-
-            pl.when(c < active)(add)
+
+    def attend(block):
+        for i, span in enumerate(spans):
+            for load in loads[i]:
+                load.wait()
+            if i + 1 < steps:
+                for load in loads[i + 1]:
+                    load.start()
+            turned = value_rows(span)
+            for c in range(blocks):
+
+                def body(c=c, span=span, turned=turned):
+                    weights = jnp.exp2(scores_of(span, c)).astype(BF16)
+                    acc_ref[:, c * cols : (c + 1) * cols] += jnp.dot(
+                        turned, weights, preferred_element_type=F32
+                    )
+
+                block(c, body)
+
+    @pl.when(active == blocks)
+    def _():
+        attend(lambda c, body: body())
+
+    @pl.when(active < blocks)
+    def _():
+        attend(lambda c, body: pl.when(c < active)(body))
+
     top_ref[...] = jnp.zeros_like(top_ref)
     total = acc_ref[depth : depth + 1, :]
     fine = (total > 2.0**-64) & (total < 2.0**100)
@@ -214,18 +220,21 @@
             sl = slice(c * cols, (c + 1) * cols)
 
             def find(i, top):
-                return jnp.maximum(top, jnp.max(scores_of(i, c), axis=0, keepdims=True))
-
-            top = lax.fori_loop(0, steps, find, jnp.full((1, cols), -jnp.inf, F32))
+                span = pl.ds(pl.multiple_of(i * CHUNKS[0], CHUNKS[0]), CHUNKS[0])
+                return jnp.maximum(top, jnp.max(scores_of(span, c), axis=0, keepdims=True))
+
+            again_steps = k_ref.shape[0] // CHUNKS[0]
+            top = lax.fori_loop(0, again_steps, find, jnp.full((1, cols), -jnp.inf, F32))
             top_ref[:, sl] = jnp.broadcast_to(top, (8, cols))
             acc_ref[:, sl] = jnp.zeros((acc_ref.shape[0], cols), F32)
 
             def again(i, carry):
-                weights = jnp.exp2(scores_of(i, c) - top).astype(BF16)
-                acc_ref[:, sl] += jnp.dot(value_rows(i), weights, preferred_element_type=F32)
+                span = pl.ds(pl.multiple_of(i * CHUNKS[0], CHUNKS[0]), CHUNKS[0])
+                weights = jnp.exp2(scores_of(span, c) - top).astype(BF16)
+                acc_ref[:, sl] += jnp.dot(value_rows(span), weights, preferred_element_type=F32)
                 return carry
 
-            lax.fori_loop(0, steps, again, 0)
+            lax.fori_loop(0, again_steps, again, 0)
 
     total = acc_ref[depth : depth + 1, :]
     inverse = 1.0 / total
@@ -234,54 +243,51 @@
     middle = (lse - high).astype(BF16).astype(F32)
     low = lse - high - middle
     wide = iota((8, blocks * cols), 0)
-    pieces = jnp.where(wide == 0, high, jnp.where(wide == 1, middle, low))
+    pieces = jnp.where(
+        wide == 0, high, jnp.where(wide == 1, middle, jnp.where(wide == 2, low, 0.0))
+    ).astype(BF16)
     tall = (buffer_rows, items)
-    result_row = one_hot((place_down[:, :items] == iota(tall, 1)) & live[:, :items])
-    gather = one_hot((row % SLOTS == CAP) & (row // SLOTS == other // SLOTS))
-    lse_row = jnp.dot(gather, result_row, preferred_element_type=F32).astype(BF16)
-    spread = jnp.concatenate([result_row, lse_row], axis=1)
-    slot = jnp.dot(
-        pick, (row % SLOTS).astype(F32).astype(BF16), preferred_element_type=F32
-    ).astype(jnp.int32)
-    offset = iota((items, depth), 1) - 3 * slot[:, :depth]
-    four = depth // GROUP
+    result_row = one_hot(place_down[:, :items] == iota(tall, 1))
     for h0 in range(0, heads, four):
-        outs, threes = [], []
+        turned = []
         for b in range(blocks):
             sl = slice(b * cols + h0 * GROUP, b * cols + (h0 + four) * GROUP)
-            outs.append((acc_ref[:depth, sl] * inverse[:, sl]).T)
-            threes.append(pieces[:, sl].T)
-        for h in range(four):
-            part = slice(h * GROUP, (h + 1) * GROUP)
-            out = jnp.concatenate([x[part] for x in outs], axis=0)
-            three = jnp.concatenate([x[part] for x in threes], axis=0)
-            packed = jnp.where(
-                offset == 0,
-                three[:, 0:1],
-                jnp.where(
-                    offset == 1, three[:, 1:2], jnp.where(offset == 2, three[:, 2:3], 0.0)
-                ),
-            )
-            both = jnp.concatenate([out.astype(BF16), packed.astype(BF16)], axis=0)
-            out_ref[:, (h0 + h) * depth : (h0 + h + 1) * depth] = jnp.dot(
-                spread, both, preferred_element_type=F32
-            ).astype(BF16)
+            turned.append((acc_ref[:depth, sl] * inverse[:, sl]).astype(BF16).T)
+        out = jnp.concatenate(
+            [
+                jnp.concatenate([x[h * GROUP : (h + 1) * GROUP] for x in turned], axis=0)
+                for h in range(four)
+            ],
+            axis=1,
+        )
+        out_ref[:, h0 * depth : (h0 + four) * depth] = jnp.dot(
+            result_row, out, preferred_element_type=F32
+        ).astype(BF16)
+    spread = (EXTRA, cols)
+    same_head = iota(spread, 0) // 8 == iota(spread, 1) // GROUP
+    lse_out = jnp.zeros((buffer_rows, EXTRA), F32)
+    for b in range(blocks):
+        part = pieces[:, b * cols : (b + 1) * cols]
+        by_head = jnp.where(same_head, jnp.concatenate([part] * heads, axis=0), 0.0).astype(BF16)
+        item = b * GROUP + iota((buffer_rows, cols), 1) % GROUP
+        to_row = one_hot(jnp.concatenate([place_down] * (cols // EXTRA), axis=1) == item)
+        lse_out += lax.dot_general(to_row, by_head, NT, preferred_element_type=F32)
+    out_ref[:, width:] = lse_out.astype(BF16)
 
 
 def merge_kernel(back_ref, dest_ref, suffix_ref, lse_ref, out_ref):
     copies, requests, width = out_ref.shape
-    depth = HDIM
-    dest = dest_ref[:, :1]
+    part = width // 4
     column = iota((requests, back_ref.shape[0]), 1)
-    pick_out = one_hot(column == dest)
-    pick_lse = one_hot(column == dest // SLOTS * SLOTS + CAP)
-    offset = iota((requests, depth), 1) - 3 * (dest % SLOTS)
-    mine = (offset >= 0) & (offset < 3)
-    for h in range(width // depth):
-        sl = slice(h * depth, (h + 1) * depth)
-        prefix = jnp.dot(pick_out, back_ref[:, sl], preferred_element_type=F32)
-        pieces = jnp.dot(pick_lse, back_ref[:, sl], preferred_element_type=F32)
-        prefix_lse = jnp.sum(jnp.where(mine, pieces, 0.0), axis=1, keepdims=True)
+    pick = one_hot(column == dest_ref[:, :1])
+    pieces = jnp.dot(pick, back_ref[:, width:], preferred_element_type=F32).astype(BF16)
+    for n in range(4):
+        sl = slice(n * part, (n + 1) * part)
+        prefix = jnp.dot(pick, back_ref[:, sl], preferred_element_type=F32)
+        head = n * (part // HDIM) + iota((EXTRA, part), 1) // HDIM
+        prefix_lse = jnp.dot(
+            pieces, one_hot(iota((EXTRA, part), 0) // 8 == head), preferred_element_type=F32
+        )
         suffix_lse = lse_ref[:, sl]
         top = jnp.maximum(prefix_lse, suffix_lse)
         prefix_part = jnp.exp(prefix_lse - top)
@@ -370,7 +376,7 @@
 
     packed = call(
         pack_kernel,
-        [((buffer_rows, width), BF16)],
+        [((buffer_rows, width + EXTRA), BF16)],
         [HBM, HBM, HBM],
         [
             pltpu.SMEM(route.shape, jnp.int32),
@@ -393,15 +399,15 @@
     )(route, place, suffix_len, queries, suffix_keys, suffix_values)
     prefix = call(
         prefix_kernel,
-        [((buffer_rows, width), BF16)],
+        [((buffer_rows, width + EXTRA), BF16)],
         [VMEM, HBM, HBM],
         [
             pltpu.VMEM(prefix_keys.shape, BF16),
             pltpu.VMEM(prefix_values.shape, BF16),
-            pltpu.VMEM((rows, 2 * HDIM), BF16),
+            pltpu.VMEM((rows, HDIM), BF16),
             pltpu.VMEM((HDIM + 16, rows), F32),
             pltpu.VMEM((8, rows), F32),
-            pltpu.SemaphoreType.DMA((2, prefix_keys.shape[0] // KEYS)),
+            pltpu.SemaphoreType.DMA((2, len(CHUNKS))),
         ],
         pl.CostEstimate(flops=10**10, bytes_accessed=5 * 10**6, transcendentals=12 * 10**6),
         62,
@@ -428,7 +434,7 @@
     )(y, mine, got)
     arrived = [
         lax.ppermute(part, "tp", [(i, (i + 2 * k) % 8) for i in range(8)])
-        for k, part in zip((1, 2, 3), parts)
+        for k, part in ((2, parts[1]), (1, parts[0]), (3, parts[2]))
     ]
     return call(sum_kernel, [((block, columns), BF16)], [VMEM] * 4)(own, *arrived)
 

time: 125 us -> 129 us (1.032)
  Pallas kernels: 41.1 us -> 47.1 us
  starting transfers between devices: 25.1 us -> 23.6 us
    pallas_call x2, Pallas kernels: 30.5 us -> 36.8 us  [the longest x1 34.8 us: on_device(): call(prefix_kernel, [((buffer_rows, width + EXTRA), BF16)], [VMEM, HBM, H...]
    all_to_all x2, starting transfers between devices: 14.6 us -> 12.5 us  [exchange(): x = lax.all_to_all(x, 'pfx', split_axis=0, concat_axis=0, tiled=True)]
  transfers between devices with their start and end apart: 6 -> 6, of which waited for: 5 -> 5; matrix products, arithmetic and copies ran while one was open for 0% -> 0% of each run, Pallas kernels for 4% -> 3%
where the time goes in v3:
time: 129 us; the launch traced here: 128 us
  Pallas kernels  47.1 us (37%)
  waiting for transfers between devices  32.8 us (25%)
  starting transfers between devices  23.6 us (18%)
  blocking collectives  19.5 us (15%)
  local copies, waits for them, and re-layouts  5.38 us (4%)
    pallas_call x1, Pallas kernels, on_device(): call(prefix_kernel, [((buffer_rows, width + EXTRA), BF16)], [VMEM, HBM, H...  34.8 us
    all_to_all x2, waiting for transfers between devices, exchange(): x = lax.all_to_all(x, 'pfx', split_axis=0, concat_axis=0, tiled=True)  27.1 us
    all_to_all x1, blocking collectives, exchange(): x = lax.all_to_all(x, 'pfx', split_axis=0, concat_axis=0, tiled=True)  19.5 us
    all_to_all x2, starting transfers between devices, exchange(): x = lax.all_to_all(x, 'pfx', split_axis=0, concat_axis=0, tiled=True)  12.5 us
    ppermute x3, starting transfers between devices, on_device(): lax.ppermute(part, 'tp', [(i, (i + 2 * k) % 8) for i in range(8)])  5.67 us
    ppermute x1, starting transfers between devices, on_device(): got = lax.ppermute(other, 'tp', [(i, i ^ 1) for i in range(8)])  5.43 us
    unnamed x14, local copies, waits for them, and re-layouts  5.38 us
    pallas_call x1, Pallas kernels, on_device(): call(suffix_kernel, [((requests, width), F32), ((requests, width), F32),...  4.46 us
  transfers between devices with their start and end apart: 6, of which 5 were waited for; matrix products, arithmetic and copies ran while one was open for 0% of the time, Pallas kernels for 3%

profile of v3, /device:TPU:1, one launch (start us, length us, event | category | flops | bytes accessed | tf_op | source)
XLA Modules:
  0.0 128.4 jit_solution(3394231697263427495)
XLA Ops:
  0.0 2.0 %shard_map.91 = bf16[128,2176]{1,0:T(8,128)(2,1)} custom-call(s32[32]{0:T(128)} %route_ref.1, s32[16]{0:T(128)} %place_ref.1, bf16[32,2048]{1,0:T(8,128)(2,1)} %q_ref.1), custom_call_target="tpu_custom_call" | custom-call | tf_op jit(solution)/shard_map/pallas_call | solution.py:377
  2.0 19.5 %all_to_all.15 = bf16[16,8,2176]{2,1,0:T(8,128)(2,1)} all-to-all(bf16[16,8,2176]{2,1,0:T(8,128)(2,1)} %bitcast.9), channel_id=1, replica_groups=mesh['pfx'=16,'tp'=8] {'pfx'}, dimensions={0} | all-to-all | bytes 1114112 | tf_op jit(solution)/shard_map/all_to_all | solution.py:374
  21.5 0.0 copy-start
  21.5 0.0 copy-start.1
  21.5 0.0 copy-start.2
  21.5 0.0 copy-start.6
  21.5 34.8 %shard_map.92 = bf16[128,2176]{1,0:T(8,128)(2,1)} custom-call(bf16[128,2176]{1,0:T(8,128)(2,1)} %bitcast.11, bf16[8192,128]{1,0:T(8,128)(2,1)} %k_in.1, bf16[8192,128]{1,0:T(8,128)(2,1)} %v_in.1), custom_call_target="tpu_custom_call" | custom-call | flops 10000000000 | bytes 5000000 | tf_op jit(solution)/shard_map/pallas_call | solution.py:400
  56.3 7.6 %all-to-all-start.1 = ((bf16[16,8,2176]{2,1,0:T(8,128)(2,1)}), bf16[16,8,2176]{2,1,0:T(8,128)(2,1)S(1)}, u32[]{:S(2)}, u32[]{:S(2)}) async-start(bf16[16,8,2176]{2,1,0:T(8,128)(2,1)} %bitcast.10), calls=%async_computation.1 | async-start | bytes 1114112 | tf_op jit(solution)/shard_map/all_to_all | solution.py:374
  63.9 0.0 copy-done
  63.9 0.0 copy-done.1
  63.9 0.0 copy-done.2
  63.9 0.0 copy-done.6
  63.9 0.0 copy-start.4
  64.0 1.6 %copy-done.4 = bf16[32,256,128]{2,1,0:T(8,128)(2,1)S(1)} copy-done((bf16[32,256,128]{2,1,0:T(8,128)(2,1)S(1)}, bf16[32,256,128]{2,1,0:T(8,128)(2,1)}, u32[]{:S(2)}) %copy-start.4) | copy-done | bytes 2097176
  65.5 0.0 copy-start.5
  65.5 1.6 %copy-done.5 = bf16[32,256,128]{2,1,0:T(8,128)(2,1)S(1)} copy-done((bf16[32,256,128]{2,1,0:T(8,128)(2,1)S(1)}, bf16[32,256,128]{2,1,0:T(8,128)(2,1)}, u32[]{:S(2)}) %copy-start.5) | copy-done | bytes 2097176
  67.1 4.5 %shard_map.93 = (f32[32,2048]{1,0:T(8,128)S(1)}, f32[32,2048]{1,0:T(8,128)S(1)}, s32[32,128]{1,0:T(8,128)S(1)}) custom-call(s32[32]{0:T(128)S(1)} %copy-done.1, s32[16]{0:T(128)S(1)} %copy-done.2, s32[32]{0:T(128)S(1)} %copy-done.6, bf16[32,2048]{1,0:T(8,128)(2,1)S(1)} %copy-done, bf16[32,256,128]{2,1,0:T(8,128)(2,1)S(1)} %copy-done.4, ...), custom_call_target="tpu_custom_call" | custom-call | flops 2000000000 | bytes 5000000 | tf_op jit(solution)/shard_map/pallas_call | solution.py:392
  71.6 1.8 %all-to-all-done.1 = bf16[16,8,2176]{2,1,0:T(8,128)(2,1)S(1)} async-done(((bf16[16,8,2176]{2,1,0:T(8,128)(2,1)}), bf16[16,8,2176]{2,1,0:T(8,128)(2,1)S(1)}, u32[]{:S(2)}, u32[]{:S(2)}) %all-to-all-start.1) | async-done | bytes 557088 | tf_op jit(solution)/shard_map/all_to_all | solution.py:374
  73.4 1.9 %shard_map.94 = bf16[16,32,2048]{2,1,0:T(8,128)(2,1)} custom-call(bf16[128,2176]{1,0:T(8,128)(2,1)S(1)} %bitcast.7, s32[32,128]{1,0:T(8,128)S(1)} %get-tuple-element.14.dest_ref, f32[32,2048]{1,0:T(8,128)S(1)} %get-tuple-element.15.suffix_ref, f32[32,2048]{1,0:T(8,128)S(1)} %get-tuple-element.16.lse_ref), custom_call_target="tpu_custom_call" | custom-call | tf_op jit(solution)/shard_map/pallas_call | solution.py:416
  75.3 4.9 %all-to-all-start.2 = ((bf16[16,32,2048]{2,1,0:T(8,128)(2,1)}), bf16[16,32,2048]{2,1,0:T(8,128)(2,1)S(1)}, u32[]{:S(2)}, u32[]{:S(2)}) async-start(bf16[16,32,2048]{2,1,0:T(8,128)(2,1)} %shard_map.94), calls=%async_computation.2 | async-start | bytes 4194304 | tf_op jit(solution)/shard_map/all_to_all | solution.py:374
  80.2 25.3 %all-to-all-done.2 = bf16[16,32,2048]{2,1,0:T(8,128)(2,1)S(1)} async-done(((bf16[16,32,2048]{2,1,0:T(8,128)(2,1)}), bf16[16,32,2048]{2,1,0:T(8,128)(2,1)S(1)}, u32[]{:S(2)}, u32[]{:S(2)}) %all-to-all-start.2) | async-done | bytes 2097184 | tf_op jit(solution)/shard_map/all_to_all | solution.py:374
  105.5 0.0 copy-start.3
  105.5 2.2 %copy-done.3 = bf16[2048,1024]{1,0:T(8,128)(2,1)S(1)} copy-done((bf16[2048,1024]{1,0:T(8,128)(2,1)S(1)}, bf16[2048,1024]{1,0:T(8,128)(2,1)}, u32[]{:S(2)}) %copy-start.3) | copy-done | bytes 4194328
  107.7 3.1 %shard_map.95 = (f32[256,1024]{1,0:T(8,128)S(1)}, bf16[256,1024]{1,0:T(8,128)(2,1)}) custom-call(s32[1]{0:T(128)} %bitcast.1.core_ref, bf16[512,2048]{1,0:T(8,128)(2,1)S(1)} %bitcast.8, bf16[2048,1024]{1,0:T(8,128)(2,1)S(1)} %copy-done.3), custom_call_target="tpu_custom_call" | custom-call | flops 2000000000 | bytes 8000000 | tf_op jit(solution)/shard_map/pallas_call | solution.py:422
  110.8 5.4 %collective-permute-start = (bf16[256,1024]{1,0:T(8,128)(2,1)}, bf16[256,1024]{1,0:T(8,128)(2,1)S(1)}, u32[]{:S(2)}, u32[]{:S(2)}) collective-permute-start(bf16[256,1024]{1,0:T(8,128)(2,1)} %get-tuple-element.18), channel_id=1, source_target_pairs={{0,1},{1,0},{2,3},{3,2},{4,5},{5,4},{6,7},{7,6},{8,9},{9,8},{10,11... | collective-permute-start | bytes 1572872 | tf_op jit(solution)/shard_map/ppermute | solution.py:430
  116.3 1.7 %collective-permute-done.got_ref = bf16[256,1024]{1,0:T(8,128)(2,1)S(1)} collective-permute-done((bf16[256,1024]{1,0:T(8,128)(2,1)}, bf16[256,1024]{1,0:T(8,128)(2,1)S(1)}, u32[]{:S(2)}, u32[]{:S(2)}) %collective-permute-start) | collective-permute-done | bytes 524320 | tf_op jit(solution)/shard_map/ppermute | solution.py:430
  118.0 0.1 shard_map.96
  118.1 3.0 %collective-permute-start.1 = (bf16[64,1024]{1,0:T(8,128)(2,1)S(1)}, bf16[64,1024]{1,0:T(8,128)(2,1)S(1)}, u32[]{:S(2)}, u32[]{:S(2)}) collective-permute-start(bf16[64,1024]{1,0:T(8,128)(2,1)S(1)} %get-tuple-element.20), channel_id=1, source_target_pairs={{0,4},{1,5},{2,6},{3,7},{4,0},{5,1},{6,2},{7,3},{8,12},{9,13},{10,... | collective-permute-start | bytes 393224 | tf_op jit(solution)/shard_map/ppermute | solution.py:436
  121.1 0.4 collective-permute-start.2
  121.5 2.3 %collective-permute-start.3 = (bf16[64,1024]{1,0:T(8,128)(2,1)S(1)}, bf16[64,1024]{1,0:T(8,128)(2,1)S(1)}, u32[]{:S(2)}, u32[]{:S(2)}) collective-permute-start(bf16[64,1024]{1,0:T(8,128)(2,1)S(1)} %get-tuple-element.22), channel_id=1, source_target_pairs={{0,6},{1,7},{2,0},{3,1},{4,2},{5,3},{6,4},{7,5},{8,14},{9,15},{10,... | collective-permute-start | bytes 393224 | tf_op jit(solution)/shard_map/ppermute | solution.py:436
  123.8 0.6 collective-permute-done.1.one_ref
  124.4 3.3 %collective-permute-done.2.two_ref = bf16[64,1024]{1,0:T(8,128)(2,1)S(1)} collective-permute-done((bf16[64,1024]{1,0:T(8,128)(2,1)S(1)}, bf16[64,1024]{1,0:T(8,128)(2,1)S(1)}, u32[]{:S(2)}, u32[]{:S(2)}) %collective-permute-start.2) | collective-permute-done | bytes 131104 | tf_op jit(solution)/shard_map/ppermute | solution.py:436
  127.7 0.0 collective-permute-done.3.three_ref
  127.7 0.7 shard_map.97
Async XLA Ops:
  21.5 42.4 %copy-start = (bf16[32,2048]{1,0:T(8,128)(2,1)S(1)}, bf16[32,2048]{1,0:T(8,128)(2,1)}, u32[]{:S(2)}) copy-start(bf16[32,2048]{1,0:T(8,128)(2,1)} %q_ref.1) | copy-start | bytes 393220
  21.5 42.4 %copy-start.1 = (s32[32]{0:T(128)S(1)}, s32[32]{0:T(128)}, u32[]{:S(2)}) copy-start(s32[32]{0:T(128)} %route_ref.1) | copy-start | bytes 388
  21.5 42.4 %copy-start.2 = (s32[16]{0:T(128)S(1)}, s32[16]{0:T(128)}, u32[]{:S(2)}) copy-start(s32[16]{0:T(128)} %place_ref.1) | copy-start | bytes 196
  21.5 42.5 %copy-start.6 = (s32[32]{0:T(128)S(1)}, s32[32]{0:T(128)}, u32[]{:S(2)}) copy-start(s32[32]{0:T(128)} %len_ref.1) | copy-start | bytes 388
  56.3 17.1 %all-to-all-start.1 = ((bf16[16,8,2176]{2,1,0:T(8,128)(2,1)}), bf16[16,8,2176]{2,1,0:T(8,128)(2,1)S(1)}, u32[]{:S(2)}, u32[]{:S(2)}) async-start(bf16[16,8,2176]{2,1,0:T(8,128)(2,1)} %bitcast.10), calls=%async_computation.1 | async-start | bytes 1114112 | tf_op jit(solution)/shard_map/all_to_all | solution.py:374
  63.9 1.6 %copy-start.4 = (bf16[32,256,128]{2,1,0:T(8,128)(2,1)S(1)}, bf16[32,256,128]{2,1,0:T(8,128)(2,1)}, u32[]{:S(2)}) copy-start(bf16[32,256,128]{2,1,0:T(8,128)(2,1)} %k_ref.1) | copy-start | bytes 6291460
  65.5 1.6 %copy-start.5 = (bf16[32,256,128]{2,1,0:T(8,128)(2,1)S(1)}, bf16[32,256,128]{2,1,0:T(8,128)(2,1)}, u32[]{:S(2)}) copy-start(bf16[32,256,128]{2,1,0:T(8,128)(2,1)} %v_ref.1) | copy-start | bytes 6291460
  75.3 30.2 %all-to-all-start.2 = ((bf16[16,32,2048]{2,1,0:T(8,128)(2,1)}), bf16[16,32,2048]{2,1,0:T(8,128)(2,1)S(1)}, u32[]{:S(2)}, u32[]{:S(2)}) async-start(bf16[16,32,2048]{2,1,0:T(8,128)(2,1)} %shard_map.94), calls=%async_computation.2 | async-start | bytes 4194304 | tf_op jit(solution)/shard_map/all_to_all | solution.py:374
  105.5 2.2 %copy-start.3 = (bf16[2048,1024]{1,0:T(8,128)(2,1)S(1)}, bf16[2048,1024]{1,0:T(8,128)(2,1)}, u32[]{:S(2)}) copy-start(bf16[2048,1024]{1,0:T(8,128)(2,1)} %w_ref.1) | copy-start | bytes 12582916
  110.8 7.2 %collective-permute-start = (bf16[256,1024]{1,0:T(8,128)(2,1)}, bf16[256,1024]{1,0:T(8,128)(2,1)S(1)}, u32[]{:S(2)}, u32[]{:S(2)}) collective-permute-start(bf16[256,1024]{1,0:T(8,128)(2,1)} %get-tuple-element.18), channel_id=1, source_target_pairs={{0,1},{1,0},{2,3},{3,2},{4,5},{5,4},{6,7},{7,6},{8,9},{9,8},{10,11... | collective-permute-start | bytes 1572872 | tf_op jit(solution)/shard_map/ppermute | solution.py:430
  118.1 6.3 %collective-permute-start.1 = (bf16[64,1024]{1,0:T(8,128)(2,1)S(1)}, bf16[64,1024]{1,0:T(8,128)(2,1)S(1)}, u32[]{:S(2)}, u32[]{:S(2)}) collective-permute-start(bf16[64,1024]{1,0:T(8,128)(2,1)S(1)} %get-tuple-element.20), channel_id=1, source_target_pairs={{0,4},{1,5},{2,6},{3,7},{4,0},{5,1},{6,2},{7,3},{8,12},{9,13},{10,... | collective-permute-start | bytes 393224 | tf_op jit(solution)/shard_map/ppermute | solution.py:436
  121.1 6.6 %collective-permute-start.2 = (bf16[64,1024]{1,0:T(8,128)(2,1)S(1)}, bf16[64,1024]{1,0:T(8,128)(2,1)S(1)}, u32[]{:S(2)}, u32[]{:S(2)}) collective-permute-start(bf16[64,1024]{1,0:T(8,128)(2,1)S(1)} %get-tuple-element.21), channel_id=1, source_target_pairs={{0,2},{1,3},{2,4},{3,5},{4,6},{5,7},{6,0},{7,1},{8,10},{9,11},{10,... | collective-permute-start | bytes 393224 | tf_op jit(solution)/shard_map/ppermute | solution.py:436
  121.5 6.2 %collective-permute-start.3 = (bf16[64,1024]{1,0:T(8,128)(2,1)S(1)}, bf16[64,1024]{1,0:T(8,128)(2,1)S(1)}, u32[]{:S(2)}, u32[]{:S(2)}) collective-permute-start(bf16[64,1024]{1,0:T(8,128)(2,1)S(1)} %get-tuple-element.22), channel_id=1, source_target_pairs={{0,6},{1,7},{2,0},{3,1},{4,2},{5,3},{6,4},{7,5},{8,14},{9,15},{10,... | collective-permute-start | bytes 393224 | tf_op jit(solution)/shard_map/ppermute | solution.py:436

commit v4 on v3

--- a/solution.py
+++ b/solution.py
@@ -54,12 +54,41 @@
         dest[0] = jnp.where(lane == r, row, dest[0])
 
     dest_rows(route_ref, place_ref, count_ref, add)
-    pick = one_hot(iota((out_ref.shape[0], rows), 0) == dest[0][:1, :rows])
+    buffer_rows, wide = out_ref.shape[0], SLOTS * rows
+    place = jnp.concatenate([dest[0][:1, :rows]] * SLOTS, axis=1)
+    row, lane = iota((buffer_rows, wide), 0), iota((buffer_rows, wide), 1)
+    owner = row // SLOTS * SLOTS
+    fits = row % SLOTS == lane // rows
+    count = jnp.dot(
+        one_hot(dest[0][:1, :rows] // SLOTS * SLOTS == owner[:, :rows]),
+        jnp.ones((rows, EXTRA), BF16),
+        preferred_element_type=F32,
+    )
+    out_ref[:, CAP * 2 * HDIM :] = count.astype(BF16)
     loads[2].wait()
-    width = q_ref.shape[1]
-    live = jnp.dot(pick, jnp.ones((rows, EXTRA), BF16), preferred_element_type=F32)
-    out_ref[:, :width] = jnp.dot(pick, q_ref[...], preferred_element_type=F32).astype(BF16)
-    out_ref[:, width:] = live.astype(BF16)
+    stacked = by_half(q_ref)
+    picks = [one_hot(fits & (place == owner + k)) for k in range(CAP)]
+    out = jnp.dot(jnp.concatenate(picks, axis=0), stacked, preferred_element_type=F32)
+    for k in range(CAP):
+        out_ref[:, k * 2 * HDIM : (k + 1) * 2 * HDIM] = out[
+            k * buffer_rows : (k + 1) * buffer_rows
+        ].astype(BF16)
+
+
+def by_half(ref):
+    parts = []
+    for sub in range(SLOTS):
+        low, high = sub * HDIM, (SLOTS + sub) * HDIM
+        parts.append(
+            jnp.concatenate([ref[:, low : low + HDIM], ref[:, high : high + HDIM]], axis=1)
+        )
+    return jnp.concatenate(parts, axis=0)
+
+
+def by_slot(ref):
+    return jnp.concatenate(
+        [ref[:, k * 2 * HDIM : (k + 1) * 2 * HDIM] for k in range(CAP)], axis=0
+    )
 
 
 def suffix_kernel(
@@ -124,8 +153,8 @@
 def prefix_kernel(recv_ref, k_in, v_in, out_ref, k_ref, v_ref, q_ref, acc_ref, top_ref, sems):
     depth = k_ref.shape[1]
     buffer_rows = recv_ref.shape[0]
-    width = recv_ref.shape[1] - EXTRA
-    heads = width // depth
+    width = CAP * 2 * depth
+    heads = 2 * SLOTS
     cols = heads * GROUP
     items = buffer_rows // SLOTS * CAP
     blocks = items // GROUP
@@ -143,34 +172,39 @@
 
     square = (buffer_rows, buffer_rows)
     row, other = iota(square, 0), iota(square, 1)
-    bits = recv_ref[:, width:]
-    place_down = jnp.dot(one_hot(other < row), bits, preferred_element_type=F32)
-    place_across = lax.dot_general(
-        bits, one_hot(row < other), (((0,), (0,)), ((), ())), preferred_element_type=F32
-    )
-    live_across = lax.dot_general(
-        bits, one_hot(row == other), (((0,), (0,)), ((), ())), preferred_element_type=F32
-    )
-    live = bits.astype(F32) > 0.5
-    place_down = jnp.where(live, place_down.astype(jnp.int32), -1)
-    used = (jnp.max(place_down) + 1).astype(jnp.int32)
-    active = (used + GROUP - 1) // GROUP
-    short = (items, buffer_rows)
-    pick = one_hot(
-        (place_across[:items].astype(jnp.int32) == iota(short, 0)) & (live_across[:items] > 0.5)
+    number = recv_ref[:, width:]
+    first = (other % SLOTS == 0) & (other // SLOTS < row // SLOTS)
+    first_turned = (row % SLOTS == 0) & (row // SLOTS < other // SLOTS)
+    turn = (((0,), (0,)), ((), ()))
+    base_down = jnp.dot(one_hot(first), number, preferred_element_type=F32)
+    base_across = lax.dot_general(number, one_hot(first_turned), turn, preferred_element_type=F32)
+    number_across = lax.dot_general(number, one_hot(row == other), turn, preferred_element_type=F32)
+    number_down = number.astype(F32)
+    used = jnp.max(base_down + number_down).astype(jnp.int32)
+    active = jnp.minimum((used + GROUP - 1) // GROUP, blocks)
+    place_down = [
+        jnp.where(number_down > k, base_down + k, -1.0).astype(jnp.int32) for k in range(CAP)
+    ]
+    place_across = jnp.concatenate(
+        [
+            jnp.where(number_across[:1] > k, base_across[:1] + k, -1.0).astype(jnp.int32)
+            for k in range(CAP)
+        ],
+        axis=1,
     )
 
     scale = depth**-0.5 * LOG2E
-    four = 4
-    for h0 in range(0, heads, four):
-        q = jnp.dot(
-            pick, recv_ref[:, h0 * depth : (h0 + four) * depth], preferred_element_type=F32
-        ).astype(BF16)
+    received = by_slot(recv_ref)
+    shape = (items, CAP * buffer_rows)
+    found = place_across == iota(shape, 0)
+    picks = [one_hot(found & (iota(shape, 1) % SLOTS == sub)) for sub in range(SLOTS)]
+    q = jnp.dot(jnp.concatenate(picks, axis=0), received, preferred_element_type=F32).astype(BF16)
+    for sub in range(SLOTS):
         for b in range(blocks):
-            of = slice(b * GROUP, (b + 1) * GROUP)
-            for h in range(four):
-                start = b * cols + (h0 + h) * GROUP
-                q_ref[start : start + GROUP, :] = q[of, h * depth : (h + 1) * depth]
+            of = slice(sub * items + b * GROUP, sub * items + (b + 1) * GROUP)
+            for half in range(2):
+                start = b * cols + (half * SLOTS + sub) * GROUP
+                q_ref[start : start + GROUP, :] = q[of, half * depth : (half + 1) * depth]
 
     def scores_of(span, c):
         q = q_ref[c * cols : (c + 1) * cols, :]
@@ -246,58 +280,98 @@
     pieces = jnp.where(
         wide == 0, high, jnp.where(wide == 1, middle, jnp.where(wide == 2, low, 0.0))
     ).astype(BF16)
-    tall = (buffer_rows, items)
-    result_row = one_hot(place_down[:, :items] == iota(tall, 1))
+    four = depth // GROUP
+    outs = []
     for h0 in range(0, heads, four):
         turned = []
         for b in range(blocks):
             sl = slice(b * cols + h0 * GROUP, b * cols + (h0 + four) * GROUP)
             turned.append((acc_ref[:depth, sl] * inverse[:, sl]).astype(BF16).T)
-        out = jnp.concatenate(
-            [
+        for h in range(four):
+            outs.append(
                 jnp.concatenate([x[h * GROUP : (h + 1) * GROUP] for x in turned], axis=0)
-                for h in range(four)
-            ],
-            axis=1,
-        )
-        out_ref[:, h0 * depth : (h0 + four) * depth] = jnp.dot(
-            result_row, out, preferred_element_type=F32
-        ).astype(BF16)
+            )
+    results = jnp.concatenate(
+        [
+            jnp.concatenate([outs[sub], outs[SLOTS + sub]], axis=1)
+            for sub in range(SLOTS)
+        ],
+        axis=0,
+    )
+    shape = (buffer_rows, SLOTS * items)
+    same = iota(shape, 0) % SLOTS == iota(shape, 1) // items
+    item = iota(shape, 1) % items
+    picks = [
+        one_hot(same & (jnp.concatenate([place] * (shape[1] // EXTRA), axis=1) == item))
+        for place in place_down
+    ]
+    out = jnp.dot(jnp.concatenate(picks, axis=0), results, preferred_element_type=F32)
+    for k in range(CAP):
+        out_ref[:, k * 2 * depth : (k + 1) * 2 * depth] = out[
+            k * buffer_rows : (k + 1) * buffer_rows
+        ].astype(BF16)
     spread = (EXTRA, cols)
     same_head = iota(spread, 0) // 8 == iota(spread, 1) // GROUP
-    lse_out = jnp.zeros((buffer_rows, EXTRA), F32)
+    to_item = one_hot(iota((GROUP, cols), 1) % GROUP == iota((GROUP, cols), 0))
+    listed = []
     for b in range(blocks):
         part = pieces[:, b * cols : (b + 1) * cols]
         by_head = jnp.where(same_head, jnp.concatenate([part] * heads, axis=0), 0.0).astype(BF16)
-        item = b * GROUP + iota((buffer_rows, cols), 1) % GROUP
-        to_row = one_hot(jnp.concatenate([place_down] * (cols // EXTRA), axis=1) == item)
-        lse_out += lax.dot_general(to_row, by_head, NT, preferred_element_type=F32)
-    out_ref[:, width:] = lse_out.astype(BF16)
+        listed.append(lax.dot_general(to_item, by_head, NT, preferred_element_type=F32))
+    listed = jnp.concatenate(listed, axis=0).astype(BF16)
+    own = row % SLOTS == other // 8 % SLOTS
+    to_row = [one_hot(place[:, :items] == iota((buffer_rows, items), 1)) for place in place_down]
+    rows_of = jnp.dot(jnp.concatenate(to_row, axis=0), listed, preferred_element_type=F32)
+    ones, lanes = [], []
+    for k in range(CAP):
+        one = rows_of[k * buffer_rows : (k + 1) * buffer_rows]
+        ones.append(jnp.where(own, one, 0.0).astype(BF16))
+        to_lane = (other // 16 == k) & (other // 8 % 2 == row // 64) & (other % 8 == row % 8)
+        lanes.append(one_hot(to_lane))
+    tail = jnp.dot(
+        jnp.concatenate(ones, axis=1), jnp.concatenate(lanes, axis=0), preferred_element_type=F32
+    )
+    out_ref[:, width:] = tail.astype(BF16)
 
 
 def merge_kernel(back_ref, dest_ref, suffix_ref, lse_ref, out_ref):
-    copies, requests, width = out_ref.shape
-    part = width // 4
-    column = iota((requests, back_ref.shape[0]), 1)
-    pick = one_hot(column == dest_ref[:, :1])
-    pieces = jnp.dot(pick, back_ref[:, width:], preferred_element_type=F32).astype(BF16)
-    for n in range(4):
-        sl = slice(n * part, (n + 1) * part)
-        prefix = jnp.dot(pick, back_ref[:, sl], preferred_element_type=F32)
-        head = n * (part // HDIM) + iota((EXTRA, part), 1) // HDIM
-        prefix_lse = jnp.dot(
-            pieces, one_hot(iota((EXTRA, part), 0) // 8 == head), preferred_element_type=F32
-        )
-        suffix_lse = lse_ref[:, sl]
-        top = jnp.maximum(prefix_lse, suffix_lse)
-        prefix_part = jnp.exp(prefix_lse - top)
-        suffix_part = jnp.exp(suffix_lse - top)
-        merged = (prefix_part * prefix + suffix_part * suffix_ref[:, sl]) / (
-            prefix_part + suffix_part
-        )
-        merged = merged.astype(BF16)
-        for copy in range(copies):
-            out_ref[copy, :, sl] = merged
+    copies, requests, _ = out_ref.shape
+    buffer_rows = back_ref.shape[0]
+    dest = dest_ref[:, :1]
+    returned = by_slot(back_ref)
+    shape = (requests, CAP * buffer_rows)
+    lane = iota(shape, 1)
+    mine = lane % buffer_rows // SLOTS * SLOTS + lane // buffer_rows == dest
+    short = (requests, buffer_rows)
+    group = iota(short, 1) // SLOTS == dest // SLOTS
+    slot = iota(short, 1) // 16 == dest % SLOTS
+    wide = (EXTRA, 2 * HDIM)
+    to_half = one_hot((iota(wide, 0) // 8 % 2 == iota(wide, 1) // HDIM) & (iota(wide, 0) % 8 < 3))
+    picks = [one_hot(mine & (lane % SLOTS == sub)) for sub in range(SLOTS)]
+    prefixes = jnp.dot(jnp.concatenate(picks, axis=0), returned, preferred_element_type=F32)
+    picks = [one_hot(group & (iota(short, 1) % SLOTS == sub)) for sub in range(SLOTS)]
+    pieces = jnp.dot(
+        jnp.concatenate(picks, axis=0), back_ref[:, CAP * 2 * HDIM :], preferred_element_type=F32
+    )
+    pieces = jnp.where(jnp.concatenate([slot] * SLOTS, axis=0), pieces, 0.0).astype(BF16)
+    lses = jnp.dot(pieces, to_half, preferred_element_type=F32)
+    for sub in range(SLOTS):
+        prefix = prefixes[sub * requests : (sub + 1) * requests]
+        prefix_lse = lses[sub * requests : (sub + 1) * requests]
+        for half in range(2):
+            part = slice(half * HDIM, (half + 1) * HDIM)
+            start = (half * SLOTS + sub) * HDIM
+            sl = slice(start, start + HDIM)
+            suffix_lse = lse_ref[:, sl]
+            top = jnp.maximum(prefix_lse[:, part], suffix_lse)
+            prefix_part = jnp.exp(prefix_lse[:, part] - top)
+            suffix_part = jnp.exp(suffix_lse - top)
+            merged = (prefix_part * prefix[:, part] + suffix_part * suffix_ref[:, sl]) / (
+                prefix_part + suffix_part
+            )
+            merged = merged.astype(BF16)
+            for copy in range(copies):
+                out_ref[copy, :, sl] = merged
 
 
 TILE = 256
@@ -376,7 +450,7 @@
 
     packed = call(
         pack_kernel,
-        [((buffer_rows, width + EXTRA), BF16)],
+        [((buffer_rows, CAP * 2 * HDIM + EXTRA), BF16)],
         [HBM, HBM, HBM],
         [
             pltpu.SMEM(route.shape, jnp.int32),
@@ -399,7 +473,7 @@
     )(route, place, suffix_len, queries, suffix_keys, suffix_values)
     prefix = call(
         prefix_kernel,
-        [((buffer_rows, width + EXTRA), BF16)],
+        [((buffer_rows, CAP * 2 * HDIM + EXTRA), BF16)],
         [VMEM, HBM, HBM],
         [
             pltpu.VMEM(prefix_keys.shape, BF16),

time: 129 us -> 127 us (0.984)
  blocking collectives: 19.5 us -> 17 us
  starting transfers between devices: 23.6 us -> 25.7 us
  waiting for transfers between devices: 32.8 us -> 31.3 us
    all_to_all x1, blocking collectives: 19.5 us -> 17 us  [exchange(): x = lax.all_to_all(x, 'pfx', split_axis=0, concat_axis=0, tiled=True)]
    all_to_all x2, starting transfers between devices: 12.5 us -> 14.3 us  [exchange(): x = lax.all_to_all(x, 'pfx', split_axis=0, concat_axis=0, tiled=True)]
    all_to_all x2, waiting for transfers between devices: 27.1 us -> 25.7 us  [exchange(): x = lax.all_to_all(x, 'pfx', split_axis=0, concat_axis=0, tiled=True)]
  transfers between devices with their start and end apart: 6 -> 6, of which waited for: 5 -> 5; matrix products, arithmetic and copies ran while one was open for 0% -> 0% of each run, Pallas kernels for 3% -> 4%
where the time goes in v4:
time: 127 us
  Pallas kernels  47.8 us (38%)
  waiting for transfers between devices  31.3 us (25%)
  starting transfers between devices  25.7 us (20%)
  blocking collectives  17 us (13%)
  local copies, waits for them, and re-layouts  5.38 us (4%)
    pallas_call x1, Pallas kernels, on_device(): call(prefix_kernel, [((buffer_rows, CAP * 2 * HDIM + EXTRA), BF16)], [VME...  35.1 us
    all_to_all x2, waiting for transfers between devices, exchange(): x = lax.all_to_all(x, 'pfx', split_axis=0, concat_axis=0, tiled=True)  25.7 us
    all_to_all x1, blocking collectives, exchange(): x = lax.all_to_all(x, 'pfx', split_axis=0, concat_axis=0, tiled=True)  17 us
    all_to_all x2, starting transfers between devices, exchange(): x = lax.all_to_all(x, 'pfx', split_axis=0, concat_axis=0, tiled=True)  14.3 us
    ppermute x1, starting transfers between devices, on_device(): got = lax.ppermute(other, 'tp', [(i, i ^ 1) for i in range(8)])  5.71 us
    ppermute x3, starting transfers between devices, on_device(): lax.ppermute(part, 'tp', [(i, (i + 2 * k) % 8) for i in range(8)])  5.68 us
    unnamed x14, local copies, waits for them, and re-layouts  5.38 us
    pallas_call x1, Pallas kernels, on_device(): call(suffix_kernel, [((requests, width), F32), ((requests, width), F32),...  4.46 us
  transfers between devices with their start and end apart: 6, of which 5 were waited for; matrix products, arithmetic and copies ran while one was open for 0% of the time, Pallas kernels for 4%

profile of v4, /device:TPU:1, one launch (start us, length us, event | category | flops | bytes accessed | tf_op | source)
XLA Modules:
  0.0 127.3 jit_solution(646251336370285970)
XLA Ops:
  0.0 2.0 %shard_map.91 = bf16[128,1664]{1,0:T(8,128)(2,1)} custom-call(s32[32]{0:T(128)} %route_ref.1, s32[16]{0:T(128)} %place_ref.1, bf16[32,2048]{1,0:T(8,128)(2,1)} %q_ref.1), custom_call_target="tpu_custom_call" | custom-call | tf_op jit(solution)/shard_map/pallas_call | solution.py:451
  2.0 17.0 %all_to_all.15 = bf16[16,8,1664]{2,1,0:T(8,128)(2,1)} all-to-all(bf16[16,8,1664]{2,1,0:T(8,128)(2,1)} %bitcast.9), channel_id=1, replica_groups=mesh['pfx'=16,'tp'=8] {'pfx'}, dimensions={0} | all-to-all | bytes 851968 | tf_op jit(solution)/shard_map/all_to_all | solution.py:448
  19.0 0.0 copy-start
  19.0 0.0 copy-start.1
  19.0 0.0 copy-start.2
  19.0 0.0 copy-start.6
  19.0 35.1 %shard_map.92 = bf16[128,1664]{1,0:T(8,128)(2,1)} custom-call(bf16[128,1664]{1,0:T(8,128)(2,1)} %bitcast.11, bf16[8192,128]{1,0:T(8,128)(2,1)} %k_in.1, bf16[8192,128]{1,0:T(8,128)(2,1)} %v_in.1), custom_call_target="tpu_custom_call" | custom-call | flops 10000000000 | bytes 5000000 | tf_op jit(solution)/shard_map/pallas_call | solution.py:474
  54.1 8.1 %all-to-all-start.1 = ((bf16[16,8,1664]{2,1,0:T(8,128)(2,1)}), bf16[16,8,1664]{2,1,0:T(8,128)(2,1)S(1)}, u32[]{:S(2)}, u32[]{:S(2)}) async-start(bf16[16,8,1664]{2,1,0:T(8,128)(2,1)} %bitcast.10), calls=%async_computation.1 | async-start | bytes 851968 | tf_op jit(solution)/shard_map/all_to_all | solution.py:448
  62.2 0.0 copy-done
  62.3 0.0 copy-done.1
  62.3 0.0 copy-done.2
  62.3 0.0 copy-done.6
  62.3 0.0 copy-start.4
  62.3 1.6 %copy-done.4 = bf16[32,256,128]{2,1,0:T(8,128)(2,1)S(1)} copy-done((bf16[32,256,128]{2,1,0:T(8,128)(2,1)S(1)}, bf16[32,256,128]{2,1,0:T(8,128)(2,1)}, u32[]{:S(2)}) %copy-start.4) | copy-done | bytes 2097176
  63.9 0.0 copy-start.5
  63.9 1.6 %copy-done.5 = bf16[32,256,128]{2,1,0:T(8,128)(2,1)S(1)} copy-done((bf16[32,256,128]{2,1,0:T(8,128)(2,1)S(1)}, bf16[32,256,128]{2,1,0:T(8,128)(2,1)}, u32[]{:S(2)}) %copy-start.5) | copy-done | bytes 2097176
  65.5 4.5 %shard_map.93 = (f32[32,2048]{1,0:T(8,128)S(1)}, f32[32,2048]{1,0:T(8,128)S(1)}, s32[32,128]{1,0:T(8,128)S(1)}) custom-call(s32[32]{0:T(128)S(1)} %copy-done.1, s32[16]{0:T(128)S(1)} %copy-done.2, s32[32]{0:T(128)S(1)} %copy-done.6, bf16[32,2048]{1,0:T(8,128)(2,1)S(1)} %copy-done, bf16[32,256,128]{2,1,0:T(8,128)(2,1)S(1)} %copy-done.4, ...), custom_call_target="tpu_custom_call" | custom-call | flops 2000000000 | bytes 5000000 | tf_op jit(solution)/shard_map/pallas_call | solution.py:466
  69.9 0.5 all-to-all-done.1
  70.4 2.3 %shard_map.94 = bf16[16,32,2048]{2,1,0:T(8,128)(2,1)} custom-call(bf16[128,1664]{1,0:T(8,128)(2,1)S(1)} %bitcast.8, s32[32,128]{1,0:T(8,128)S(1)} %get-tuple-element.14.dest_ref, f32[32,2048]{1,0:T(8,128)S(1)} %get-tuple-element.15.suffix_ref, f32[32,2048]{1,0:T(8,128)S(1)} %get-tuple-element.16.lse_ref), custom_call_target="tpu_custom_call" | custom-call | tf_op jit(solution)/shard_map/pallas_call | solution.py:490
  72.7 6.2 %all-to-all-start.2 = ((bf16[16,32,2048]{2,1,0:T(8,128)(2,1)}), bf16[16,32,2048]{2,1,0:T(8,128)(2,1)S(1)}, u32[]{:S(2)}, u32[]{:S(2)}) async-start(bf16[16,32,2048]{2,1,0:T(8,128)(2,1)} %shard_map.94), calls=%async_computation.2 | async-start | bytes 4194304 | tf_op jit(solution)/shard_map/all_to_all | solution.py:448
  78.9 25.2 %all-to-all-done.2 = bf16[16,32,2048]{2,1,0:T(8,128)(2,1)S(1)} async-done(((bf16[16,32,2048]{2,1,0:T(8,128)(2,1)}), bf16[16,32,2048]{2,1,0:T(8,128)(2,1)S(1)}, u32[]{:S(2)}, u32[]{:S(2)}) %all-to-all-start.2) | async-done | bytes 2097184 | tf_op jit(solution)/shard_map/all_to_all | solution.py:448
  104.1 0.0 copy-start.3
  104.1 2.2 %copy-done.3 = bf16[2048,1024]{1,0:T(8,128)(2,1)S(1)} copy-done((bf16[2048,1024]{1,0:T(8,128)(2,1)S(1)}, bf16[2048,1024]{1,0:T(8,128)(2,1)}, u32[]{:S(2)}) %copy-start.3) | copy-done | bytes 4194328
  106.3 3.1 %shard_map.95 = (f32[256,1024]{1,0:T(8,128)S(1)}, bf16[256,1024]{1,0:T(8,128)(2,1)}) custom-call(s32[1]{0:T(128)} %bitcast.1.core_ref, bf16[512,2048]{1,0:T(8,128)(2,1)S(1)} %bitcast.7, bf16[2048,1024]{1,0:T(8,128)(2,1)S(1)} %copy-done.3), custom_call_target="tpu_custom_call" | custom-call | flops 2000000000 | bytes 8000000 | tf_op jit(solution)/shard_map/pallas_call | solution.py:496
  109.4 5.7 %collective-permute-start = (bf16[256,1024]{1,0:T(8,128)(2,1)}, bf16[256,1024]{1,0:T(8,128)(2,1)S(1)}, u32[]{:S(2)}, u32[]{:S(2)}) collective-permute-start(bf16[256,1024]{1,0:T(8,128)(2,1)} %get-tuple-element.18), channel_id=1, source_target_pairs={{0,1},{1,0},{2,3},{3,2},{4,5},{5,4},{6,7},{7,6},{8,9},{9,8},{10,11... | collective-permute-start | bytes 1572872 | tf_op jit(solution)/shard_map/ppermute | solution.py:504
  115.1 1.7 %collective-permute-done.got_ref = bf16[256,1024]{1,0:T(8,128)(2,1)S(1)} collective-permute-done((bf16[256,1024]{1,0:T(8,128)(2,1)}, bf16[256,1024]{1,0:T(8,128)(2,1)S(1)}, u32[]{:S(2)}, u32[]{:S(2)}) %collective-permute-start) | collective-permute-done | bytes 524320 | tf_op jit(solution)/shard_map/ppermute | solution.py:504
  116.9 0.1 shard_map.96
  117.0 3.0 %collective-permute-start.1 = (bf16[64,1024]{1,0:T(8,128)(2,1)S(1)}, bf16[64,1024]{1,0:T(8,128)(2,1)S(1)}, u32[]{:S(2)}, u32[]{:S(2)}) collective-permute-start(bf16[64,1024]{1,0:T(8,128)(2,1)S(1)} %get-tuple-element.20), channel_id=1, source_target_pairs={{0,4},{1,5},{2,6},{3,7},{4,0},{5,1},{6,2},{7,3},{8,12},{9,13},{10,... | collective-permute-start | bytes 393224 | tf_op jit(solution)/shard_map/ppermute | solution.py:510
  120.0 0.4 collective-permute-start.2
  120.4 2.3 %collective-permute-start.3 = (bf16[64,1024]{1,0:T(8,128)(2,1)S(1)}, bf16[64,1024]{1,0:T(8,128)(2,1)S(1)}, u32[]{:S(2)}, u32[]{:S(2)}) collective-permute-start(bf16[64,1024]{1,0:T(8,128)(2,1)S(1)} %get-tuple-element.22), channel_id=1, source_target_pairs={{0,6},{1,7},{2,0},{3,1},{4,2},{5,3},{6,4},{7,5},{8,14},{9,15},{10,... | collective-permute-start | bytes 393224 | tf_op jit(solution)/shard_map/ppermute | solution.py:510
  122.6 0.6 collective-permute-done.1.one_ref
  123.3 3.3 %collective-permute-done.2.two_ref = bf16[64,1024]{1,0:T(8,128)(2,1)S(1)} collective-permute-done((bf16[64,1024]{1,0:T(8,128)(2,1)S(1)}, bf16[64,1024]{1,0:T(8,128)(2,1)S(1)}, u32[]{:S(2)}, u32[]{:S(2)}) %collective-permute-start.2) | collective-permute-done | bytes 131104 | tf_op jit(solution)/shard_map/ppermute | solution.py:510
  126.6 0.0 collective-permute-done.3.three_ref
  126.6 0.7 shard_map.97
Async XLA Ops:
  19.0 43.3 %copy-start = (bf16[32,2048]{1,0:T(8,128)(2,1)S(1)}, bf16[32,2048]{1,0:T(8,128)(2,1)}, u32[]{:S(2)}) copy-start(bf16[32,2048]{1,0:T(8,128)(2,1)} %q_ref.1) | copy-start | bytes 393220
  19.0 43.3 %copy-start.1 = (s32[32]{0:T(128)S(1)}, s32[32]{0:T(128)}, u32[]{:S(2)}) copy-start(s32[32]{0:T(128)} %route_ref.1) | copy-start | bytes 388
  19.0 43.3 %copy-start.2 = (s32[16]{0:T(128)S(1)}, s32[16]{0:T(128)}, u32[]{:S(2)}) copy-start(s32[16]{0:T(128)} %place_ref.1) | copy-start | bytes 196
  19.0 43.3 %copy-start.6 = (s32[32]{0:T(128)S(1)}, s32[32]{0:T(128)}, u32[]{:S(2)}) copy-start(s32[32]{0:T(128)} %len_ref.1) | copy-start | bytes 388
  54.1 16.3 %all-to-all-start.1 = ((bf16[16,8,1664]{2,1,0:T(8,128)(2,1)}), bf16[16,8,1664]{2,1,0:T(8,128)(2,1)S(1)}, u32[]{:S(2)}, u32[]{:S(2)}) async-start(bf16[16,8,1664]{2,1,0:T(8,128)(2,1)} %bitcast.10), calls=%async_computation.1 | async-start | bytes 851968 | tf_op jit(solution)/shard_map/all_to_all | solution.py:448
  62.3 1.6 %copy-start.4 = (bf16[32,256,128]{2,1,0:T(8,128)(2,1)S(1)}, bf16[32,256,128]{2,1,0:T(8,128)(2,1)}, u32[]{:S(2)}) copy-start(bf16[32,256,128]{2,1,0:T(8,128)(2,1)} %k_ref.1) | copy-start | bytes 6291460
  63.9 1.6 %copy-start.5 = (bf16[32,256,128]{2,1,0:T(8,128)(2,1)S(1)}, bf16[32,256,128]{2,1,0:T(8,128)(2,1)}, u32[]{:S(2)}) copy-start(bf16[32,256,128]{2,1,0:T(8,128)(2,1)} %v_ref.1) | copy-start | bytes 6291460
  72.7 31.4 %all-to-all-start.2 = ((bf16[16,32,2048]{2,1,0:T(8,128)(2,1)}), bf16[16,32,2048]{2,1,0:T(8,128)(2,1)S(1)}, u32[]{:S(2)}, u32[]{:S(2)}) async-start(bf16[16,32,2048]{2,1,0:T(8,128)(2,1)} %shard_map.94), calls=%async_computation.2 | async-start | bytes 4194304 | tf_op jit(solution)/shard_map/all_to_all | solution.py:448
  104.1 2.2 %copy-start.3 = (bf16[2048,1024]{1,0:T(8,128)(2,1)S(1)}, bf16[2048,1024]{1,0:T(8,128)(2,1)}, u32[]{:S(2)}) copy-start(bf16[2048,1024]{1,0:T(8,128)(2,1)} %w_ref.1) | copy-start | bytes 12582916
  109.4 7.5 %collective-permute-start = (bf16[256,1024]{1,0:T(8,128)(2,1)}, bf16[256,1024]{1,0:T(8,128)(2,1)S(1)}, u32[]{:S(2)}, u32[]{:S(2)}) collective-permute-start(bf16[256,1024]{1,0:T(8,128)(2,1)} %get-tuple-element.18), channel_id=1, source_target_pairs={{0,1},{1,0},{2,3},{3,2},{4,5},{5,4},{6,7},{7,6},{8,9},{9,8},{10,11... | collective-permute-start | bytes 1572872 | tf_op jit(solution)/shard_map/ppermute | solution.py:504
  117.0 6.3 %collective-permute-start.1 = (bf16[64,1024]{1,0:T(8,128)(2,1)S(1)}, bf16[64,1024]{1,0:T(8,128)(2,1)S(1)}, u32[]{:S(2)}, u32[]{:S(2)}) collective-permute-start(bf16[64,1024]{1,0:T(8,128)(2,1)S(1)} %get-tuple-element.20), channel_id=1, source_target_pairs={{0,4},{1,5},{2,6},{3,7},{4,0},{5,1},{6,2},{7,3},{8,12},{9,13},{10,... | collective-permute-start | bytes 393224 | tf_op jit(solution)/shard_map/ppermute | solution.py:510
  120.0 6.6 %collective-permute-start.2 = (bf16[64,1024]{1,0:T(8,128)(2,1)S(1)}, bf16[64,1024]{1,0:T(8,128)(2,1)S(1)}, u32[]{:S(2)}, u32[]{:S(2)}) collective-permute-start(bf16[64,1024]{1,0:T(8,128)(2,1)S(1)} %get-tuple-element.21), channel_id=1, source_target_pairs={{0,2},{1,3},{2,4},{3,5},{4,6},{5,7},{6,0},{7,1},{8,10},{9,11},{10,... | collective-permute-start | bytes 393224 | tf_op jit(solution)/shard_map/ppermute | solution.py:510
  120.4 6.2 %collective-permute-start.3 = (bf16[64,1024]{1,0:T(8,128)(2,1)S(1)}, bf16[64,1024]{1,0:T(8,128)(2,1)S(1)}, u32[]{:S(2)}, u32[]{:S(2)}) collective-permute-start(bf16[64,1024]{1,0:T(8,128)(2,1)S(1)} %get-tuple-element.22), channel_id=1, source_target_pairs={{0,6},{1,7},{2,0},{3,1},{4,2},{5,3},{6,4},{7,5},{8,14},{9,15},{10,... | collective-permute-start | bytes 393224 | tf_op jit(solution)/shard_map/ppermute | solution.py:510

commit v5 on v4

--- a/solution.py
+++ b/solution.py
@@ -96,16 +96,26 @@
     place_ref,
     len_ref,
     q_ref,
-    k_ref,
-    v_ref,
+    k_in,
+    v_in,
     out_ref,
     lse_ref,
     dest_ref,
+    k_ref,
+    v_ref,
     count_ref,
+    sems,
 ):
     requests, cache, depth = k_ref.shape
     heads = q_ref.shape[1] // depth
     batch = 16
+    loads = []
+    for b in range(requests // batch):
+        sl = pl.ds(b * batch, batch)
+        loads.append(pltpu.make_async_copy(k_in.at[sl], k_ref.at[sl], sems.at[0, b]))
+        loads.append(pltpu.make_async_copy(v_in.at[sl], v_ref.at[sl], sems.at[1, b]))
+    for load in loads:
+        load.start()
     dest = [jnp.zeros((requests, 128), jnp.int32)]
     row = iota((requests, 128), 0)
 
@@ -122,6 +132,8 @@
         live = jnp.zeros((batch, 128), jnp.int32)
         for r in range(batch):
             live = jnp.where(own == r, len_ref[first + r], live)
+        loads[2 * b].wait()
+        loads[2 * b + 1].wait()
         keys = k_ref[sl].reshape(batch * cache, depth)
         values = v_ref[sl].reshape(batch * cache, depth)
         scores = lax.dot_general(q, keys, NT, preferred_element_type=F32)
@@ -374,10 +386,17 @@
                 out_ref[copy, :, sl] = merged
 
 
+DEEP = 512
 TILE = 256
 
 
-def project_kernel(core_ref, a_ref, w_ref, mine_ref, other_ref):
+def project_kernel(core_ref, a_ref, w_in, mine_ref, other_ref, w_ref, acc_ref, sems):
+    steps = w_ref.shape[0] // DEEP
+    loads = []
+    for n in range(steps):
+        sl = pl.ds(n * DEEP, DEEP)
+        loads.append(pltpu.make_async_copy(w_in.at[sl, :], w_ref.at[sl, :], sems.at[n]))
+        loads[n].start()
     core = core_ref[0]
     block = a_ref.shape[0] // 8
     half = 4 * block
@@ -386,11 +405,19 @@
         [a_ref[pl.ds(pl.multiple_of((2 * y + c) * block, block), block), :] for y, c in order],
         axis=0,
     )
-    for n in range(w_ref.shape[1] // TILE):
-        sl = slice(n * TILE, (n + 1) * TILE)
-        out = jnp.dot(a, w_ref[:, sl], preferred_element_type=F32)
-        mine_ref[:, sl] = out[:half]
-        other_ref[:, sl] = out[half:].astype(BF16)
+    for n in range(steps):
+        loads[n].wait()
+        deep = slice(n * DEEP, (n + 1) * DEEP)
+        for t in range(w_ref.shape[1] // TILE):
+            sl = slice(t * TILE, (t + 1) * TILE)
+            out = jnp.dot(a[:, deep], w_ref[deep, sl], preferred_element_type=F32)
+            if n > 0:
+                out += acc_ref[:, sl]
+            if n + 1 < steps:
+                acc_ref[:, sl] = out
+            else:
+                mine_ref[:, sl] = out[:half]
+                other_ref[:, sl] = out[half:].astype(BF16)
 
 
 def pair_kernel(y_ref, mine_ref, got_ref, own_ref, one_ref, two_ref, three_ref):
@@ -414,6 +441,10 @@
         + two_ref[...].astype(F32)
         + three_ref[...].astype(F32)
     ).astype(BF16)
+
+
+def in_hbm(array):
+    return pltpu.with_memory_space_constraint(array, pltpu.HBM)
 
 
 def call(kernel, outs, specs, scratch=(), cost=None, mib=16):
@@ -461,16 +492,21 @@
         ],
         None,
         62,
-    )(route, place, queries)
+    )(in_hbm(route), in_hbm(place), in_hbm(queries))
     received = exchange(packed)
     suffix_out, suffix_lse, dest = call(
         suffix_kernel,
         [((requests, width), F32), ((requests, width), F32), ((requests, 128), jnp.int32)],
-        [SMEM, SMEM, SMEM, VMEM, VMEM, VMEM],
-        [count],
+        [SMEM, SMEM, SMEM, VMEM, HBM, HBM],
+        [
+            pltpu.VMEM(suffix_keys.shape, BF16),
+            pltpu.VMEM(suffix_values.shape, BF16),
+            count,
+            pltpu.SemaphoreType.DMA((2, 2)),
+        ],
         pl.CostEstimate(flops=2 * 10**9, bytes_accessed=5 * 10**6, transcendentals=2 * 10**6),
         32,
-    )(route, place, suffix_len, queries, suffix_keys, suffix_values)
+    )(route, place, suffix_len, queries, in_hbm(suffix_keys), in_hbm(suffix_values))
     prefix = call(
         prefix_kernel,
         [((buffer_rows, CAP * 2 * HDIM + EXTRA), BF16)],
@@ -484,8 +520,8 @@
             pltpu.SemaphoreType.DMA((2, len(CHUNKS))),
         ],
         pl.CostEstimate(flops=10**10, bytes_accessed=5 * 10**6, transcendentals=12 * 10**6),
-        62,
-    )(received, prefix_keys, prefix_values)
+        44,
+    )(received, in_hbm(prefix_keys), in_hbm(prefix_values))
     back = exchange(prefix)
     copies = call(merge_kernel, [((owners, requests, width), BF16)], [VMEM] * 4)(
         back, dest, suffix_out, suffix_lse
@@ -496,11 +532,15 @@
     mine, other = call(
         project_kernel,
         [((half, columns), F32), ((half, columns), BF16)],
-        [SMEM, VMEM, VMEM],
-        (),
+        [SMEM, VMEM, HBM],
+        [
+            pltpu.VMEM(out_weight.shape, BF16),
+            pltpu.VMEM((2 * half, columns), F32),
+            pltpu.SemaphoreType.DMA((out_weight.shape[0] // DEEP,)),
+        ],
         pl.CostEstimate(flops=2 * 10**9, bytes_accessed=8 * 10**6, transcendentals=0),
-        24,
-    )(core, attention, out_weight)
+        28,
+    )(core, attention, in_hbm(out_weight))
     got = lax.ppermute(other, "tp", [(i, i ^ 1) for i in range(8)])
     block = half // 4
     own, *parts = call(

time: 127 us -> 126 us (level)
  local copies, waits for them, and re-layouts: 5.38 us -> 0.01 us
  Pallas kernels: 47.8 us -> 51.2 us
    unnamed x14 -> x8, local copies, waits for them, and re-layouts: 5.38 us -> 0.01 us
    pallas_call x1, Pallas kernels: 4.46 us -> 7.35 us  [on_device(): call(suffix_kernel, [((requests, width), F32), ((requests, width), F32),...]
    pallas_call x1, Pallas kernels: 3.12 us -> 4.55 us  [on_device(): call(project_kernel, [((half, columns), F32), ((half, columns), BF16)], [...]
  transfers between devices with their start and end apart: 6 -> 6, of which waited for: 5 -> 5; matrix products, arithmetic and copies ran while one was open for 0% -> 0% of each run, Pallas kernels for 4% -> 6%
where the time goes in v5:
time: 126 us; the launch traced here: 125 us
  Pallas kernels  51.2 us (41%)
  waiting for transfers between devices  31.6 us (25%)
  starting transfers between devices  25.5 us (20%)
  blocking collectives  16.9 us (13%)
    pallas_call x1, Pallas kernels, on_device(): call(prefix_kernel, [((buffer_rows, CAP * 2 * HDIM + EXTRA), BF16)], [VME...  34.2 us
    all_to_all x2, waiting for transfers between devices, exchange(): x = lax.all_to_all(x, 'pfx', split_axis=0, concat_axis=0, tiled=True)  25.9 us
    all_to_all x1, blocking collectives, exchange(): x = lax.all_to_all(x, 'pfx', split_axis=0, concat_axis=0, tiled=True)  16.9 us
    all_to_all x2, starting transfers between devices, exchange(): x = lax.all_to_all(x, 'pfx', split_axis=0, concat_axis=0, tiled=True)  14 us
    pallas_call x1, Pallas kernels, on_device(): call(suffix_kernel, [((requests, width), F32), ((requests, width), F32),...  7.35 us
    ppermute x1, starting transfers between devices, on_device(): got = lax.ppermute(other, 'tp', [(i, i ^ 1) for i in range(8)])  5.91 us
    ppermute x3, starting transfers between devices, on_device(): lax.ppermute(part, 'tp', [(i, (i + 2 * k) % 8) for i in range(8)])  5.67 us
    pallas_call x1, Pallas kernels, on_device(): call(project_kernel, [((half, columns), F32), ((half, columns), BF16)], [...  4.55 us
  transfers between devices with their start and end apart: 6, of which 5 were waited for; matrix products, arithmetic and copies ran while one was open for 0% of the time, Pallas kernels for 6%

profile of v5, /device:TPU:1, one launch (start us, length us, event | category | flops | bytes accessed | tf_op | source)
XLA Modules:
  0.0 125.3 jit_solution(11967101504794598237)
XLA Ops:
  0.0 2.0 %shard_map.91 = bf16[128,1664]{1,0:T(8,128)(2,1)} custom-call(s32[32]{0:T(128)} %route_ref.1, s32[16]{0:T(128)} %place_ref.1, bf16[32,2048]{1,0:T(8,128)(2,1)} %q_ref.1), custom_call_target="tpu_custom_call" | custom-call | tf_op jit(solution)/shard_map/pallas_call | solution.py:482
  2.0 16.9 %all_to_all.15 = bf16[16,8,1664]{2,1,0:T(8,128)(2,1)S(1)} all-to-all(bf16[16,8,1664]{2,1,0:T(8,128)(2,1)} %bitcast.10), channel_id=1, replica_groups=mesh['pfx'=16,'tp'=8] {'pfx'}, dimensions={0} | all-to-all | bytes 851968 | tf_op jit(solution)/shard_map/all_to_all | solution.py:479
  18.9 0.0 copy-start
  18.9 0.0 copy-start.1
  18.9 0.0 copy-start.2
  18.9 0.0 copy-start.3
  18.9 34.2 %shard_map.92 = bf16[128,1664]{1,0:T(8,128)(2,1)} custom-call(bf16[128,1664]{1,0:T(8,128)(2,1)S(1)} %bitcast.9, bf16[8192,128]{1,0:T(8,128)(2,1)} %k_in.2, bf16[8192,128]{1,0:T(8,128)(2,1)} %v_in.2), custom_call_target="tpu_custom_call" | custom-call | flops 10000000000 | bytes 5000000 | tf_op jit(solution)/shard_map/pallas_call | solution.py:510
  53.1 8.1 %all-to-all-start.1 = ((bf16[16,8,1664]{2,1,0:T(8,128)(2,1)}), bf16[16,8,1664]{2,1,0:T(8,128)(2,1)S(1)}, u32[]{:S(2)}, u32[]{:S(2)}) async-start(bf16[16,8,1664]{2,1,0:T(8,128)(2,1)} %bitcast.4), calls=%async_computation.1 | async-start | bytes 851968 | tf_op jit(solution)/shard_map/all_to_all | solution.py:479
  61.2 0.0 copy-done
  61.2 0.0 copy-done.1
  61.2 0.0 copy-done.2
  61.2 0.0 copy-done.3
  61.2 7.3 %shard_map.93 = (f32[32,2048]{1,0:T(8,128)S(1)}, f32[32,2048]{1,0:T(8,128)S(1)}, s32[32,128]{1,0:T(8,128)S(1)}) custom-call(s32[32]{0:T(128)S(1)} %copy-done.1, s32[16]{0:T(128)S(1)} %copy-done.2, s32[32]{0:T(128)S(1)} %copy-done.3, bf16[32,2048]{1,0:T(8,128)(2,1)S(1)} %copy-done, bf16[32,256,128]{2,1,0:T(8,128)(2,1)} %k_in.3, bf16[32,256,128]{2,1,0:T(8,128)(2,1)} %v_in.3), custom_call_target="tpu_custom_call" | custom-call | flops 2000000000 | bytes 5000000 | tf_op jit(solution)/shard_map/pallas_call | solution.py:497
  68.6 0.8 all-to-all-done.1
  69.3 2.3 %shard_map.94 = bf16[16,32,2048]{2,1,0:T(8,128)(2,1)} custom-call(bf16[128,1664]{1,0:T(8,128)(2,1)S(1)} %bitcast.8, s32[32,128]{1,0:T(8,128)S(1)} %get-tuple-element.14.dest_ref, f32[32,2048]{1,0:T(8,128)S(1)} %get-tuple-element.15.suffix_ref, f32[32,2048]{1,0:T(8,128)S(1)} %get-tuple-element.16.lse_ref), custom_call_target="tpu_custom_call" | custom-call | tf_op jit(solution)/shard_map/pallas_call | solution.py:526
  71.6 5.9 %all-to-all-start.2 = ((bf16[16,32,2048]{2,1,0:T(8,128)(2,1)}), bf16[16,32,2048]{2,1,0:T(8,128)(2,1)S(1)}, u32[]{:S(2)}, u32[]{:S(2)}) async-start(bf16[16,32,2048]{2,1,0:T(8,128)(2,1)} %shard_map.94), calls=%async_computation.2 | async-start | bytes 4194304 | tf_op jit(solution)/shard_map/all_to_all | solution.py:479
  77.5 25.2 %all-to-all-done.2 = bf16[16,32,2048]{2,1,0:T(8,128)(2,1)S(1)} async-done(((bf16[16,32,2048]{2,1,0:T(8,128)(2,1)}), bf16[16,32,2048]{2,1,0:T(8,128)(2,1)S(1)}, u32[]{:S(2)}, u32[]{:S(2)}) %all-to-all-start.2) | async-done | bytes 2097184 | tf_op jit(solution)/shard_map/all_to_all | solution.py:479
  102.7 4.5 %shard_map.95 = (f32[256,1024]{1,0:T(8,128)S(1)}, bf16[256,1024]{1,0:T(8,128)(2,1)}) custom-call(s32[1]{0:T(128)} %bitcast.1.core_ref, bf16[512,2048]{1,0:T(8,128)(2,1)S(1)} %bitcast.7, bf16[2048,1024]{1,0:T(8,128)(2,1)} %w_in.1), custom_call_target="tpu_custom_call" | custom-call | flops 2000000000 | bytes 8000000 | tf_op jit(solution)/shard_map/pallas_call | solution.py:532
  107.2 5.9 %collective-permute-start = (bf16[256,1024]{1,0:T(8,128)(2,1)}, bf16[256,1024]{1,0:T(8,128)(2,1)S(1)}, u32[]{:S(2)}, u32[]{:S(2)}) collective-permute-start(bf16[256,1024]{1,0:T(8,128)(2,1)} %get-tuple-element.18), channel_id=1, source_target_pairs={{0,1},{1,0},{2,3},{3,2},{4,5},{5,4},{6,7},{7,6},{8,9},{9,8},{10,11... | collective-permute-start | bytes 1572872 | tf_op jit(solution)/shard_map/ppermute | solution.py:544
  113.1 1.7 %collective-permute-done.got_ref = bf16[256,1024]{1,0:T(8,128)(2,1)S(1)} collective-permute-done((bf16[256,1024]{1,0:T(8,128)(2,1)}, bf16[256,1024]{1,0:T(8,128)(2,1)S(1)}, u32[]{:S(2)}, u32[]{:S(2)}) %collective-permute-start) | collective-permute-done | bytes 524320 | tf_op jit(solution)/shard_map/ppermute | solution.py:544
  114.9 0.1 shard_map.96
  115.0 3.0 %collective-permute-start.1 = (bf16[64,1024]{1,0:T(8,128)(2,1)S(1)}, bf16[64,1024]{1,0:T(8,128)(2,1)S(1)}, u32[]{:S(2)}, u32[]{:S(2)}) collective-permute-start(bf16[64,1024]{1,0:T(8,128)(2,1)S(1)} %get-tuple-element.20), channel_id=1, source_target_pairs={{0,4},{1,5},{2,6},{3,7},{4,0},{5,1},{6,2},{7,3},{8,12},{9,13},{10,... | collective-permute-start | bytes 393224 | tf_op jit(solution)/shard_map/ppermute | solution.py:550
  118.0 0.4 collective-permute-start.2
  118.4 2.3 %collective-permute-start.3 = (bf16[64,1024]{1,0:T(8,128)(2,1)S(1)}, bf16[64,1024]{1,0:T(8,128)(2,1)S(1)}, u32[]{:S(2)}, u32[]{:S(2)}) collective-permute-start(bf16[64,1024]{1,0:T(8,128)(2,1)S(1)} %get-tuple-element.22), channel_id=1, source_target_pairs={{0,6},{1,7},{2,0},{3,1},{4,2},{5,3},{6,4},{7,5},{8,14},{9,15},{10,... | collective-permute-start | bytes 393224 | tf_op jit(solution)/shard_map/ppermute | solution.py:550
  120.6 0.6 collective-permute-done.1.one_ref
  121.3 3.3 %collective-permute-done.2.two_ref = bf16[64,1024]{1,0:T(8,128)(2,1)S(1)} collective-permute-done((bf16[64,1024]{1,0:T(8,128)(2,1)S(1)}, bf16[64,1024]{1,0:T(8,128)(2,1)S(1)}, u32[]{:S(2)}, u32[]{:S(2)}) %collective-permute-start.2) | collective-permute-done | bytes 131104 | tf_op jit(solution)/shard_map/ppermute | solution.py:550
  124.6 0.0 collective-permute-done.3.three_ref
  124.6 0.7 shard_map.97
Async XLA Ops:
  18.9 42.3 %copy-start = (bf16[32,2048]{1,0:T(8,128)(2,1)S(1)}, bf16[32,2048]{1,0:T(8,128)(2,1)}, u32[]{:S(2)}) copy-start(bf16[32,2048]{1,0:T(8,128)(2,1)} %q_ref.1) | copy-start | bytes 393220
  18.9 42.3 %copy-start.1 = (s32[32]{0:T(128)S(1)}, s32[32]{0:T(128)}, u32[]{:S(2)}) copy-start(s32[32]{0:T(128)} %route_ref.1) | copy-start | bytes 388
  18.9 42.3 %copy-start.2 = (s32[16]{0:T(128)S(1)}, s32[16]{0:T(128)}, u32[]{:S(2)}) copy-start(s32[16]{0:T(128)} %place_ref.1) | copy-start | bytes 196
  18.9 42.3 %copy-start.3 = (s32[32]{0:T(128)S(1)}, s32[32]{0:T(128)}, u32[]{:S(2)}) copy-start(s32[32]{0:T(128)} %len_ref.1) | copy-start | bytes 388
  53.1 16.2 %all-to-all-start.1 = ((bf16[16,8,1664]{2,1,0:T(8,128)(2,1)}), bf16[16,8,1664]{2,1,0:T(8,128)(2,1)S(1)}, u32[]{:S(2)}, u32[]{:S(2)}) async-start(bf16[16,8,1664]{2,1,0:T(8,128)(2,1)} %bitcast.4), calls=%async_computation.1 | async-start | bytes 851968 | tf_op jit(solution)/shard_map/all_to_all | solution.py:479
  71.6 31.1 %all-to-all-start.2 = ((bf16[16,32,2048]{2,1,0:T(8,128)(2,1)}), bf16[16,32,2048]{2,1,0:T(8,128)(2,1)S(1)}, u32[]{:S(2)}, u32[]{:S(2)}) async-start(bf16[16,32,2048]{2,1,0:T(8,128)(2,1)} %shard_map.94), calls=%async_computation.2 | async-start | bytes 4194304 | tf_op jit(solution)/shard_map/all_to_all | solution.py:479
  107.2 7.7 %collective-permute-start = (bf16[256,1024]{1,0:T(8,128)(2,1)}, bf16[256,1024]{1,0:T(8,128)(2,1)S(1)}, u32[]{:S(2)}, u32[]{:S(2)}) collective-permute-start(bf16[256,1024]{1,0:T(8,128)(2,1)} %get-tuple-element.18), channel_id=1, source_target_pairs={{0,1},{1,0},{2,3},{3,2},{4,5},{5,4},{6,7},{7,6},{8,9},{9,8},{10,11... | collective-permute-start | bytes 1572872 | tf_op jit(solution)/shard_map/ppermute | solution.py:544
  115.0 6.3 %collective-permute-start.1 = (bf16[64,1024]{1,0:T(8,128)(2,1)S(1)}, bf16[64,1024]{1,0:T(8,128)(2,1)S(1)}, u32[]{:S(2)}, u32[]{:S(2)}) collective-permute-start(bf16[64,1024]{1,0:T(8,128)(2,1)S(1)} %get-tuple-element.20), channel_id=1, source_target_pairs={{0,4},{1,5},{2,6},{3,7},{4,0},{5,1},{6,2},{7,3},{8,12},{9,13},{10,... | collective-permute-start | bytes 393224 | tf_op jit(solution)/shard_map/ppermute | solution.py:550
  118.0 6.6 %collective-permute-start.2 = (bf16[64,1024]{1,0:T(8,128)(2,1)S(1)}, bf16[64,1024]{1,0:T(8,128)(2,1)S(1)}, u32[]{:S(2)}, u32[]{:S(2)}) collective-permute-start(bf16[64,1024]{1,0:T(8,128)(2,1)S(1)} %get-tuple-element.21), channel_id=1, source_target_pairs={{0,2},{1,3},{2,4},{3,5},{4,6},{5,7},{6,0},{7,1},{8,10},{9,11},{10,... | collective-permute-start | bytes 393224 | tf_op jit(solution)/shard_map/ppermute | solution.py:550
  118.4 6.2 %collective-permute-start.3 = (bf16[64,1024]{1,0:T(8,128)(2,1)S(1)}, bf16[64,1024]{1,0:T(8,128)(2,1)S(1)}, u32[]{:S(2)}, u32[]{:S(2)}) collective-permute-start(bf16[64,1024]{1,0:T(8,128)(2,1)S(1)} %get-tuple-element.22), channel_id=1, source_target_pairs={{0,6},{1,7},{2,0},{3,1},{4,2},{5,3},{6,4},{7,5},{8,14},{9,15},{10,... | collective-permute-start | bytes 393224 | tf_op jit(solution)/shard_map/ppermute | solution.py:550

commit v6 on v5

--- a/solution.py
+++ b/solution.py
@@ -346,7 +346,7 @@
     out_ref[:, width:] = tail.astype(BF16)
 
 
-def merge_kernel(back_ref, dest_ref, suffix_ref, lse_ref, out_ref):
+def merge_kernel(back_ref, dest_ref, suffix_ref, lse_ref, out_ref, merged_ref, sems):
     copies, requests, _ = out_ref.shape
     buffer_rows = back_ref.shape[0]
     dest = dest_ref[:, :1]
@@ -367,23 +367,31 @@
     )
     pieces = jnp.where(jnp.concatenate([slot] * SLOTS, axis=0), pieces, 0.0).astype(BF16)
     lses = jnp.dot(pieces, to_half, preferred_element_type=F32)
-    for sub in range(SLOTS):
-        prefix = prefixes[sub * requests : (sub + 1) * requests]
-        prefix_lse = lses[sub * requests : (sub + 1) * requests]
-        for half in range(2):
-            part = slice(half * HDIM, (half + 1) * HDIM)
+    sends = []
+    for half in range(2):
+        part = slice(half * HDIM, (half + 1) * HDIM)
+        for sub in range(SLOTS):
+            rows = slice(sub * requests, (sub + 1) * requests)
             start = (half * SLOTS + sub) * HDIM
             sl = slice(start, start + HDIM)
+            prefix_lse = lses[rows, part]
             suffix_lse = lse_ref[:, sl]
-            top = jnp.maximum(prefix_lse[:, part], suffix_lse)
-            prefix_part = jnp.exp(prefix_lse[:, part] - top)
+            top = jnp.maximum(prefix_lse, suffix_lse)
+            prefix_part = jnp.exp(prefix_lse - top)
             suffix_part = jnp.exp(suffix_lse - top)
-            merged = (prefix_part * prefix[:, part] + suffix_part * suffix_ref[:, sl]) / (
+            merged = (prefix_part * prefixes[rows, part] + suffix_part * suffix_ref[:, sl]) / (
                 prefix_part + suffix_part
             )
-            merged = merged.astype(BF16)
-            for copy in range(copies):
-                out_ref[copy, :, sl] = merged
+            merged_ref[:, sl] = merged.astype(BF16)
+        columns = pl.ds(half * SLOTS * HDIM, SLOTS * HDIM)
+        for copy in range(copies):
+            send = pltpu.make_async_copy(
+                merged_ref.at[:, columns], out_ref.at[copy, :, columns], sems.at[half, copy]
+            )
+            send.start()
+            sends.append(send)
+    for send in sends:
+        send.wait()
 
 
 DEEP = 512
@@ -523,9 +531,17 @@
         44,
     )(received, in_hbm(prefix_keys), in_hbm(prefix_values))
     back = exchange(prefix)
-    copies = call(merge_kernel, [((owners, requests, width), BF16)], [VMEM] * 4)(
-        back, dest, suffix_out, suffix_lse
-    )
+    copies = pl.pallas_call(
+        merge_kernel,
+        out_shape=pltpu.HBM((owners, requests, width), BF16),
+        in_specs=[VMEM] * 4,
+        out_specs=HBM,
+        scratch_shapes=[
+            pltpu.VMEM((requests, width), BF16),
+            pltpu.SemaphoreType.DMA((2, owners)),
+        ],
+        compiler_params=pltpu.CompilerParams(vmem_limit_bytes=16 * 2**20),
+    )(back, dest, suffix_out, suffix_lse)
     attention = exchange(copies.reshape(owners * requests, width))
     columns = out_weight.shape[1]
     half = owners * requests // 2

time: 126 us -> 125 us (level)
  no operation moved by 1% of the time
where the time goes in v6:
time: 125 us
  Pallas kernels  51 us (41%)
  waiting for transfers between devices  31.7 us (25%)
  starting transfers between devices  25.5 us (20%)
  blocking collectives  16.9 us (14%)
    pallas_call x1, Pallas kernels, on_device(): call(prefix_kernel, [((buffer_rows, CAP * 2 * HDIM + EXTRA), BF16)], [VME...  34.2 us
    all_to_all x2, waiting for transfers between devices, exchange(): x = lax.all_to_all(x, 'pfx', split_axis=0, concat_axis=0, tiled=True)  26.1 us
    all_to_all x1, blocking collectives, exchange(): x = lax.all_to_all(x, 'pfx', split_axis=0, concat_axis=0, tiled=True)  16.9 us
    all_to_all x2, starting transfers between devices, exchange(): x = lax.all_to_all(x, 'pfx', split_axis=0, concat_axis=0, tiled=True)  14.3 us
    pallas_call x1, Pallas kernels, on_device(): call(suffix_kernel, [((requests, width), F32), ((requests, width), F32),...  7.35 us
    ppermute x3, starting transfers between devices, on_device(): lax.ppermute(part, 'tp', [(i, (i + 2 * k) % 8) for i in range(8)])  5.67 us
    ppermute x1, starting transfers between devices, on_device(): got = lax.ppermute(other, 'tp', [(i, i ^ 1) for i in range(8)])  5.57 us
    pallas_call x1, Pallas kernels, on_device(): call(project_kernel, [((half, columns), F32), ((half, columns), BF16)], [...  4.55 us
  transfers between devices with their start and end apart: 6, of which 5 were waited for; matrix products, arithmetic and copies ran while one was open for 0% of the time, Pallas kernels for 6%

profile of v6, /device:TPU:1, one launch (start us, length us, event | category | flops | bytes accessed | tf_op | source)
XLA Modules:
  0.0 125.3 jit_solution(17198532941085221323)
XLA Ops:
  0.0 2.0 %shard_map.91 = bf16[128,1664]{1,0:T(8,128)(2,1)} custom-call(s32[32]{0:T(128)} %route_ref.1, s32[16]{0:T(128)} %place_ref.1, bf16[32,2048]{1,0:T(8,128)(2,1)} %q_ref.1), custom_call_target="tpu_custom_call" | custom-call | tf_op jit(solution)/shard_map/pallas_call | solution.py:490
  2.0 16.9 %all_to_all.15 = bf16[16,8,1664]{2,1,0:T(8,128)(2,1)S(1)} all-to-all(bf16[16,8,1664]{2,1,0:T(8,128)(2,1)} %bitcast.10), channel_id=1, replica_groups=mesh['pfx'=16,'tp'=8] {'pfx'}, dimensions={0} | all-to-all | bytes 851968 | tf_op jit(solution)/shard_map/all_to_all | solution.py:487
  18.9 0.0 copy-start
  18.9 0.0 copy-start.1
  18.9 0.0 copy-start.2
  18.9 0.0 copy-start.3
  18.9 34.2 %shard_map.92 = bf16[128,1664]{1,0:T(8,128)(2,1)} custom-call(bf16[128,1664]{1,0:T(8,128)(2,1)S(1)} %bitcast.9, bf16[8192,128]{1,0:T(8,128)(2,1)} %k_in.2, bf16[8192,128]{1,0:T(8,128)(2,1)} %v_in.2), custom_call_target="tpu_custom_call" | custom-call | flops 10000000000 | bytes 5000000 | tf_op jit(solution)/shard_map/pallas_call | solution.py:518
  53.1 8.4 %all-to-all-start.1 = ((bf16[16,8,1664]{2,1,0:T(8,128)(2,1)}), bf16[16,8,1664]{2,1,0:T(8,128)(2,1)S(1)}, u32[]{:S(2)}, u32[]{:S(2)}) async-start(bf16[16,8,1664]{2,1,0:T(8,128)(2,1)} %bitcast.4), calls=%async_computation.1 | async-start | bytes 851968 | tf_op jit(solution)/shard_map/all_to_all | solution.py:487
  61.5 0.0 copy-done
  61.5 0.0 copy-done.1
  61.5 0.0 copy-done.2
  61.5 0.0 copy-done.3
  61.5 7.3 %shard_map.93 = (f32[32,2048]{1,0:T(8,128)S(1)}, f32[32,2048]{1,0:T(8,128)S(1)}, s32[32,128]{1,0:T(8,128)S(1)}) custom-call(s32[32]{0:T(128)S(1)} %copy-done.1, s32[16]{0:T(128)S(1)} %copy-done.2, s32[32]{0:T(128)S(1)} %copy-done.3, bf16[32,2048]{1,0:T(8,128)(2,1)S(1)} %copy-done, bf16[32,256,128]{2,1,0:T(8,128)(2,1)} %k_in.3, bf16[32,256,128]{2,1,0:T(8,128)(2,1)} %v_in.3), custom_call_target="tpu_custom_call" | custom-call | flops 2000000000 | bytes 5000000 | tf_op jit(solution)/shard_map/pallas_call | solution.py:505
  68.9 0.8 all-to-all-done.1
  69.6 2.1 %shard_map.94 = bf16[16,32,2048]{2,1,0:T(8,128)(2,1)} custom-call(bf16[128,1664]{1,0:T(8,128)(2,1)S(1)} %bitcast.8, s32[32,128]{1,0:T(8,128)S(1)} %get-tuple-element.14.dest_ref, f32[32,2048]{1,0:T(8,128)S(1)} %get-tuple-element.15.suffix_ref, f32[32,2048]{1,0:T(8,128)S(1)} %get-tuple-element.16.lse_ref), custom_call_target="tpu_custom_call" | custom-call | tf_op jit(solution)/shard_map/pallas_call | solution.py:534
  71.7 5.9 %all-to-all-start.2 = ((bf16[16,32,2048]{2,1,0:T(8,128)(2,1)}), bf16[16,32,2048]{2,1,0:T(8,128)(2,1)S(1)}, u32[]{:S(2)}, u32[]{:S(2)}) async-start(bf16[16,32,2048]{2,1,0:T(8,128)(2,1)} %shard_map.94), calls=%async_computation.2 | async-start | bytes 4194304 | tf_op jit(solution)/shard_map/all_to_all | solution.py:487
  77.7 25.3 %all-to-all-done.2 = bf16[16,32,2048]{2,1,0:T(8,128)(2,1)S(1)} async-done(((bf16[16,32,2048]{2,1,0:T(8,128)(2,1)}), bf16[16,32,2048]{2,1,0:T(8,128)(2,1)S(1)}, u32[]{:S(2)}, u32[]{:S(2)}) %all-to-all-start.2) | async-done | bytes 2097184 | tf_op jit(solution)/shard_map/all_to_all | solution.py:487
  103.0 4.5 %shard_map.95 = (f32[256,1024]{1,0:T(8,128)S(1)}, bf16[256,1024]{1,0:T(8,128)(2,1)}) custom-call(s32[1]{0:T(128)} %bitcast.1.core_ref, bf16[512,2048]{1,0:T(8,128)(2,1)S(1)} %bitcast.7, bf16[2048,1024]{1,0:T(8,128)(2,1)} %w_in.1), custom_call_target="tpu_custom_call" | custom-call | flops 2000000000 | bytes 8000000 | tf_op jit(solution)/shard_map/pallas_call | solution.py:548
  107.6 5.6 %collective-permute-start = (bf16[256,1024]{1,0:T(8,128)(2,1)}, bf16[256,1024]{1,0:T(8,128)(2,1)S(1)}, u32[]{:S(2)}, u32[]{:S(2)}) collective-permute-start(bf16[256,1024]{1,0:T(8,128)(2,1)} %get-tuple-element.18), channel_id=1, source_target_pairs={{0,1},{1,0},{2,3},{3,2},{4,5},{5,4},{6,7},{7,6},{8,9},{9,8},{10,11... | collective-permute-start | bytes 1572872 | tf_op jit(solution)/shard_map/ppermute | solution.py:560
  113.1 1.7 %collective-permute-done.got_ref = bf16[256,1024]{1,0:T(8,128)(2,1)S(1)} collective-permute-done((bf16[256,1024]{1,0:T(8,128)(2,1)}, bf16[256,1024]{1,0:T(8,128)(2,1)S(1)}, u32[]{:S(2)}, u32[]{:S(2)}) %collective-permute-start) | collective-permute-done | bytes 524320 | tf_op jit(solution)/shard_map/ppermute | solution.py:560
  114.9 0.1 shard_map.96
  115.0 3.0 %collective-permute-start.1 = (bf16[64,1024]{1,0:T(8,128)(2,1)S(1)}, bf16[64,1024]{1,0:T(8,128)(2,1)S(1)}, u32[]{:S(2)}, u32[]{:S(2)}) collective-permute-start(bf16[64,1024]{1,0:T(8,128)(2,1)S(1)} %get-tuple-element.20), channel_id=1, source_target_pairs={{0,4},{1,5},{2,6},{3,7},{4,0},{5,1},{6,2},{7,3},{8,12},{9,13},{10,... | collective-permute-start | bytes 393224 | tf_op jit(solution)/shard_map/ppermute | solution.py:566
  118.0 0.4 collective-permute-start.2
  118.4 2.3 %collective-permute-start.3 = (bf16[64,1024]{1,0:T(8,128)(2,1)S(1)}, bf16[64,1024]{1,0:T(8,128)(2,1)S(1)}, u32[]{:S(2)}, u32[]{:S(2)}) collective-permute-start(bf16[64,1024]{1,0:T(8,128)(2,1)S(1)} %get-tuple-element.22), channel_id=1, source_target_pairs={{0,6},{1,7},{2,0},{3,1},{4,2},{5,3},{6,4},{7,5},{8,14},{9,15},{10,... | collective-permute-start | bytes 393224 | tf_op jit(solution)/shard_map/ppermute | solution.py:566
  120.6 0.6 collective-permute-done.1.one_ref
  121.3 3.3 %collective-permute-done.2.two_ref = bf16[64,1024]{1,0:T(8,128)(2,1)S(1)} collective-permute-done((bf16[64,1024]{1,0:T(8,128)(2,1)S(1)}, bf16[64,1024]{1,0:T(8,128)(2,1)S(1)}, u32[]{:S(2)}, u32[]{:S(2)}) %collective-permute-start.2) | collective-permute-done | bytes 131104 | tf_op jit(solution)/shard_map/ppermute | solution.py:566
  124.6 0.0 collective-permute-done.3.three_ref
  124.6 0.7 shard_map.97
Async XLA Ops:
  18.9 42.6 %copy-start = (bf16[32,2048]{1,0:T(8,128)(2,1)S(1)}, bf16[32,2048]{1,0:T(8,128)(2,1)}, u32[]{:S(2)}) copy-start(bf16[32,2048]{1,0:T(8,128)(2,1)} %q_ref.1) | copy-start | bytes 393220
  18.9 42.6 %copy-start.1 = (s32[32]{0:T(128)S(1)}, s32[32]{0:T(128)}, u32[]{:S(2)}) copy-start(s32[32]{0:T(128)} %route_ref.1) | copy-start | bytes 388
  18.9 42.6 %copy-start.2 = (s32[16]{0:T(128)S(1)}, s32[16]{0:T(128)}, u32[]{:S(2)}) copy-start(s32[16]{0:T(128)} %place_ref.1) | copy-start | bytes 196
  18.9 42.6 %copy-start.3 = (s32[32]{0:T(128)S(1)}, s32[32]{0:T(128)}, u32[]{:S(2)}) copy-start(s32[32]{0:T(128)} %len_ref.1) | copy-start | bytes 388
  53.1 16.5 %all-to-all-start.1 = ((bf16[16,8,1664]{2,1,0:T(8,128)(2,1)}), bf16[16,8,1664]{2,1,0:T(8,128)(2,1)S(1)}, u32[]{:S(2)}, u32[]{:S(2)}) async-start(bf16[16,8,1664]{2,1,0:T(8,128)(2,1)} %bitcast.4), calls=%async_computation.1 | async-start | bytes 851968 | tf_op jit(solution)/shard_map/all_to_all | solution.py:487
  71.7 31.3 %all-to-all-start.2 = ((bf16[16,32,2048]{2,1,0:T(8,128)(2,1)}), bf16[16,32,2048]{2,1,0:T(8,128)(2,1)S(1)}, u32[]{:S(2)}, u32[]{:S(2)}) async-start(bf16[16,32,2048]{2,1,0:T(8,128)(2,1)} %shard_map.94), calls=%async_computation.2 | async-start | bytes 4194304 | tf_op jit(solution)/shard_map/all_to_all | solution.py:487
  107.6 7.3 %collective-permute-start = (bf16[256,1024]{1,0:T(8,128)(2,1)}, bf16[256,1024]{1,0:T(8,128)(2,1)S(1)}, u32[]{:S(2)}, u32[]{:S(2)}) collective-permute-start(bf16[256,1024]{1,0:T(8,128)(2,1)} %get-tuple-element.18), channel_id=1, source_target_pairs={{0,1},{1,0},{2,3},{3,2},{4,5},{5,4},{6,7},{7,6},{8,9},{9,8},{10,11... | collective-permute-start | bytes 1572872 | tf_op jit(solution)/shard_map/ppermute | solution.py:560
  115.0 6.3 %collective-permute-start.1 = (bf16[64,1024]{1,0:T(8,128)(2,1)S(1)}, bf16[64,1024]{1,0:T(8,128)(2,1)S(1)}, u32[]{:S(2)}, u32[]{:S(2)}) collective-permute-start(bf16[64,1024]{1,0:T(8,128)(2,1)S(1)} %get-tuple-element.20), channel_id=1, source_target_pairs={{0,4},{1,5},{2,6},{3,7},{4,0},{5,1},{6,2},{7,3},{8,12},{9,13},{10,... | collective-permute-start | bytes 393224 | tf_op jit(solution)/shard_map/ppermute | solution.py:566
  118.0 6.6 %collective-permute-start.2 = (bf16[64,1024]{1,0:T(8,128)(2,1)S(1)}, bf16[64,1024]{1,0:T(8,128)(2,1)S(1)}, u32[]{:S(2)}, u32[]{:S(2)}) collective-permute-start(bf16[64,1024]{1,0:T(8,128)(2,1)S(1)} %get-tuple-element.21), channel_id=1, source_target_pairs={{0,2},{1,3},{2,4},{3,5},{4,6},{5,7},{6,0},{7,1},{8,10},{9,11},{10,... | collective-permute-start | bytes 393224 | tf_op jit(solution)/shard_map/ppermute | solution.py:566
  118.4 6.2 %collective-permute-start.3 = (bf16[64,1024]{1,0:T(8,128)(2,1)S(1)}, bf16[64,1024]{1,0:T(8,128)(2,1)S(1)}, u32[]{:S(2)}, u32[]{:S(2)}) collective-permute-start(bf16[64,1024]{1,0:T(8,128)(2,1)S(1)} %get-tuple-element.22), channel_id=1, source_target_pairs={{0,6},{1,7},{2,0},{3,1},{4,2},{5,3},{6,4},{7,5},{8,14},{9,15},{10,... | collective-permute-start | bytes 393224 | tf_op jit(solution)/shard_map/ppermute | solution.py:566
